TPU v7x, 32 devices: a whole 2x2x4 slice. The times are simulated.
32 devices in a mesh: parts: 2 (over x), sub: 16 (over z, y, core).
Axes of the slice: x: 2, y: 2, z: 4, core: 2. Of those that a mesh axis runs over, the one named last changes fastest.
Arguments:
- load: float32 [64, 16, 16, 128], P(('parts', 'sub')), parts along dimension 0, may hold values from -140 to 140
- stiff_inv: bfloat16 [64, 2048, 2048], P(('parts', 'sub')), parts along dimension 0, may hold values from -4 to 5, as said below
- face_blocks: bfloat16 [64, 16, 128, 128], P(('parts', 'sub')), parts along dimension 0, may hold values from -8 to 10, as said below
- coupling: float32 [64, 24, 2048], P(('parts', 'sub')), parts along dimension 0, may hold values from -0.6 to 0.6
- coarse_inv: float32 [1024, 512], P(('parts', 'sub')), parts along dimension 0, may hold values from -2 to 2, as said below
- corners: int32 [64, 24], P(('parts', 'sub')), parts along dimension 0, may hold values from 0 to 511
- partner: int32 [64, 16], P(('parts', 'sub')), parts along dimension 0, may hold values from 0 to 511, as said below
Outputs:
- multipliers: float32 [64, 16, 16, 128], P(('parts', 'sub')), parts along dimension 0
- residual: float32 [64, 16, 16, 128], P(('parts', 'sub')), parts along dimension 0
There are 2 independent parts, one for each index of `parts`. A program takes and returns all parts, laid end to end along the dimension named above; each array names one. Nothing has to cross between parts.
Inputs may be any that keep to these rules, and one draw needn't show every extreme that they name: `stiff_inv`: every subdomain's matrix is symmetric positive definite. `face_blocks`: every face block is symmetric positive definite. `coarse_inv`: symmetric positive definite. partner[s, j] is the number s2 * 16 + j2 of the face that shares its unknowns, in the same order, with face j of subdomain s; the relation is symmetric; a device of sub holds 2 subdomains in a row; the two faces of a pair lie on devices one, two or three indices apart along sub; between two devices at most 12 pairs of faces are shared, a bound that is reached by some pair of devices at each of the three distances.
All inputs are finite; a program needn't handle non-finite values.
Results may differ from a plain program's by a relative error of at most 0.004.
Values sent between devices are 32-bit elements; how exact they have to be, the bound alone decides.
No kernel may reach another device: no remote copies, remote signals or barrier semaphores. Data moves between devices by JAX's collectives and lax.ppermute only.
A program may use at most 128 MiB of HBM per device.

v0:
```python
import jax
import jax.numpy as jnp
from jax import lax
from jax.sharding import PartitionSpec as P

ITERS = 3


def shifted(value, axis, by):
    devices = lax.axis_size(axis)
    pairs = [(i, i + by) for i in range(devices) if 0 <= i + by < devices]
    return lax.ppermute(value, axis, pairs)


def routing(partner):
    face_count = partner.shape[0] * partner.shape[1]
    capacity = 3 * face_count // 8
    own_index = lax.axis_index("sub")
    partner_ids = partner.reshape(face_count)
    peer_dev = partner_ids // face_count
    offset = peer_dev - own_index
    lane_index = jnp.where(offset > 0, offset - 1, 2 - offset)
    back_lane = jnp.where(offset > 0, offset + 2, -offset - 1)
    same_peer = peer_dev[:, None] == peer_dev[None, :]
    send_pos = jnp.sum(same_peer & (partner_ids[None, :] < partner_ids[:, None]), axis=1)
    face_order = jnp.arange(face_count, dtype=jnp.int32)
    recv_pos = jnp.sum(same_peer & (face_order[None, :] < face_order[:, None]), axis=1)
    target = lane_index * capacity + send_pos
    source = jnp.zeros((6 * capacity,), jnp.int32).at[target].set(face_order)
    filled = jnp.zeros((6 * capacity,), jnp.bool_).at[target].set(True)
    arrival = back_lane * capacity + recv_pos
    return (source, filled, arrival, capacity)


def partner_values(field_vec, routes):
    source, filled, arrival, capacity = routes
    face_rows = field_vec.reshape((-1,) + field_vec.shape[2:])
    outgoing = jnp.where(filled[:, None, None], face_rows[source], 0.0)
    outgoing = outgoing.reshape(6, capacity, face_rows.shape[1], face_rows.shape[2])
    arrived = []
    for lane_pos, offset_by in enumerate((1, 2, 3, -1, -2, -3)):
        arrived.append(shifted(outgoing[lane_pos], "sub", offset_by))
    incoming = jnp.stack(arrived).reshape((6 * capacity,) + face_rows.shape[1:])
    return incoming[arrival].reshape(field_vec.shape)


def inner_sum(first_vec, second_vec):
    return jnp.sum(first_vec * second_vec, axis=(0, 1, 3))


def on_device(load, stiff_inv, face_blocks, coupling, coarse_inv, corners, partner):
    sub_count, faces, loads, face_dof = load.shape
    routes = routing(partner)
    primal_count = corners.shape[0] * corners.shape[1]
    coarse_total = coarse_inv.shape[1]
    indicator = (
        corners.reshape(primal_count)[:, None] == jnp.arange(coarse_total, dtype=jnp.int32)[None, :]
    ).astype(jnp.float32)
    coupling_faces = coupling.reshape(sub_count, coupling.shape[1], faces, face_dof)
    stiff_faces = stiff_inv.reshape(sub_count, faces, face_dof, faces, face_dof)
    coarse_whole = lax.all_gather(coarse_inv, "sub", axis=0, tiled=True)

    def apply_op(vector):
        rounded = vector.astype(jnp.bfloat16)
        local_part = jnp.einsum(
            "sflb,sfbga->sgla", rounded, stiff_faces, preferred_element_type=jnp.float32
        )
        primal_rows = jnp.einsum(
            "scfb,sflb->scl", coupling_faces, vector, precision=lax.Precision.HIGHEST
        )
        primal_local = jnp.einsum(
            "cl,cn->ln",
            primal_rows.reshape(primal_count, loads),
            indicator,
            precision=lax.Precision.HIGHEST,
        )
        primal_sum = lax.psum(primal_local, "sub")
        side_sum = None
        lifted = jnp.dot(
            primal_sum,
            coarse_whole,
            precision=lax.Precision.HIGHEST,
            preferred_element_type=jnp.float32,
        )
        picked = jnp.einsum(
            "ln,cn->cl", lifted, indicator, precision=lax.Precision.HIGHEST
        ).reshape(sub_count, -1, loads)
        coarse_part = jnp.einsum(
            "scfb,scl->sflb", coupling_faces, picked, precision=lax.Precision.HIGHEST
        )
        return (local_part + coarse_part, primal_sum, lifted, side_sum)

    def precond(vector):
        weighted = jnp.einsum(
            "sflb,sfba->sfla",
            vector.astype(jnp.bfloat16),
            face_blocks,
            preferred_element_type=jnp.float32,
        )
        return 0.25 * (weighted - partner_values(weighted, routes))

    def residual_inner(first_vec, second_vec):
        return lax.psum(inner_sum(first_vec, second_vec), "sub")

    response = apply_op(load)[0]
    rhs = response - partner_values(response, routes)
    multipliers = jnp.zeros_like(rhs)
    residual = rhs
    precon_res = precond(residual)
    gamma_now = residual_inner(residual, precon_res)
    direction = precon_res
    for iteration in range(ITERS):
        response, primal_sum, lifted, side_sum = apply_op(direction)
        image_vec = response - partner_values(response, routes)
        curvature_sum = lax.psum(inner_sum(direction, image_vec), "sub")
        step_size = (gamma_now / curvature_sum)[None, None, :, None]
        multipliers = multipliers + step_size * direction
        residual = residual - step_size * image_vec
        if iteration + 1 < ITERS:
            precon_res = precond(residual)
            gamma_new = residual_inner(residual, precon_res)
            direction = precon_res + (gamma_new / gamma_now)[None, None, :, None] * direction
            gamma_now = gamma_new
    return (multipliers, residual)


def solution(mesh):
    return jax.shard_map(
        on_device,
        mesh=mesh,
        in_specs=(
            P(("parts", "sub"), None, None, None),
            P(("parts", "sub"), None, None),
            P(("parts", "sub"), None, None, None),
            P(("parts", "sub"), None, None),
            P(("parts", "sub"), None),
            P(("parts", "sub"), None),
            P(("parts", "sub"), None),
        ),
        out_specs=(P(("parts", "sub"), None, None, None), P(("parts", "sub"), None, None, None)),
        check_vma=False,
    )
```

profile of v0, /device:TPU:0, one launch (start us, length us, event | category | flops | bytes accessed | tf_op | source)
XLA Modules:
  0.0 661.8 jit_solution(14888177187031473002)
XLA Ops:
  10.2 1.6 convolution_bitcast_fusion.4
  11.9 15.1 %copy.90 = bf16[512,8,16,128]{3,2,1,0:T(8,128)(2,1)} copy(bf16[512,8,16,128]{3,1,2,0:T(8,128)(2,1)} %bitcast.293) | data formatting | bytes 33554432
  28.9 63.0 %psum.70 = f32[16,512]{1,0:T(8,128)S(1)} all-reduce(f32[16,512]{1,0:T(8,128)S(1)} %fusion.61), channel_id=1, replica_groups=mesh['parts'=2,'sub'=16] {'sub'}, use_global_device_ids=true, to_apply=%region_0.1 | all-reduce | flops 8192 | bytes 65536 | tf_op jit(solution)/shard_map/psum | solution.py:77
  91.9 10.1 %fusion.9 = f32[2,16,16,128]{3,2,1,0:T(8,128)S(1)} fusion(bf16[2,16,128,16,128]{4,3,2,1,0:T(8,128)(2,1)} %bitcast.289, f32[2,16,16,128]{3,2,1,0:T(8,128)S(1)} %copy-done.8), kind=kOutput, calls=%fused_computation.29 | convolution fusion | flops 268500992 | bytes 17301504 | tf_op jit(solution)/shard_map/sflb,sfbga->sgla/dot_general | solution.py:65
  102.0 1.9 fusion.95
  105.5 1.3 collective-permute-start
  110.7 5.5 collective-permute-start.2
  116.3 4.5 collective-permute-start.1
  120.8 2.8 collective-permute-done.1
  124.6 1.6 gather_fusion.1
  126.7 1.5 gather_fusion.2
  129.5 1.7 collective-permute-start.6
  135.1 7.6 %collective-permute-start.8 = (f32[12,16,128]{2,1,0:T(8,128)S(1)}, f32[12,16,128]{2,1,0:T(8,128)S(1)}, u32[]{:S(2)}, u32[]{:S(2)}) collective-permute-start(f32[12,16,128]{2,1,0:T(8,128)S(1)} %get-tuple-element.45), channel_id=1, source_target_pairs={{0,3},{1,4},{2,5},{3,6},{4,7},{5,8},{6,9},{7,10},{8,11},{9,12},{10... | collective-permute-start | bytes 294920 | tf_op jit(solution)/shard_map/ppermute | solution.py:12
  142.7 4.7 collective-permute-start.7
  147.4 2.7 collective-permute-done.7
  151.1 1.6 gather_fusion.3
  153.3 10.1 %fusion.12 = f32[2,16,16,128]{3,1,2,0:T(8,128)S(1)} fusion(bf16[2,16,128,16,128]{4,3,2,1,0:T(8,128)(2,1)} %bitcast.290, f32[2,16,16,128]{3,2,1,0:T(8,128)S(1)} %sub.79), kind=kOutput, calls=%fused_computation.30 | convolution fusion | flops 268566528 | bytes 17301504 | tf_op jit(solution)/shard_map/sflb,sfbga->sgla/dot_general | solution.py:65
  163.7 57.6 %psum.72 = f32[16,512]{1,0:T(8,128)S(1)} all-reduce(f32[16,512]{1,0:T(8,128)S(1)} %fusion.59), channel_id=1, replica_groups=mesh['parts'=2,'sub'=16] {'sub'}, use_global_device_ids=true, to_apply=%region_7.8 | all-reduce | flops 8192 | bytes 65536 | tf_op jit(solution)/shard_map/psum | solution.py:77
  222.6 1.6 gather_fusion.4
  225.5 1.3 collective-permute-start.12
  226.8 1.3 collective-permute-start.17
  228.1 1.3 collective-permute-start.16
  229.4 1.3 collective-permute-start.15
  230.7 5.5 collective-permute-start.14
  236.3 4.5 collective-permute-start.13
  240.8 2.8 collective-permute-done.13
  244.6 1.8 gather_fusion.5
  246.6 29.5 %all-reduce = (f32[16]{0:T(128)S(1)}, f32[16]{0:T(128)S(1)}) all-reduce(f32[16]{0:T(128)S(1)} %get-tuple-element.3, f32[16]{0:T(128)S(1)} %get-tuple-element.2), channel_id=1, replica_groups=mesh['parts'=2,'sub'=16] {'sub'}, use_global_device_ids=true, to_apply=%region_6.7 | all-reduce | flops 32 | bytes 256 | tf_op jit(solution)/shard_map/psum | solution.py:103
  278.0 1.6 gather_fusion.6
  280.9 1.8 collective-permute-start.18
  286.6 5.5 collective-permute-start.20
  292.1 4.5 collective-permute-start.19
  296.7 2.8 collective-permute-done.19
  300.5 1.8 gather_fusion.7
  302.4 29.5 %psum.74 = f32[16]{0:T(128)S(1)} all-reduce(f32[16]{0:T(128)S(1)} %multiply_reduce_fusion.3), channel_id=1, replica_groups=mesh['parts'=2,'sub'=16] {'sub'}, use_global_device_ids=true, to_apply=%region_11.12 | all-reduce | flops 16 | bytes 128 | tf_op jit(solution)/shard_map/psum | solution.py:103
  333.5 10.8 %fusion.15 = f32[2,16,16,128]{3,1,2,0:T(8,128)} fusion(bf16[2,16,128,16,128]{4,3,2,1,0:T(8,128)(2,1)} %bitcast.291, f32[2,16,16,128]{3,2,1,0:T(8,128)S(1)} %multiply_add_fusion.2), kind=kOutput, calls=%fused_computation.31 | convolution fusion | flops 268500992 | bytes 17301504 | tf_op jit(solution)/shard_map/sflb,sfbga->sgla/dot_general | solution.py:65
  345.3 57.8 %psum.75 = f32[16,512]{1,0:T(8,128)S(1)} all-reduce(f32[16,512]{1,0:T(8,128)S(1)} %fusion.57), channel_id=1, replica_groups=mesh['parts'=2,'sub'=16] {'sub'}, use_global_device_ids=true, to_apply=%region_12.13 | all-reduce | flops 8192 | bytes 65536 | tf_op jit(solution)/shard_map/psum | solution.py:77
  404.7 1.3 convolution_add_fusion.1
  406.0 1.6 gather_fusion.8
  408.9 1.3 collective-permute-start.24
  414.1 5.5 collective-permute-start.26
  419.7 4.5 collective-permute-start.25
  424.8 2.2 collective-permute-done.25
  430.3 2.5 gather_fusion.9
  433.8 29.5 %psum.76 = f32[16]{0:T(128)S(1)} all-reduce(f32[16]{0:T(128)S(1)} %multiply_reduce_fusion.2), channel_id=1, replica_groups=mesh['parts'=2,'sub'=16] {'sub'}, use_global_device_ids=true, to_apply=%region_14.15 | all-reduce | flops 16 | bytes 128 | tf_op jit(solution)/shard_map/psum | solution.py:115
  465.5 1.6 gather_fusion.10
  468.4 1.8 collective-permute-start.30
  474.1 5.5 collective-permute-start.32
  479.6 4.5 collective-permute-start.31
  484.8 2.2 collective-permute-done.31
  490.3 2.5 gather_fusion.11
  493.8 29.5 %psum.77 = f32[16]{0:T(128)S(1)} all-reduce(f32[16]{0:T(128)S(1)} %multiply_reduce_fusion.1), channel_id=1, replica_groups=mesh['parts'=2,'sub'=16] {'sub'}, use_global_device_ids=true, to_apply=%region_16.17 | all-reduce | flops 16 | bytes 128 | tf_op jit(solution)/shard_map/psum | solution.py:103
  525.1 10.8 %fusion.18 = f32[2,16,16,128]{3,1,2,0:T(8,128)} fusion(bf16[2,16,128,16,128]{4,3,2,1,0:T(8,128)(2,1)} %bitcast.292, f32[2,16,16,128]{3,2,1,0:T(8,128)S(1)} %multiply_add_fusion.1), kind=kOutput, calls=%fused_computation.32 | convolution fusion | flops 268500992 | bytes 17301504 | tf_op jit(solution)/shard_map/sflb,sfbga->sgla/dot_general | solution.py:65
  537.1 1.5 fusion.55
  538.6 58.9 %psum.78 = f32[16,512]{1,0:T(8,128)} all-reduce(f32[16,512]{1,0:T(8,128)} %fusion.55), channel_id=1, replica_groups=mesh['parts'=2,'sub'=16] {'sub'}, use_global_device_ids=true, to_apply=%region_17.18 | all-reduce | flops 8192 | bytes 65536 | tf_op jit(solution)/shard_map/psum | solution.py:77
  597.5 1.4 fusion.98
  599.9 1.3 convolution_add_fusion
  601.2 1.6 gather_fusion.12
  604.1 1.3 collective-permute-start.36
  609.3 5.5 collective-permute-start.38
  614.8 4.5 collective-permute-start.37
  619.4 2.8 collective-permute-done.37
  623.2 29.5 %psum.79 = f32[16]{0:T(128)S(1)} all-reduce(f32[16]{0:T(128)S(1)} %multiply_reduce_fusion), channel_id=1, replica_groups=mesh['parts'=2,'sub'=16] {'sub'}, use_global_device_ids=true, to_apply=%region_19.20 | all-reduce | flops 16 | bytes 128 | tf_op jit(solution)/shard_map/psum | solution.py:115
  653.3 1.6 multiply_subtract_fusion
  (213 shorter events, 67.5 us)
Async XLA Ops:
  7.2 119.2 %copy-start = (bf16[2,16,128,128]{3,2,1,0:T(8,128)(2,1)S(1)}, bf16[2,16,128,128]{3,2,1,0:T(8,128)(2,1)}, u32[]{:S(2)}) copy-start(bf16[2,16,128,128]{3,2,1,0:T(8,128)(2,1)} %param.9) | copy-start | bytes 3145732
  7.2 94.8 %all-gather.2.cloned.1.call-start = ((), (), s32[]{:S(2)}) async-start(), calls=%async_computation | async-start | bytes 1114112 | tf_op jit(solution)/shard_map/all_gather | solution.py:61
  10.2 211.7 %copy-start.17 = (s32[48]{0:T(128)}, s32[48]{0:T(128)S(1)}, u32[]{:S(2)}) copy-start(s32[48]{0:T(128)S(1)} %eq.28) | copy-start | bytes 580
  11.9 80.0 %copy-start.8 = (f32[2,16,16,128]{3,2,1,0:T(8,128)S(1)}, f32[2,16,16,128]{3,2,1,0:T(8,128)}, u32[]{:S(2)}) copy-start(f32[2,16,16,128]{3,2,1,0:T(8,128)} %param.7) | copy-start | bytes 786436
  27.1 77.2 %copy-start.1 = (f32[2,24,2048]{2,1,0:T(8,128)S(1)}, f32[2,24,2048]{2,1,0:T(8,128)}, u32[]{:S(2)}) copy-start(f32[2,24,2048]{2,1,0:T(8,128)} %param.10) | copy-start | bytes 1179652
  28.0 122.2 %copy-start.13 = (pred[72]{0:T(512)(128)(4,1)}, pred[72]{0:T(512)(128)(4,1)S(1)}, u32[]{:S(2)}) copy-start(pred[72]{0:T(512)(128)(4,1)S(1)} %scatter_custom_fusion) | copy-start | bytes 220
  91.9 58.3 %copy-start.15 = (s32[1024]{0:T(1024)}, s32[1024]{0:T(1024)S(1)}, u32[]{:S(2)}) copy-start(s32[1024]{0:T(1024)S(1)} %pad_clamp_fusion.1) | copy-start | bytes 12292
  102.0 119.3 %copy-start.2 = (f32[512,512]{1,0:T(8,128)S(1)}, f32[512,512]{1,0:T(8,128)}, u32[]{:S(2)}) copy-start(f32[512,512]{1,0:T(8,128)} %all-gather.2.cloned.1.call-done) | copy-start | bytes 3145732
  105.5 10.8 %collective-permute-start = (f32[12,16,128]{2,1,0:T(8,128)S(1)}, f32[12,16,128]{2,1,0:T(8,128)S(1)}, u32[]{:S(2)}, u32[]{:S(2)}) collective-permute-start(f32[12,16,128]{2,1,0:T(8,128)S(1)} %get-tuple-element.53), channel_id=1, source_target_pairs={{0,1},{1,2},{2,3},{3,4},{4,5},{5,6},{6,7},{7,8},{8,9},{9,10},{10,1... | collective-permute-start | bytes 294920 | tf_op jit(solution)/shard_map/ppermute | solution.py:12
  106.8 115.1 %copy-start.14 = (s32[1024]{0:T(1024)}, s32[1024]{0:T(1024)S(1)}, u32[]{:S(2)}) copy-start(s32[1024]{0:T(1024)S(1)} %pad_clamp_fusion) | copy-start | bytes 12292
  106.8 16.9 %collective-permute-start.5 = (f32[12,16,128]{2,1,0:T(8,128)S(1)}, f32[12,16,128]{2,1,0:T(8,128)S(1)}, u32[]{:S(2)}, u32[]{:S(2)}) collective-permute-start(f32[12,16,128]{2,1,0:T(8,128)S(1)} %get-tuple-element.48), channel_id=1, source_target_pairs={{3,0},{4,1},{5,2},{6,3},{7,4},{8,5},{9,6},{10,7},{11,8},{12,9},{13... | collective-permute-start | bytes 294920 | tf_op jit(solution)/shard_map/ppermute | solution.py:12
  108.1 15.6 %collective-permute-start.4 = (f32[12,16,128]{2,1,0:T(8,128)S(1)}, f32[12,16,128]{2,1,0:T(8,128)S(1)}, u32[]{:S(2)}, u32[]{:S(2)}) collective-permute-start(f32[12,16,128]{2,1,0:T(8,128)S(1)} %get-tuple-element.49), channel_id=1, source_target_pairs={{2,0},{3,1},{4,2},{5,3},{6,4},{7,5},{8,6},{9,7},{10,8},{11,9},{12,... | collective-permute-start | bytes 294920 | tf_op jit(solution)/shard_map/ppermute | solution.py:12
  109.4 14.3 %collective-permute-start.3 = (f32[12,16,128]{2,1,0:T(8,128)S(1)}, f32[12,16,128]{2,1,0:T(8,128)S(1)}, u32[]{:S(2)}, u32[]{:S(2)}) collective-permute-start(f32[12,16,128]{2,1,0:T(8,128)S(1)} %get-tuple-element.50), channel_id=1, source_target_pairs={{1,0},{2,1},{3,2},{4,3},{5,4},{6,5},{7,6},{8,7},{9,8},{10,9},{11,1... | collective-permute-start | bytes 294920 | tf_op jit(solution)/shard_map/ppermute | solution.py:12
  110.7 13.0 %collective-permute-start.2 = (f32[12,16,128]{2,1,0:T(8,128)S(1)}, f32[12,16,128]{2,1,0:T(8,128)S(1)}, u32[]{:S(2)}, u32[]{:S(2)}) collective-permute-start(f32[12,16,128]{2,1,0:T(8,128)S(1)} %get-tuple-element.51), channel_id=1, source_target_pairs={{0,3},{1,4},{2,5},{3,6},{4,7},{5,8},{6,9},{7,10},{8,11},{9,12},{10... | collective-permute-start | bytes 294920 | tf_op jit(solution)/shard_map/ppermute | solution.py:12
  116.3 7.4 %collective-permute-start.1 = (f32[12,16,128]{2,1,0:T(8,128)S(1)}, f32[12,16,128]{2,1,0:T(8,128)S(1)}, u32[]{:S(2)}, u32[]{:S(2)}) collective-permute-start(f32[12,16,128]{2,1,0:T(8,128)S(1)} %get-tuple-element.52), channel_id=1, source_target_pairs={{0,2},{1,3},{2,4},{3,5},{4,6},{5,7},{6,8},{7,9},{8,10},{9,11},{10,... | collective-permute-start | bytes 294920 | tf_op jit(solution)/shard_map/ppermute | solution.py:12
  123.8 0.8 copy-start.9
  129.5 13.2 %collective-permute-start.6 = (f32[12,16,128]{2,1,0:T(8,128)S(1)}, f32[12,16,128]{2,1,0:T(8,128)S(1)}, u32[]{:S(2)}, u32[]{:S(2)}) collective-permute-start(f32[12,16,128]{2,1,0:T(8,128)S(1)} %get-tuple-element.47), channel_id=1, source_target_pairs={{0,1},{1,2},{2,3},{3,4},{4,5},{5,6},{6,7},{7,8},{8,9},{9,10},{10,1... | collective-permute-start | bytes 294920 | tf_op jit(solution)/shard_map/ppermute | solution.py:12
  131.2 19.0 %collective-permute-start.11 = (f32[12,16,128]{2,1,0:T(8,128)S(1)}, f32[12,16,128]{2,1,0:T(8,128)S(1)}, u32[]{:S(2)}, u32[]{:S(2)}) collective-permute-start(f32[12,16,128]{2,1,0:T(8,128)S(1)} %get-tuple-element.42), channel_id=1, source_target_pairs={{3,0},{4,1},{5,2},{6,3},{7,4},{8,5},{9,6},{10,7},{11,8},{12,9},{13... | collective-permute-start | bytes 294920 | tf_op jit(solution)/shard_map/ppermute | solution.py:12
  132.5 17.6 %collective-permute-start.10 = (f32[12,16,128]{2,1,0:T(8,128)S(1)}, f32[12,16,128]{2,1,0:T(8,128)S(1)}, u32[]{:S(2)}, u32[]{:S(2)}) collective-permute-start(f32[12,16,128]{2,1,0:T(8,128)S(1)} %get-tuple-element.43), channel_id=1, source_target_pairs={{2,0},{3,1},{4,2},{5,3},{6,4},{7,5},{8,6},{9,7},{10,8},{11,9},{12,... | collective-permute-start | bytes 294920 | tf_op jit(solution)/shard_map/ppermute | solution.py:12
  133.8 16.3 %collective-permute-start.9 = (f32[12,16,128]{2,1,0:T(8,128)S(1)}, f32[12,16,128]{2,1,0:T(8,128)S(1)}, u32[]{:S(2)}, u32[]{:S(2)}) collective-permute-start(f32[12,16,128]{2,1,0:T(8,128)S(1)} %get-tuple-element.44), channel_id=1, source_target_pairs={{1,0},{2,1},{3,2},{4,3},{5,4},{6,5},{7,6},{8,7},{9,8},{10,9},{11,1... | collective-permute-start | bytes 294920 | tf_op jit(solution)/shard_map/ppermute | solution.py:12
  135.1 15.0 %collective-permute-start.8 = (f32[12,16,128]{2,1,0:T(8,128)S(1)}, f32[12,16,128]{2,1,0:T(8,128)S(1)}, u32[]{:S(2)}, u32[]{:S(2)}) collective-permute-start(f32[12,16,128]{2,1,0:T(8,128)S(1)} %get-tuple-element.45), channel_id=1, source_target_pairs={{0,3},{1,4},{2,5},{3,6},{4,7},{5,8},{6,9},{7,10},{8,11},{9,12},{10... | collective-permute-start | bytes 294920 | tf_op jit(solution)/shard_map/ppermute | solution.py:12
  142.7 7.4 %collective-permute-start.7 = (f32[12,16,128]{2,1,0:T(8,128)S(1)}, f32[12,16,128]{2,1,0:T(8,128)S(1)}, u32[]{:S(2)}, u32[]{:S(2)}) collective-permute-start(f32[12,16,128]{2,1,0:T(8,128)S(1)} %get-tuple-element.46), channel_id=1, source_target_pairs={{0,2},{1,3},{2,4},{3,5},{4,6},{5,7},{6,8},{7,9},{8,10},{9,11},{10,... | collective-permute-start | bytes 294920 | tf_op jit(solution)/shard_map/ppermute | solution.py:12
  150.2 0.8 copy-start.10
  225.5 10.7 %collective-permute-start.12 = (f32[12,16,128]{2,1,0:T(8,128)S(1)}, f32[12,16,128]{2,1,0:T(8,128)S(1)}, u32[]{:S(2)}, u32[]{:S(2)}) collective-permute-start(f32[12,16,128]{2,1,0:T(8,128)S(1)} %get-tuple-element.41), channel_id=1, source_target_pairs={{0,1},{1,2},{2,3},{3,4},{4,5},{5,6},{6,7},{7,8},{8,9},{9,10},{10,1... | collective-permute-start | bytes 294920 | tf_op jit(solution)/shard_map/ppermute | solution.py:12
  226.8 16.9 %collective-permute-start.17 = (f32[12,16,128]{2,1,0:T(8,128)S(1)}, f32[12,16,128]{2,1,0:T(8,128)S(1)}, u32[]{:S(2)}, u32[]{:S(2)}) collective-permute-start(f32[12,16,128]{2,1,0:T(8,128)S(1)} %get-tuple-element.36), channel_id=1, source_target_pairs={{3,0},{4,1},{5,2},{6,3},{7,4},{8,5},{9,6},{10,7},{11,8},{12,9},{13... | collective-permute-start | bytes 294920 | tf_op jit(solution)/shard_map/ppermute | solution.py:12
  228.1 15.6 %collective-permute-start.16 = (f32[12,16,128]{2,1,0:T(8,128)S(1)}, f32[12,16,128]{2,1,0:T(8,128)S(1)}, u32[]{:S(2)}, u32[]{:S(2)}) collective-permute-start(f32[12,16,128]{2,1,0:T(8,128)S(1)} %get-tuple-element.37), channel_id=1, source_target_pairs={{2,0},{3,1},{4,2},{5,3},{6,4},{7,5},{8,6},{9,7},{10,8},{11,9},{12,... | collective-permute-start | bytes 294920 | tf_op jit(solution)/shard_map/ppermute | solution.py:12
  229.4 14.3 %collective-permute-start.15 = (f32[12,16,128]{2,1,0:T(8,128)S(1)}, f32[12,16,128]{2,1,0:T(8,128)S(1)}, u32[]{:S(2)}, u32[]{:S(2)}) collective-permute-start(f32[12,16,128]{2,1,0:T(8,128)S(1)} %get-tuple-element.38), channel_id=1, source_target_pairs={{1,0},{2,1},{3,2},{4,3},{5,4},{6,5},{7,6},{8,7},{9,8},{10,9},{11,1... | collective-permute-start | bytes 294920 | tf_op jit(solution)/shard_map/ppermute | solution.py:12
  230.7 13.0 %collective-permute-start.14 = (f32[12,16,128]{2,1,0:T(8,128)S(1)}, f32[12,16,128]{2,1,0:T(8,128)S(1)}, u32[]{:S(2)}, u32[]{:S(2)}) collective-permute-start(f32[12,16,128]{2,1,0:T(8,128)S(1)} %get-tuple-element.39), channel_id=1, source_target_pairs={{0,3},{1,4},{2,5},{3,6},{4,7},{5,8},{6,9},{7,10},{8,11},{9,12},{10... | collective-permute-start | bytes 294920 | tf_op jit(solution)/shard_map/ppermute | solution.py:12
  236.3 7.4 %collective-permute-start.13 = (f32[12,16,128]{2,1,0:T(8,128)S(1)}, f32[12,16,128]{2,1,0:T(8,128)S(1)}, u32[]{:S(2)}, u32[]{:S(2)}) collective-permute-start(f32[12,16,128]{2,1,0:T(8,128)S(1)} %get-tuple-element.40), channel_id=1, source_target_pairs={{0,2},{1,3},{2,4},{3,5},{4,6},{5,7},{6,8},{7,9},{8,10},{9,11},{10,... | collective-permute-start | bytes 294920 | tf_op jit(solution)/shard_map/ppermute | solution.py:12
  243.8 0.8 copy-start.11
  246.4 30.2 %copy-start.6 = (f32[32,16,128]{2,1,0:T(8,128)}, f32[32,16,128]{2,1,0:T(8,128)S(1)}, u32[]{:S(2)}) copy-start(f32[32,16,128]{2,1,0:T(8,128)S(1)} %gather_fusion.5) | copy-start | bytes 786436
  277.6 185.7 %copy-start.5 = (f32[2,16,16,128]{3,2,1,0:T(8,128)}, f32[2,16,16,128]{3,2,1,0:T(8,128)S(1)}, u32[]{:S(2)}) copy-start(f32[2,16,16,128]{3,2,1,0:T(8,128)S(1)} %multiply_subtract_fusion.2) | copy-start | bytes 786436
  280.9 11.2 %collective-permute-start.18 = (f32[12,16,128]{2,1,0:T(8,128)S(1)}, f32[12,16,128]{2,1,0:T(8,128)S(1)}, u32[]{:S(2)}, u32[]{:S(2)}) collective-permute-start(f32[12,16,128]{2,1,0:T(8,128)S(1)} %get-tuple-element.35), channel_id=1, source_target_pairs={{0,1},{1,2},{2,3},{3,4},{4,5},{5,6},{6,7},{7,8},{8,9},{9,10},{10,1... | collective-permute-start | bytes 294920 | tf_op jit(solution)/shard_map/ppermute | solution.py:12
  282.7 16.9 %collective-permute-start.23 = (f32[12,16,128]{2,1,0:T(8,128)S(1)}, f32[12,16,128]{2,1,0:T(8,128)S(1)}, u32[]{:S(2)}, u32[]{:S(2)}) collective-permute-start(f32[12,16,128]{2,1,0:T(8,128)S(1)} %get-tuple-element.30), channel_id=1, source_target_pairs={{3,0},{4,1},{5,2},{6,3},{7,4},{8,5},{9,6},{10,7},{11,8},{12,9},{13... | collective-permute-start | bytes 294920 | tf_op jit(solution)/shard_map/ppermute | solution.py:12
  284.0 15.6 %collective-permute-start.22 = (f32[12,16,128]{2,1,0:T(8,128)S(1)}, f32[12,16,128]{2,1,0:T(8,128)S(1)}, u32[]{:S(2)}, u32[]{:S(2)}) collective-permute-start(f32[12,16,128]{2,1,0:T(8,128)S(1)} %get-tuple-element.31), channel_id=1, source_target_pairs={{2,0},{3,1},{4,2},{5,3},{6,4},{7,5},{8,6},{9,7},{10,8},{11,9},{12,... | collective-permute-start | bytes 294920 | tf_op jit(solution)/shard_map/ppermute | solution.py:12
  285.3 14.3 %collective-permute-start.21 = (f32[12,16,128]{2,1,0:T(8,128)S(1)}, f32[12,16,128]{2,1,0:T(8,128)S(1)}, u32[]{:S(2)}, u32[]{:S(2)}) collective-permute-start(f32[12,16,128]{2,1,0:T(8,128)S(1)} %get-tuple-element.32), channel_id=1, source_target_pairs={{1,0},{2,1},{3,2},{4,3},{5,4},{6,5},{7,6},{8,7},{9,8},{10,9},{11,1... | collective-permute-start | bytes 294920 | tf_op jit(solution)/shard_map/ppermute | solution.py:12
  286.6 13.0 %collective-permute-start.20 = (f32[12,16,128]{2,1,0:T(8,128)S(1)}, f32[12,16,128]{2,1,0:T(8,128)S(1)}, u32[]{:S(2)}, u32[]{:S(2)}) collective-permute-start(f32[12,16,128]{2,1,0:T(8,128)S(1)} %get-tuple-element.33), channel_id=1, source_target_pairs={{0,3},{1,4},{2,5},{3,6},{4,7},{5,8},{6,9},{7,10},{8,11},{9,12},{10... | collective-permute-start | bytes 294920 | tf_op jit(solution)/shard_map/ppermute | solution.py:12
  292.1 7.4 %collective-permute-start.19 = (f32[12,16,128]{2,1,0:T(8,128)S(1)}, f32[12,16,128]{2,1,0:T(8,128)S(1)}, u32[]{:S(2)}, u32[]{:S(2)}) collective-permute-start(f32[12,16,128]{2,1,0:T(8,128)S(1)} %get-tuple-element.34), channel_id=1, source_target_pairs={{0,2},{1,3},{2,4},{3,5},{4,6},{5,7},{6,8},{7,9},{8,10},{9,11},{10,... | collective-permute-start | bytes 294920 | tf_op jit(solution)/shard_map/ppermute | solution.py:12
  299.6 0.8 copy-start.12
  302.2 29.7 %copy-start.7 = (f32[32,16,128]{2,1,0:T(8,128)}, f32[32,16,128]{2,1,0:T(8,128)S(1)}, u32[]{:S(2)}) copy-start(f32[32,16,128]{2,1,0:T(8,128)S(1)} %gather_fusion.7) | copy-start | bytes 786436
  331.9 71.8 %copy-start.18 = (f32[16]{0:T(128)}, f32[16]{0:T(128)S(1)}, u32[]{:S(2)}) copy-start(f32[16]{0:T(128)S(1)} %psum.74) | copy-start | bytes 196
  408.9 10.7 %collective-permute-start.24 = (f32[12,16,128]{2,1,0:T(8,128)S(1)}, f32[12,16,128]{2,1,0:T(8,128)S(1)}, u32[]{:S(2)}, u32[]{:S(2)}) collective-permute-start(f32[12,16,128]{2,1,0:T(8,128)S(1)} %get-tuple-element.29), channel_id=1, source_target_pairs={{0,1},{1,2},{2,3},{3,4},{4,5},{5,6},{6,7},{7,8},{8,9},{9,10},{10,1... | collective-permute-start | bytes 294920 | tf_op jit(solution)/shard_map/ppermute | solution.py:12
  410.2 19.4 %collective-permute-start.29 = (f32[12,16,128]{2,1,0:T(8,128)S(1)}, f32[12,16,128]{2,1,0:T(8,128)S(1)}, u32[]{:S(2)}, u32[]{:S(2)}) collective-permute-start(f32[12,16,128]{2,1,0:T(8,128)S(1)} %get-tuple-element.24), channel_id=1, source_target_pairs={{3,0},{4,1},{5,2},{6,3},{7,4},{8,5},{9,6},{10,7},{11,8},{12,9},{13... | collective-permute-start | bytes 294920 | tf_op jit(solution)/shard_map/ppermute | solution.py:12
  411.5 17.5 %collective-permute-start.28 = (f32[12,16,128]{2,1,0:T(8,128)S(1)}, f32[12,16,128]{2,1,0:T(8,128)S(1)}, u32[]{:S(2)}, u32[]{:S(2)}) collective-permute-start(f32[12,16,128]{2,1,0:T(8,128)S(1)} %get-tuple-element.25), channel_id=1, source_target_pairs={{2,0},{3,1},{4,2},{5,3},{6,4},{7,5},{8,6},{9,7},{10,8},{11,9},{12,... | collective-permute-start | bytes 294920 | tf_op jit(solution)/shard_map/ppermute | solution.py:12
  412.8 15.5 %collective-permute-start.27 = (f32[12,16,128]{2,1,0:T(8,128)S(1)}, f32[12,16,128]{2,1,0:T(8,128)S(1)}, u32[]{:S(2)}, u32[]{:S(2)}) collective-permute-start(f32[12,16,128]{2,1,0:T(8,128)S(1)} %get-tuple-element.26), channel_id=1, source_target_pairs={{1,0},{2,1},{3,2},{4,3},{5,4},{6,5},{7,6},{8,7},{9,8},{10,9},{11,1... | collective-permute-start | bytes 294920 | tf_op jit(solution)/shard_map/ppermute | solution.py:12
  414.1 13.6 %collective-permute-start.26 = (f32[12,16,128]{2,1,0:T(8,128)S(1)}, f32[12,16,128]{2,1,0:T(8,128)S(1)}, u32[]{:S(2)}, u32[]{:S(2)}) collective-permute-start(f32[12,16,128]{2,1,0:T(8,128)S(1)} %get-tuple-element.27), channel_id=1, source_target_pairs={{0,3},{1,4},{2,5},{3,6},{4,7},{5,8},{6,9},{7,10},{8,11},{9,12},{10... | collective-permute-start | bytes 294920 | tf_op jit(solution)/shard_map/ppermute | solution.py:12
  419.7 7.4 %collective-permute-start.25 = (f32[12,16,128]{2,1,0:T(8,128)S(1)}, f32[12,16,128]{2,1,0:T(8,128)S(1)}, u32[]{:S(2)}, u32[]{:S(2)}) collective-permute-start(f32[12,16,128]{2,1,0:T(8,128)S(1)} %get-tuple-element.28), channel_id=1, source_target_pairs={{0,2},{1,3},{2,4},{3,5},{4,6},{5,7},{6,8},{7,9},{8,10},{9,11},{10,... | collective-permute-start | bytes 294920 | tf_op jit(solution)/shard_map/ppermute | solution.py:12
  464.0 1.1 copy-start.16
  465.1 58.2 %copy-start.3 = (f32[2,16,16,128]{3,2,1,0:T(8,128)}, f32[2,16,16,128]{3,2,1,0:T(8,128)S(1)}, u32[]{:S(2)}) copy-start(f32[2,16,16,128]{3,2,1,0:T(8,128)S(1)} %multiply_subtract_fusion.1) | copy-start | bytes 786436
  468.4 11.2 %collective-permute-start.30 = (f32[12,16,128]{2,1,0:T(8,128)S(1)}, f32[12,16,128]{2,1,0:T(8,128)S(1)}, u32[]{:S(2)}, u32[]{:S(2)}) collective-permute-start(f32[12,16,128]{2,1,0:T(8,128)S(1)} %get-tuple-element.23), channel_id=1, source_target_pairs={{0,1},{1,2},{2,3},{3,4},{4,5},{5,6},{6,7},{7,8},{8,9},{9,10},{10,1... | collective-permute-start | bytes 294920 | tf_op jit(solution)/shard_map/ppermute | solution.py:12
  470.2 19.4 %collective-permute-start.35 = (f32[12,16,128]{2,1,0:T(8,128)S(1)}, f32[12,16,128]{2,1,0:T(8,128)S(1)}, u32[]{:S(2)}, u32[]{:S(2)}) collective-permute-start(f32[12,16,128]{2,1,0:T(8,128)S(1)} %get-tuple-element.18), channel_id=1, source_target_pairs={{3,0},{4,1},{5,2},{6,3},{7,4},{8,5},{9,6},{10,7},{11,8},{12,9},{13... | collective-permute-start | bytes 294920 | tf_op jit(solution)/shard_map/ppermute | solution.py:12
  471.5 17.5 %collective-permute-start.34 = (f32[12,16,128]{2,1,0:T(8,128)S(1)}, f32[12,16,128]{2,1,0:T(8,128)S(1)}, u32[]{:S(2)}, u32[]{:S(2)}) collective-permute-start(f32[12,16,128]{2,1,0:T(8,128)S(1)} %get-tuple-element.19), channel_id=1, source_target_pairs={{2,0},{3,1},{4,2},{5,3},{6,4},{7,5},{8,6},{9,7},{10,8},{11,9},{12,... | collective-permute-start | bytes 294920 | tf_op jit(solution)/shard_map/ppermute | solution.py:12
  472.8 15.5 %collective-permute-start.33 = (f32[12,16,128]{2,1,0:T(8,128)S(1)}, f32[12,16,128]{2,1,0:T(8,128)S(1)}, u32[]{:S(2)}, u32[]{:S(2)}) collective-permute-start(f32[12,16,128]{2,1,0:T(8,128)S(1)} %get-tuple-element.20), channel_id=1, source_target_pairs={{1,0},{2,1},{3,2},{4,3},{5,4},{6,5},{7,6},{8,7},{9,8},{10,9},{11,1... | collective-permute-start | bytes 294920 | tf_op jit(solution)/shard_map/ppermute | solution.py:12
  474.1 13.6 %collective-permute-start.32 = (f32[12,16,128]{2,1,0:T(8,128)S(1)}, f32[12,16,128]{2,1,0:T(8,128)S(1)}, u32[]{:S(2)}, u32[]{:S(2)}) collective-permute-start(f32[12,16,128]{2,1,0:T(8,128)S(1)} %get-tuple-element.21), channel_id=1, source_target_pairs={{0,3},{1,4},{2,5},{3,6},{4,7},{5,8},{6,9},{7,10},{8,11},{9,12},{10... | collective-permute-start | bytes 294920 | tf_op jit(solution)/shard_map/ppermute | solution.py:12
  479.6 7.4 %collective-permute-start.31 = (f32[12,16,128]{2,1,0:T(8,128)S(1)}, f32[12,16,128]{2,1,0:T(8,128)S(1)}, u32[]{:S(2)}, u32[]{:S(2)}) collective-permute-start(f32[12,16,128]{2,1,0:T(8,128)S(1)} %get-tuple-element.22), channel_id=1, source_target_pairs={{0,2},{1,3},{2,4},{3,5},{4,6},{5,7},{6,8},{7,9},{8,10},{9,11},{10,... | collective-permute-start | bytes 294920 | tf_op jit(solution)/shard_map/ppermute | solution.py:12
  523.3 12.6 %copy-start.19 = (f32[16]{0:T(128)}, f32[16]{0:T(128)S(1)}, u32[]{:S(2)}) copy-start(f32[16]{0:T(128)S(1)} %psum.77) | copy-start | bytes 196
  525.0 128.3 %copy-start.4 = (f32[2,16,16,128]{3,2,1,0:T(8,128)S(1)}, f32[2,16,16,128]{3,2,1,0:T(8,128)}, u32[]{:S(2)}) copy-start(f32[2,16,16,128]{3,2,1,0:T(8,128)} %copy-done.3) | copy-start | bytes 786436
  604.1 10.7 %collective-permute-start.36 = (f32[12,16,128]{2,1,0:T(8,128)S(1)}, f32[12,16,128]{2,1,0:T(8,128)S(1)}, u32[]{:S(2)}, u32[]{:S(2)}) collective-permute-start(f32[12,16,128]{2,1,0:T(8,128)S(1)} %get-tuple-element.17), channel_id=1, source_target_pairs={{0,1},{1,2},{2,3},{3,4},{4,5},{5,6},{6,7},{7,8},{8,9},{9,10},{10,1... | collective-permute-start | bytes 294920 | tf_op jit(solution)/shard_map/ppermute | solution.py:12
  605.4 16.9 %collective-permute-start.41 = (f32[12,16,128]{2,1,0:T(8,128)S(1)}, f32[12,16,128]{2,1,0:T(8,128)S(1)}, u32[]{:S(2)}, u32[]{:S(2)}) collective-permute-start(f32[12,16,128]{2,1,0:T(8,128)S(1)} %get-tuple-element.12), channel_id=1, source_target_pairs={{3,0},{4,1},{5,2},{6,3},{7,4},{8,5},{9,6},{10,7},{11,8},{12,9},{13... | collective-permute-start | bytes 294920 | tf_op jit(solution)/shard_map/ppermute | solution.py:12
  606.7 15.6 %collective-permute-start.40 = (f32[12,16,128]{2,1,0:T(8,128)S(1)}, f32[12,16,128]{2,1,0:T(8,128)S(1)}, u32[]{:S(2)}, u32[]{:S(2)}) collective-permute-start(f32[12,16,128]{2,1,0:T(8,128)S(1)} %get-tuple-element.13), channel_id=1, source_target_pairs={{2,0},{3,1},{4,2},{5,3},{6,4},{7,5},{8,6},{9,7},{10,8},{11,9},{12,... | collective-permute-start | bytes 294920 | tf_op jit(solution)/shard_map/ppermute | solution.py:12
  608.0 14.3 %collective-permute-start.39 = (f32[12,16,128]{2,1,0:T(8,128)S(1)}, f32[12,16,128]{2,1,0:T(8,128)S(1)}, u32[]{:S(2)}, u32[]{:S(2)}) collective-permute-start(f32[12,16,128]{2,1,0:T(8,128)S(1)} %get-tuple-element.14), channel_id=1, source_target_pairs={{1,0},{2,1},{3,2},{4,3},{5,4},{6,5},{7,6},{8,7},{9,8},{10,9},{11,1... | collective-permute-start | bytes 294920 | tf_op jit(solution)/shard_map/ppermute | solution.py:12
  609.3 13.0 %collective-permute-start.38 = (f32[12,16,128]{2,1,0:T(8,128)S(1)}, f32[12,16,128]{2,1,0:T(8,128)S(1)}, u32[]{:S(2)}, u32[]{:S(2)}) collective-permute-start(f32[12,16,128]{2,1,0:T(8,128)S(1)} %get-tuple-element.15), channel_id=1, source_target_pairs={{0,3},{1,4},{2,5},{3,6},{4,7},{5,8},{6,9},{7,10},{8,11},{9,12},{10... | collective-permute-start | bytes 294920 | tf_op jit(solution)/shard_map/ppermute | solution.py:12
  614.8 7.4 %collective-permute-start.37 = (f32[12,16,128]{2,1,0:T(8,128)S(1)}, f32[12,16,128]{2,1,0:T(8,128)S(1)}, u32[]{:S(2)}, u32[]{:S(2)}) collective-permute-start(f32[12,16,128]{2,1,0:T(8,128)S(1)} %get-tuple-element.16), channel_id=1, source_target_pairs={{0,2},{1,3},{2,4},{3,5},{4,6},{5,7},{6,8},{7,9},{8,10},{9,11},{10,... | collective-permute-start | bytes 294920 | tf_op jit(solution)/shard_map/ppermute | solution.py:12
Sparse Core Ops, SparseCore 0:
  10.2 40.6 all-gather.1
where the time goes:
time: 664 us; the launch traced here: 662 us
  blocking collectives  385 us (58%)
  starting transfers between devices  110 us (17%)
  matrix products  59 us (9%)
  local copies, waits for them, and re-layouts  54.4 us (8%)
  waiting for transfers between devices  19.3 us (3%)
  other arithmetic  18.8 us (3%)
  between operations  15.3 us (2%)
    psum x4, blocking collectives, apply_op(): primal_sum = lax.psum(primal_local, 'sub')  237 us
    ppermute x42, starting transfers between devices, shifted(): return lax.ppermute(value, axis, pairs)  110 us
    psum x3, blocking collectives, residual_inner(): return lax.psum(inner_sum(first_vec, second_vec), 'sub')  88.5 us
    psum x2, blocking collectives, on_device(): curvature_sum = lax.psum(inner_sum(direction, image_vec), 'sub')  59 us
    dot_general x4, matrix products, apply_op(): jnp.einsum('sflb,sfbga->sgla', rounded, stiff_faces, preferred_element_ty...  41.9 us
    unnamed x76, local copies, waits for them, and re-layouts  25.1 us
    ppermute x42, waiting for transfers between devices, shifted(): return lax.ppermute(value, axis, pairs)  18.6 us
  transfers between devices with their start and end apart: 43, of which 7 were waited for; matrix products, arithmetic and copies ran while one was open for 6% of the time, Pallas kernels for 0%

commit v1 on v0

v1 whole, which is shorter than its diff:
```python
import functools
import jax
import jax.numpy as jnp
from jax import lax
from jax.experimental import pallas as pl
from jax.experimental.pallas import tpu as pltpu
from jax.sharding import PartitionSpec as P

ITERS = 3
LANES = 6
PAD = 32
WIDE = 128
BF = jnp.bfloat16
F32 = jnp.float32
VMEM = pl.BlockSpec(memory_space=pltpu.VMEM)
SMEM = pl.BlockSpec(memory_space=pltpu.SMEM)
HBM = pl.BlockSpec(memory_space=pl.ANY)


def completed(pairs, devices):
    table = dict(pairs)
    table.update({second: first for first, second in pairs})
    free = [i for i in range(devices) if i not in table]
    for first, second in zip(free[0::2], free[1::2]):
        table[first] = second
        table[second] = first
    return sorted(table.items())


def flipped(mask, devices):
    return [(i, i ^ mask) for i in range(devices)]


def lane_pairs(devices):
    odd = range(2, devices - 2, 4)
    return (
        flipped(1, devices),
        flipped(2, devices),
        flipped(3, devices),
        completed([(i + core, i + 2 + core) for i in odd for core in (0, 1)], devices),
        completed([(i + core, i + 3 - core) for i in odd for core in (0, 1)], devices),
        completed([(i, i + 3) for i in range(1, devices - 3, 2)], devices),
    )


def split_hi_lo(value):
    high = value.astype(BF)
    return high, (value - high.astype(F32)).astype(BF)


def routing(partner, capacity):
    face_count = partner.size
    subs = partner.shape[0]
    own = lax.axis_index("sub")
    ids = partner.reshape(face_count)
    peer = ids // face_count
    chip_gap = jnp.abs(peer // 2 - own // 2)
    lowest = jnp.minimum(peer // 2, own // 2)
    crossed = (peer + own) % 2
    lane = jnp.where(chip_gap == 0, 0, jnp.where(chip_gap == 1, 1 + 2 * (lowest % 2) + crossed, 5))
    order = jnp.arange(face_count, dtype=jnp.int32)
    same = lane[:, None] == lane[None, :]
    send_pos = jnp.sum(same & (order[None, :] < order[:, None]), axis=1, dtype=jnp.int32)
    recv_pos = jnp.sum(same & (ids[None, :] < ids[:, None]), axis=1, dtype=jnp.int32)
    slots = jnp.arange(LANES * capacity, dtype=jnp.int32)
    hit = slots[:, None] == (lane * capacity + send_pos)[None, :]
    source = jnp.sum(jnp.where(hit, order[None, :], 0), axis=1, dtype=jnp.int32)
    arrival = lane * capacity + recv_pos
    block = (1 + lane) * subs + (ids // partner.shape[1]) % subs
    return jnp.concatenate([source, arrival, block]).astype(jnp.int32)


class Sizes:
    def __init__(self, load, coupling, coarse_inv):
        self.subs, self.faces, self.loads, self.dof = load.shape
        self.total = self.subs * self.faces
        self.unknowns = self.faces * self.dof
        self.slots_per_lane = 3 * self.total // 8
        self.slots = LANES * self.slots_per_lane
        self.primal = coupling.shape[1]
        self.coarse = coarse_inv.shape[1]
        self.blocks = (1 + LANES) * self.subs
        self.pick_width = -(-self.blocks * PAD // WIDE) * WIDE
        self.carry_rows = self.slots_per_lane * self.primal + 8
        self.small_width = self.coarse + WIDE


def call(kernel, sizes, outs, ins, specs, scratch, limit, name, flops=0, moved=0):
    return pl.pallas_call(
        functools.partial(kernel, sizes),
        out_shape=outs,
        in_specs=specs,
        out_specs=[VMEM] * len(outs),
        scratch_shapes=scratch,
        compiler_params=pltpu.CompilerParams(vmem_limit_bytes=limit * 2**20),
        cost_estimate=pl.CostEstimate(flops=flops, bytes_accessed=moved, transcendentals=0),
        name=name,
    )(*ins)


def shape(*dims, dtype=F32):
    return jax.ShapeDtypeStruct(dims, dtype)


def pack_kernel(z, tab, coupling, corner_row, *rest):
    lanes, weights = rest[:LANES], rest[LANES]
    for lane in range(LANES):
        for pos in range(z.slots_per_lane):
            face = tab[lane * z.slots_per_lane + pos]
            sub = face // z.faces
            start = pl.multiple_of((face - sub * z.faces) * z.dof, z.dof)
            lanes[lane][pos * z.primal:(pos + 1) * z.primal, :] = coupling[sub, :, pl.ds(start, z.dof)]
        lanes[lane][z.slots_per_lane * z.primal:, :] = corner_row[...]
    weights[...] = jnp.zeros_like(weights)
    gap = jnp.zeros((PAD - z.primal, z.unknowns), F32)
    for sub in range(z.subs):
        high, low = split_hi_lo(jnp.concatenate([coupling[sub], gap], axis=0))
        weights[sub, sub * 2 * PAD:sub * 2 * PAD + PAD, :] = high
        weights[sub, sub * 2 * PAD + PAD:sub * 2 * PAD + 2 * PAD, :] = low


def unpack_kernel(z, tab, coupling, corner_row, *rest):
    arrived, rest = rest[:LANES], rest[LANES:]
    spread, pick, held, names = rest
    per = z.slots_per_lane
    width = z.subs * PAD
    names[...] = jnp.full(names.shape, -1.0, F32)
    names[:, 0:width] = corner_row[:, 0:width]
    for lane in range(LANES):
        names[:, (1 + lane) * width:(2 + lane) * width] = arrived[lane][per * z.primal:, 0:width]
        for pos in range(per):
            held[lane * per + pos] = arrived[lane][pos * z.primal:(pos + 1) * z.primal, :]
    rows = lax.broadcasted_iota(jnp.int32, pick.shape, 0).astype(F32)
    pick[...] = jnp.where(rows == names[0:1, :], 1.0, 0.0).astype(BF)
    gap = jnp.zeros((PAD - z.primal, z.dof), F32)
    blank = jnp.zeros((PAD, z.dof), BF)
    for face in range(z.total):
        sub, side = face // z.faces, face % z.faces
        own = coupling[sub, :, side * z.dof:(side + 1) * z.dof]
        other = -held[tab[z.slots + face]]
        for place, value in enumerate((own, other)):
            high, low = split_hi_lo(jnp.concatenate([value, gap], axis=0))
            spread[face, place * 4 * PAD:(place + 1) * 4 * PAD, :] = jnp.concatenate([high, low, high, blank], axis=0)


def stiff_copies(z, stiff, buffer, sems):
    step = z.unknowns // 8
    return [
        pltpu.make_async_copy(
            stiff.at[sub, pl.ds(part * step, step), :],
            buffer.at[sub, pl.ds(part * step, step), :],
            sems.at[sub * 8 + part],
        )
        for sub in range(z.subs)
        for part in range(8)
    ]


def apply_in_kernel(z, tab, vec, gamma, eta, weights, spot, copies, buffer, packed, image, small, lanes):
    for face in range(z.total):
        sub, side = face // z.faces, face % z.faces
        high, low = split_hi_lo(vec[face])
        packed[sub, 0:z.loads, side * z.dof:(side + 1) * z.dof] = high
        packed[sub, z.loads:, side * z.dof:(side + 1) * z.dof] = low
    rows = None
    for sub in range(z.subs):
        part = lax.dot_general(
            packed[sub], weights[sub], (((1,), (1,)), ((), ())), preferred_element_type=F32
        )
        rows = part if rows is None else rows + part
    high, low = split_hi_lo(rows)
    summed = jnp.dot(jnp.concatenate([high, low], axis=0), spot[...], preferred_element_type=F32)
    n = z.loads
    small[:, 0:z.coarse] = (summed[0:n] + summed[n:2 * n]) + (summed[2 * n:3 * n] + summed[3 * n:])
    step = z.unknowns // 8
    kappa = jnp.zeros((z.loads, z.dof), F32)
    for sub in range(z.subs):
        total = jnp.zeros((2 * z.loads, z.unknowns), F32)
        for part in range(8):
            copies[sub * 8 + part].wait()
            total = total + jnp.dot(
                packed[sub, :, part * step:(part + 1) * step],
                buffer[sub, part * step:(part + 1) * step, :],
                preferred_element_type=F32,
            )
        total = total[0:n] + total[n:]
        for side in range(z.faces):
            piece = total[:, side * z.dof:(side + 1) * z.dof]
            image[sub * z.faces + side] = piece
            kappa = kappa + piece * vec[sub * z.faces + side]
    column = lax.broadcasted_iota(jnp.int32, (z.loads, WIDE), 1)
    tail = jnp.where(column == 1, jnp.sum(kappa, axis=1, keepdims=True), 0.0)
    if gamma is not None:
        tail = jnp.where(column == 0, jnp.sum(gamma, axis=1, keepdims=True), tail)
        tail = jnp.where(column == 2, jnp.sum(eta, axis=1, keepdims=True), tail)
    small[:, z.coarse:] = tail
    fill_lanes(z, tab, image, lanes)


def fill_lanes(z, tab, field, lanes):
    for lane in range(LANES):
        for pos in range(z.slots_per_lane):
            lanes[lane][pos] = field[tab[lane * z.slots_per_lane + pos]]


def take_lanes(z, arrived, held):
    per = z.slots_per_lane
    for lane in range(LANES):
        held[lane * per:(lane + 1) * per] = arrived[lane][...]


def load_kernel(z, tab, load, weights, spot, stiff, image, small, *rest):
    lanes, (buffer, packed, sems) = rest[:LANES], rest[LANES:]
    copies = stiff_copies(z, stiff, buffer, sems)
    for copy in copies:
        copy.start()
    apply_in_kernel(z, tab, load, None, None, weights, spot, copies, buffer, packed, image, small, lanes)


def precond_kernel(z, tab, weighted, residual, old_image, weights, spot, stiff, *rest):
    arrived, rest = rest[:LANES], rest[LANES:]
    vec, image, small = rest[:3]
    lanes, (buffer, packed, sems, held) = rest[3:3 + LANES], rest[3 + LANES:]
    copies = stiff_copies(z, stiff, buffer, sems)
    for copy in copies:
        copy.start()
    take_lanes(z, arrived, held)
    gamma = jnp.zeros((z.loads, z.dof), F32)
    eta = jnp.zeros((z.loads, z.dof), F32)
    for face in range(z.total):
        value = 0.25 * (weighted[face] - held[tab[z.slots + face]])
        vec[face] = value
        gamma = gamma + residual[face] * value
        eta = eta + old_image[face] * value
    apply_in_kernel(z, tab, vec, gamma, eta, weights, spot, copies, buffer, packed, image, small, lanes)


def coarse_in_kernel(z, small, coarse, pick, picked):
    n = z.loads
    primal = small[:, 0:z.coarse]
    high, low = split_hi_lo(primal)
    inv_high, inv_low = split_hi_lo(coarse[...])
    both = jnp.dot(jnp.concatenate([high, low], axis=0), inv_high, preferred_element_type=F32)
    lifted = (both[0:n] + both[n:]) + jnp.dot(high, inv_low, preferred_element_type=F32)
    energy = jnp.sum(primal * lifted, axis=1, keepdims=True)
    high, low = split_hi_lo(lifted)
    values = jnp.dot(jnp.concatenate([high, low], axis=0), pick[...], preferred_element_type=F32)
    column = lax.broadcasted_iota(jnp.int32, (n, WIDE), 1)
    for block in range(z.blocks):
        group, place = divmod(block * PAD, WIDE)
        upper = values[0:n, group * WIDE:(group + 1) * WIDE]
        lower = values[n:, group * WIDE:(group + 1) * WIDE]
        first = pltpu.roll(upper, (WIDE - place) % WIDE, 1)
        second = pltpu.roll(upper, (WIDE + PAD - place) % WIDE, 1)
        third = pltpu.roll(lower, (WIDE + 2 * PAD - place) % WIDE, 1)
        mixed = jnp.where(column < PAD, first, jnp.where(column < 2 * PAD, second, third))
        picked[block] = jnp.where(column < 3 * PAD, mixed, 0.0).astype(BF)
    return energy


def image_of_face(z, tab, face, image, held, picked, spread):
    sides = jnp.concatenate([picked[face // z.faces], picked[tab[z.slots + z.total + face]]], axis=1)
    lift = jnp.dot(sides, spread[face], preferred_element_type=F32)
    return (image[face] - held[tab[z.slots + face]]) + lift


def start_kernel(z, tab, image, small_a, small_b, coarse, pick, spread, blocks, *rest):
    arrived, rest = rest[:LANES], rest[LANES:]
    residual, weighted = rest[:2]
    lanes, (held, picked) = rest[2:2 + LANES], rest[2 + LANES:]
    take_lanes(z, arrived, held)
    coarse_in_kernel(z, small_a[...] + small_b[...], coarse, pick, picked)
    for face in range(z.total):
        value = image_of_face(z, tab, face, image, held, picked, spread)
        residual[face] = value
        weighted[face] = jnp.dot(value.astype(BF), blocks[face], preferred_element_type=F32)
    fill_lanes(z, tab, weighted, lanes)


def step_kernel(first, last, z, tab, image, small_a, small_b, coarse, pick, spread, blocks, vec, old_residual, *rest):
    if not first:
        old_solution, old_direction, old_image, old_scalars = rest[:4]
        rest = rest[4:]
    arrived, rest = rest[:LANES], rest[LANES:]
    solution_out, residual = rest[:2]
    rest = rest[2:]
    if not last:
        direction, new_image, scalars, weighted = rest[:4]
        lanes, rest = rest[4:4 + LANES], rest[4 + LANES:]
    held, picked = rest
    take_lanes(z, arrived, held)
    small = small_a[...] + small_b[...]
    energy = coarse_in_kernel(z, small, coarse, pick, picked)
    gamma = small[:, z.coarse:z.coarse + 1]
    kappa = small[:, z.coarse + 1:z.coarse + 2]
    eta = small[:, z.coarse + 2:z.coarse + 3]
    curvature = 2.0 * (kappa + energy)
    beta = None
    if not first:
        beta = gamma / old_scalars[:, 0:1]
        curvature = curvature + beta * (2.0 * eta + beta * old_scalars[:, 1:2])
    alpha = gamma / curvature
    if not last:
        column = lax.broadcasted_iota(jnp.int32, (z.loads, WIDE), 1)
        scalars[...] = jnp.where(column == 0, gamma, curvature)
    wide = (z.loads, z.dof)
    alpha_wide = jnp.broadcast_to(alpha, wide)
    beta_wide = None if first else jnp.broadcast_to(beta, wide)
    for face in range(z.total):
        ahead = image_of_face(z, tab, face, image, held, picked, spread)
        along = vec[face]
        if not first:
            ahead = ahead + beta_wide * old_image[face]
            along = along + beta_wide * old_direction[face]
        moved = alpha_wide * along
        solution_out[face] = moved if first else old_solution[face] + moved
        value = old_residual[face] - alpha_wide * ahead
        residual[face] = value
        if not last:
            direction[face] = along
            new_image[face] = ahead
            weighted[face] = jnp.dot(value.astype(BF), blocks[face], preferred_element_type=F32)
    if not last:
        fill_lanes(z, tab, weighted, lanes)


def exchange(lanes, devices):
    return [lax.ppermute(lane, "sub", pairs) for lane, pairs in zip(lanes, lane_pairs(devices))]


def summed_shares(small, devices):
    def other(value, pairs):
        return lax.ppermute(value, "sub", pairs)

    core = lax.axis_index("sub") % 2
    chip = small + other(small, flipped(1, devices))
    plane = chip + other(chip, flipped(2, devices))
    if devices == 4:
        return plane, jnp.zeros_like(plane)
    near = other(plane, [(i, i ^ (8 if i % 2 else 4)) for i in range(devices)])
    far = other(plane, flipped(12, devices))
    half = near + jnp.where(core == 0, plane, far)
    rest = other(half, flipped(1, devices))
    mask = 16
    while mask < devices:
        whole = half + rest
        half, rest = whole, other(whole, flipped(mask, devices))
        mask *= 2
    return half, rest


def on_device(load, stiff_inv, face_blocks, coupling, coarse_inv, corners, partner):
    devices = lax.axis_size("sub")
    z = Sizes(load, coupling, coarse_inv)
    coarse = lax.all_gather(coarse_inv, "sub", axis=0, tiled=True)
    tab = routing(partner, z.slots_per_lane)

    numbers = jnp.pad(corners.astype(F32), ((0, 0), (0, PAD - z.primal)), constant_values=-1.0)
    row = jnp.pad(numbers.reshape(1, -1), ((0, 0), (0, WIDE - z.subs * PAD)), constant_values=-1.0)
    corner_row = jnp.broadcast_to(row, (8, WIDE))
    twice = jnp.stack([numbers, numbers], axis=1).reshape(-1)
    spot = (twice[:, None] == jnp.arange(z.coarse, dtype=F32)[None, :]).astype(BF)

    field = shape(z.total, z.loads, z.dof)
    lane_field = [shape(z.slots_per_lane, z.loads, z.dof)] * LANES
    small_shape = shape(z.loads, z.small_width)
    held = pltpu.VMEM((z.slots, z.loads, z.dof), F32)
    picked = pltpu.VMEM((z.blocks, z.loads, WIDE), BF)
    apply_scratch = [
        pltpu.VMEM((z.subs, z.unknowns, z.unknowns), BF),
        pltpu.VMEM((z.subs, 2 * z.loads, z.unknowns), BF),
        pltpu.SemaphoreType.DMA((z.subs * 8,)),
    ]
    apply_cost = dict(flops=2 * z.total * z.dof * z.unknowns * z.loads, moved=stiff_inv.size * 2)

    packed = call(
        pack_kernel, z,
        [shape(z.carry_rows, z.dof)] * LANES + [shape(z.subs, 4 * PAD, z.unknowns, dtype=BF)],
        (tab, coupling, corner_row), [SMEM, VMEM, VMEM], [], 16, "pack_coupling",
    )
    weights = packed[LANES]
    carried = exchange(packed[:LANES], devices)

    load_faces = load.reshape(z.total, z.loads, z.dof)
    image, small, *lanes = call(
        load_kernel, z, [field, small_shape] + lane_field,
        (tab, load_faces, weights, spot, stiff_inv), [SMEM, VMEM, VMEM, VMEM, HBM],
        apply_scratch, 32, "apply_load", **apply_cost,
    )
    spread, pick = call(
        unpack_kernel, z,
        [shape(z.total, 8 * PAD, z.dof, dtype=BF), shape(z.coarse, z.pick_width, dtype=BF)],
        (tab, coupling, corner_row, *carried), [SMEM] + [VMEM] * (2 + LANES),
        [pltpu.VMEM((z.slots, z.primal, z.dof), F32), pltpu.VMEM((8, z.pick_width), F32)],
        16, "unpack_coupling",
    )
    blocks = face_blocks.reshape(z.total, z.dof, z.dof)

    arrived = exchange(lanes, devices)
    share_a, share_b = summed_shares(small, devices)
    fixed = (coarse, pick, spread, blocks)
    residual, weighted, *lanes = call(
        start_kernel, z, [field, field] + lane_field,
        (tab, image, share_a, share_b, *fixed, *arrived), [SMEM] + [VMEM] * (7 + LANES),
        [held, picked], 24, "first_residual",
    )
    state = None
    for iteration in range(ITERS):
        first, last = iteration == 0, iteration + 1 == ITERS
        arrived = exchange(lanes, devices)
        old_image = residual if first else state[2]
        vec, image, small, *lanes = call(
            precond_kernel, z, [field, field, small_shape] + lane_field,
            (tab, weighted, residual, old_image, weights, spot, stiff_inv, *arrived),
            [SMEM] + [VMEM] * 5 + [HBM] + [VMEM] * LANES,
            apply_scratch + [held], 32, "precond_apply", **apply_cost,
        )
        arrived = exchange(lanes, devices)
        share_a, share_b = summed_shares(small, devices)
        ins = [tab, image, share_a, share_b, *fixed, vec, residual] + ([] if first else list(state)) + list(arrived)
        outs = [field, field] + ([] if last else [field, field, shape(z.loads, WIDE), field] + lane_field)
        result = call(
            functools.partial(step_kernel, first, last), z, outs, ins, [SMEM] + [VMEM] * (len(ins) - 1),
            [held, picked], 24, "cg_step",
        )
        multipliers, residual = result[:2]
        if not last:
            direction, old, scalars, weighted = result[2:6]
            lanes = result[6:]
            state = (multipliers, direction, old, scalars)
    return multipliers.reshape(load.shape), residual.reshape(load.shape)


def solution(mesh):
    return jax.shard_map(
        on_device,
        mesh=mesh,
        in_specs=(
            P(("parts", "sub"), None, None, None),
            P(("parts", "sub"), None, None),
            P(("parts", "sub"), None, None, None),
            P(("parts", "sub"), None, None),
            P(("parts", "sub"), None),
            P(("parts", "sub"), None),
            P(("parts", "sub"), None),
        ),
        out_specs=(P(("parts", "sub"), None, None, None), P(("parts", "sub"), None, None, None)),
        check_vma=False,
    )
```

time: 664 us -> 219 us (0.33)
  blocking collectives: 385 us -> 0 us
  matrix products: 59 us -> 0 us
  starting transfers between devices: 110 us -> 67 us
  Pallas kernels: 0 us -> 41.2 us
  waiting for transfers between devices: 19.3 us -> 55.6 us
  other arithmetic: 18.8 us -> 1.25 us
  local copies, waits for them, and re-layouts: 54.4 us -> 38.3 us
    psum x9 -> x0, blocking collectives: 385 us -> none  [the longest x4 237 us: apply_op(): primal_sum = lax.psum(primal_local, 'sub')]
    dot_general x27 -> x0, matrix products: 59 us -> none  [the longest x4 41.9 us: apply_op(): jnp.einsum('sflb,sfbga->sgla', rounded, stiff_faces, preferred_element_ty...]
    ppermute x42 -> x68, starting transfers between devices: 110 us -> 67 us  [the longest x48 48.1 us: exchange(): lax.ppermute(lane, 'sub', pairs)]
    pallas_call x0 -> x10, Pallas kernels: none -> 41.2 us  [call(): pl.pallas_call(functools.partial(kernel, sizes), out_shape=outs, in_specs...]
    ppermute x42 -> x68, waiting for transfers between devices: 18.6 us -> 54.9 us  [the longest x48 35.4 us: exchange(): lax.ppermute(lane, 'sub', pairs)]
    gather x14 -> x0, local copies, waits for them, and re-layouts: 22.5 us -> none  [the longest x7 12.4 us: partner_values(): return incoming[arrival].reshape(field_vec.shape)]
    unnamed x76, local copies, waits for them, and re-layouts: 25.1 us -> 37.4 us
    select_n x11 -> x0, other arithmetic: 7.42 us -> none  [the longest x8 7.38 us: partner_values(): outgoing = jnp.where(filled[:, None, None], face_rows[source], 0.0)]
  transfers between devices with their start and end apart: 43 -> 69, of which waited for: 7 -> 26; matrix products, arithmetic and copies ran while one was open for 6% -> 1% of each run, Pallas kernels for 0% -> 5%
where the time goes in v1:
time: 219 us; the launch traced here: 218 us
  starting transfers between devices  67 us (31%)
  waiting for transfers between devices  55.6 us (25%)
  Pallas kernels  41.2 us (19%)
  local copies, waits for them, and re-layouts  38.3 us (17%)
  between operations  14.4 us (7%)
    ppermute x48, starting transfers between devices, exchange(): lax.ppermute(lane, 'sub', pairs)  48.1 us
    pallas_call x10, Pallas kernels, call(): pl.pallas_call(functools.partial(kernel, sizes), out_shape=outs, in_specs...  41.2 us
    unnamed x76, local copies, waits for them, and re-layouts  37.4 us
    ppermute x48, waiting for transfers between devices, exchange(): lax.ppermute(lane, 'sub', pairs)  35.4 us
    ppermute x20, waiting for transfers between devices, other(): return lax.ppermute(value, 'sub', pairs)  19.5 us
    ppermute x20, starting transfers between devices, other(): return lax.ppermute(value, 'sub', pairs)  18.8 us
  transfers between devices with their start and end apart: 69, of which 26 were waited for; matrix products, arithmetic and copies ran while one was open for 1% of the time, Pallas kernels for 5%

profile of v1, /device:TPU:0, one launch (start us, length us, event | category | flops | bytes accessed | tf_op | source)
XLA Modules:
  0.0 217.7 jit_solution(11100345698485392812)
XLA Ops:
  9.9 1.0 copy-done.9
  10.9 1.1 pack_coupling.1
  12.1 5.8 %copy-done = bf16[2,2048,2048]{2,1,0:T(8,128)(2,1)S(1)} copy-done((bf16[2,2048,2048]{2,1,0:T(8,128)(2,1)S(1)}, bf16[2,2048,2048]{2,1,0:T(8,128)(2,1)}, u32[]{:S(2)}) %copy-start) | copy-done | bytes 16777240
  17.9 0.9 copy-done.11
  18.8 8.1 %apply_load.1 = (f32[32,16,128]{2,1,0:T(8,128)S(1)}, f32[16,640]{1,0:T(8,128)S(1)}, f32[12,16,128]{2,1,0:T(8,128)S(1)}, f32[12,16,128]{2,1,0:T(8,128)S(1)}, f32[...) custom-call(s32[136]{0:T(256)S(1)} %pad_add_fusion.tab, ...), custom_call_target="tpu_custom_call" | custom-call | flops 268435456 | bytes 16777216 | tf_op jit(solution)/shard_map/apply_load/pallas_call | solution.py:89
  27.5 2.9 %collective-permute-start.12 = (f32[12,16,128]{2,1,0:T(8,128)S(1)}, f32[12,16,128]{2,1,0:T(8,128)S(1)}, u32[]{:S(2)}, u32[]{:S(2)}) collective-permute-start(f32[12,16,128]{2,1,0:T(8,128)S(1)} %get-tuple-element.92), channel_id=1, source_target_pairs={{0,2},{1,3},{2,0},{3,1},{4,6},{5,7},{6,4},{7,5},{8,10},{9,11},{10,... | collective-permute-start | bytes 294920 | tf_op jit(solution)/shard_map/ppermute | solution.py:328
  31.2 3.4 %collective-permute-done.1 = f32[16,640]{1,0:T(8,128)S(1)} collective-permute-done((f32[16,640]{1,0:T(8,128)S(1)}, f32[16,640]{1,0:T(8,128)S(1)}, u32[]{:S(2)}, u32[]{:S(2)}) %collective-permute-start.1) | collective-permute-done | bytes 40992 | tf_op jit(solution)/shard_map/ppermute | solution.py:333
  34.6 3.7 %collective-permute-start.3 = (f32[16,640]{1,0:T(8,128)S(1)}, f32[16,640]{1,0:T(8,128)S(1)}, u32[]{:S(2)}, u32[]{:S(2)}) collective-permute-start(f32[16,640]{1,0:T(8,128)S(1)} %add.182), channel_id=1, source_target_pairs={{0,12},{1,13},{2,14},{3,15},{4,8},{5,9},{6,10},{7,11},{8,4},{9,5},... | collective-permute-start | bytes 122888 | tf_op jit(solution)/shard_map/ppermute | solution.py:333
  38.9 1.5 collective-permute-start.6
  41.7 0.9 collective-permute-done.2
  42.7 2.8 %collective-permute-start.10 = (f32[296,128]{1,0:T(8,128)S(1)}, f32[296,128]{1,0:T(8,128)S(1)}, u32[]{:S(2)}, u32[]{:S(2)}) collective-permute-start(f32[296,128]{1,0:T(8,128)S(1)} %get-tuple-element.88), channel_id=1, source_target_pairs={{0,2},{1,4},{2,0},{3,6},{4,1},{5,8},{6,3},{7,10},{8,5},{9,12},{10,... | collective-permute-start | bytes 454664 | tf_op jit(solution)/shard_map/ppermute | solution.py:328
  46.3 1.6 collective-permute-start.13
  47.9 6.5 %collective-permute-done.7.rest_2_ = f32[296,128]{1,0:T(8,128)S(1)} collective-permute-done((f32[296,128]{1,0:T(8,128)S(1)}, f32[296,128]{1,0:T(8,128)S(1)}, u32[]{:S(2)}, u32[]{:S(2)}) %collective-permute-start.7) | collective-permute-done | bytes 151584 | tf_op jit(solution)/shard_map/ppermute | solution.py:328
  56.9 4.3 %collective-permute-start.16 = (f32[12,16,128]{2,1,0:T(8,128)}, f32[12,16,128]{2,1,0:T(8,128)S(1)}, u32[]{:S(2)}, u32[]{:S(2)}) collective-permute-start(f32[12,16,128]{2,1,0:T(8,128)} %get-tuple-element.96), channel_id=1, source_target_pairs={{0,2},{1,4},{2,0},{3,6},{4,1},{5,8},{6,3},{7,10},{8,5},{9,12},{10,... | collective-permute-start | bytes 294920 | tf_op jit(solution)/shard_map/ppermute | solution.py:328
  62.0 1.0 copy-done.10
  67.5 1.0 unpack_coupling.1
  72.5 1.2 copy-done.2
  73.8 1.2 copy-done.4
  75.0 1.0 copy-done.7
  83.0 1.9 first_residual.1
  85.0 1.6 collective-permute-start.18
  87.3 3.6 %collective-permute-start.22 = (f32[12,16,128]{2,1,0:T(8,128)S(1)}, f32[12,16,128]{2,1,0:T(8,128)S(1)}, u32[]{:S(2)}, u32[]{:S(2)}) collective-permute-start(f32[12,16,128]{2,1,0:T(8,128)S(1)} %get-tuple-element.104), channel_id=1, source_target_pairs={{0,2},{1,4},{2,0},{3,6},{4,1},{5,8},{6,3},{7,10},{8,5},{9,12},{10,... | collective-permute-start | bytes 294920 | tf_op jit(solution)/shard_map/ppermute | solution.py:328
  90.9 4.6 %collective-permute-done.19.rest_2_ = f32[12,16,128]{2,1,0:T(8,128)S(1)} collective-permute-done((f32[12,16,128]{2,1,0:T(8,128)S(1)}, f32[12,16,128]{2,1,0:T(8,128)S(1)}, u32[]{:S(2)}, u32[]{:S(2)}) %collective-permute-start.19) | collective-permute-done | bytes 98336 | tf_op jit(solution)/shard_map/ppermute | solution.py:328
  95.5 1.0 collective-permute-done.22.rest_5_
  96.6 5.8 %copy-done.1 = bf16[2,2048,2048]{2,1,0:T(8,128)(2,1)S(1)} copy-done((bf16[2,2048,2048]{2,1,0:T(8,128)(2,1)S(1)}, bf16[2,2048,2048]{2,1,0:T(8,128)(2,1)}, u32[]{:S(2)}) %copy-start.1) | copy-done | bytes 16777240
  102.4 7.6 %precond_apply.3 = (f32[32,16,128]{2,1,0:T(8,128)S(1)}, f32[32,16,128]{2,1,0:T(8,128)S(1)}, f32[16,640]{1,0:T(8,128)S(1)}, f32[12,16,128]{2,1,0:T(8,128)S(1)}, f...) custom-call(s32[136]{0:T(256)S(1)} %pad_add_fusion.tab, ...), custom_call_target="tpu_custom_call" | custom-call | flops 268435456 | bytes 16777216 | tf_op jit(solution)/shard_map/precond_apply/pallas_call | solution.py:89
  111.3 2.5 %collective-permute-start.24 = (f32[16,640]{1,0:T(8,128)S(1)}, f32[16,640]{1,0:T(8,128)S(1)}, u32[]{:S(2)}, u32[]{:S(2)}) collective-permute-start(f32[16,640]{1,0:T(8,128)S(1)} %add.185), channel_id=1, source_target_pairs={{0,2},{1,3},{2,0},{3,1},{4,6},{5,7},{6,4},{7,5},{8,10},{9,11},{10,... | collective-permute-start | bytes 122888 | tf_op jit(solution)/shard_map/ppermute | solution.py:333
  113.7 2.0 collective-permute-done.24
  115.7 1.1 collective-permute-start.26
  116.9 1.0 collective-permute-start.29
  117.9 1.1 collective-permute-start.31
  119.0 2.5 %collective-permute-done.26 = f32[16,640]{1,0:T(8,128)S(1)} collective-permute-done((f32[16,640]{1,0:T(8,128)S(1)}, f32[16,640]{1,0:T(8,128)S(1)}, u32[]{:S(2)}, u32[]{:S(2)}) %collective-permute-start.26) | collective-permute-done | bytes 40992 | tf_op jit(solution)/shard_map/ppermute | solution.py:333
  121.5 2.0 collective-permute-start.33
  123.7 1.8 collective-permute-done.30.rest_2_
  125.5 2.0 collective-permute-done.33.rest_5_
  127.5 2.0 cg_step.3
  129.9 2.2 %collective-permute-start.35 = (f32[12,16,128]{2,1,0:T(8,128)S(1)}, f32[12,16,128]{2,1,0:T(8,128)S(1)}, u32[]{:S(2)}, u32[]{:S(2)}) collective-permute-start(f32[12,16,128]{2,1,0:T(8,128)S(1)} %get-tuple-element.118), channel_id=1, source_target_pairs={{0,2},{1,3},{2,0},{3,1},{4,6},{5,7},{6,4},{7,5},{8,10},{9,11},{10,... | collective-permute-start | bytes 294920 | tf_op jit(solution)/shard_map/ppermute | solution.py:328
  132.7 3.8 %collective-permute-start.39 = (f32[12,16,128]{2,1,0:T(8,128)S(1)}, f32[12,16,128]{2,1,0:T(8,128)S(1)}, u32[]{:S(2)}, u32[]{:S(2)}) collective-permute-start(f32[12,16,128]{2,1,0:T(8,128)S(1)} %get-tuple-element.122), channel_id=1, source_target_pairs={{0,2},{1,4},{2,0},{3,6},{4,1},{5,8},{6,3},{7,10},{8,5},{9,12},{10,... | collective-permute-start | bytes 294920 | tf_op jit(solution)/shard_map/ppermute | solution.py:328
  136.5 4.6 %collective-permute-done.36.rest_2_ = f32[12,16,128]{2,1,0:T(8,128)S(1)} collective-permute-done((f32[12,16,128]{2,1,0:T(8,128)S(1)}, f32[12,16,128]{2,1,0:T(8,128)S(1)}, u32[]{:S(2)}, u32[]{:S(2)}) %collective-permute-start.36) | collective-permute-done | bytes 98336 | tf_op jit(solution)/shard_map/ppermute | solution.py:328
  141.1 1.0 collective-permute-done.39.rest_5_
  142.1 7.4 %precond_apply.4 = (f32[32,16,128]{2,1,0:T(8,128)S(1)}, f32[32,16,128]{2,1,0:T(8,128)S(1)}, f32[16,640]{1,0:T(8,128)S(1)}, f32[12,16,128]{2,1,0:T(8,128)S(1)}, f...) custom-call(s32[136]{0:T(256)S(1)} %pad_add_fusion.tab, ...), custom_call_target="tpu_custom_call" | custom-call | flops 268435456 | bytes 16777216 | tf_op jit(solution)/shard_map/precond_apply/pallas_call | solution.py:89
  150.8 2.5 %collective-permute-start.41 = (f32[16,640]{1,0:T(8,128)S(1)}, f32[16,640]{1,0:T(8,128)S(1)}, u32[]{:S(2)}, u32[]{:S(2)}) collective-permute-start(f32[16,640]{1,0:T(8,128)S(1)} %add.188), channel_id=1, source_target_pairs={{0,2},{1,3},{2,0},{3,1},{4,6},{5,7},{6,4},{7,5},{8,10},{9,11},{10,... | collective-permute-start | bytes 122888 | tf_op jit(solution)/shard_map/ppermute | solution.py:333
  153.3 2.0 collective-permute-done.41
  155.3 2.5 %collective-permute-start.43 = (f32[16,640]{1,0:T(8,128)S(1)}, f32[16,640]{1,0:T(8,128)S(1)}, u32[]{:S(2)}, u32[]{:S(2)}) collective-permute-start(f32[16,640]{1,0:T(8,128)S(1)} %add.189), channel_id=1, source_target_pairs={{0,12},{1,13},{2,14},{3,15},{4,8},{5,9},{6,10},{7,11},{8,4},{9,5},... | collective-permute-start | bytes 122888 | tf_op jit(solution)/shard_map/ppermute | solution.py:333
  157.8 1.3 collective-permute-start.46
  160.0 1.1 collective-permute-done.43
  161.8 1.7 collective-permute-start.50
  163.6 0.9 collective-permute-start.44
  164.5 3.1 %collective-permute-done.47.rest_6_ = f32[12,16,128]{2,1,0:T(8,128)S(1)} collective-permute-done((f32[12,16,128]{2,1,0:T(8,128)S(1)}, f32[12,16,128]{2,1,0:T(8,128)S(1)}, u32[]{:S(2)}, u32[]{:S(2)}) %collective-permute-start.47) | collective-permute-done | bytes 98336 | tf_op jit(solution)/shard_map/ppermute | solution.py:328
  167.6 1.0 collective-permute-done.50.rest_9_
  168.6 2.1 cg_step.4
  170.8 2.5 %collective-permute-start.52 = (f32[12,16,128]{2,1,0:T(8,128)S(1)}, f32[12,16,128]{2,1,0:T(8,128)S(1)}, u32[]{:S(2)}, u32[]{:S(2)}) collective-permute-start(f32[12,16,128]{2,1,0:T(8,128)S(1)} %get-tuple-element.139), channel_id=1, source_target_pairs={{0,2},{1,3},{2,0},{3,1},{4,6},{5,7},{6,4},{7,5},{8,10},{9,11},{10,... | collective-permute-start | bytes 294920 | tf_op jit(solution)/shard_map/ppermute | solution.py:328
  173.9 3.8 %collective-permute-start.56 = (f32[12,16,128]{2,1,0:T(8,128)S(1)}, f32[12,16,128]{2,1,0:T(8,128)S(1)}, u32[]{:S(2)}, u32[]{:S(2)}) collective-permute-start(f32[12,16,128]{2,1,0:T(8,128)S(1)} %get-tuple-element.143), channel_id=1, source_target_pairs={{0,2},{1,4},{2,0},{3,6},{4,1},{5,8},{6,3},{7,10},{8,5},{9,12},{10,... | collective-permute-start | bytes 294920 | tf_op jit(solution)/shard_map/ppermute | solution.py:328
  177.7 4.6 %collective-permute-done.53.rest_2_ = f32[12,16,128]{2,1,0:T(8,128)S(1)} collective-permute-done((f32[12,16,128]{2,1,0:T(8,128)S(1)}, f32[12,16,128]{2,1,0:T(8,128)S(1)}, u32[]{:S(2)}, u32[]{:S(2)}) %collective-permute-start.53) | collective-permute-done | bytes 98336 | tf_op jit(solution)/shard_map/ppermute | solution.py:328
  182.3 1.0 collective-permute-done.56.rest_5_
  183.4 7.6 %precond_apply.5 = (f32[32,16,128]{2,1,0:T(8,128)S(1)}, f32[32,16,128]{2,1,0:T(8,128)S(1)}, f32[16,640]{1,0:T(8,128)S(1)}, f32[12,16,128]{2,1,0:T(8,128)S(1)}, f...) custom-call(s32[136]{0:T(256)S(1)} %pad_add_fusion.tab, ...), custom_call_target="tpu_custom_call" | custom-call | flops 268435456 | bytes 16777216 | tf_op jit(solution)/shard_map/precond_apply/pallas_call | solution.py:89
  192.3 2.5 %collective-permute-start.58 = (f32[16,640]{1,0:T(8,128)S(1)}, f32[16,640]{1,0:T(8,128)S(1)}, u32[]{:S(2)}, u32[]{:S(2)}) collective-permute-start(f32[16,640]{1,0:T(8,128)S(1)} %add.191), channel_id=1, source_target_pairs={{0,2},{1,3},{2,0},{3,1},{4,6},{5,7},{6,4},{7,5},{8,10},{9,11},{10,... | collective-permute-start | bytes 122888 | tf_op jit(solution)/shard_map/ppermute | solution.py:333
  194.8 2.0 collective-permute-done.58
  197.7 1.3 collective-permute-start.63
  199.8 2.8 %collective-permute-done.60 = f32[16,640]{1,0:T(8,128)S(1)} collective-permute-done((f32[16,640]{1,0:T(8,128)S(1)}, f32[16,640]{1,0:T(8,128)S(1)}, u32[]{:S(2)}, u32[]{:S(2)}) %collective-permute-start.60) | collective-permute-done | bytes 40992 | tf_op jit(solution)/shard_map/ppermute | solution.py:333
  202.6 2.0 collective-permute-start.67
  204.7 1.8 collective-permute-done.64.rest_6_
  206.5 2.0 collective-permute-done.67.rest_9_
  208.5 2.4 %cg_step.5 = (f32[32,16,128]{2,1,0:T(8,128)}, f32[32,16,128]{2,1,0:T(8,128)}) custom-call(s32[136]{0:T(256)S(1)} %pad_add_fusion.tab, f32[32,16,128]{2,1,0:T(8,128)S(1)} %get-tuple-element.144.image, f32[16,640]{1,0:T(8,128)S(1)} %select_add_fusion.small_a, f32[16,640]{1,0:T(8,128)S(1)} %collective-permute-done.61.small_b, f32[512,512]{1,0:T(8,128)S(1)} %copy-done.5, ...), custom_call_target="tpu_custom_call" | custom-call | tf_op jit(solution)/shard_map/cg_step/pallas_call | solution.py:89
  (188 shorter events, 35.5 us)
Async XLA Ops:
  7.2 65.4 %all-gather.2.cloned.1.call-start = ((), (), s32[]{:S(2)}) async-start(), calls=%async_computation | async-start | bytes 1114112 | tf_op jit(solution)/shard_map/all_gather | solution.py:355
  26.9 3.5 %collective-permute-start = (f32[16,640]{1,0:T(8,128)S(1)}, f32[16,640]{1,0:T(8,128)S(1)}, u32[]{:S(2)}, u32[]{:S(2)}) collective-permute-start(f32[16,640]{1,0:T(8,128)S(1)} %get-tuple-element.82), channel_id=1, source_target_pairs={{0,1},{1,0},{2,3},{3,2},{4,5},{5,4},{6,7},{7,6},{8,9},{9,8},{10,11... | collective-permute-start | bytes 122888 | tf_op jit(solution)/shard_map/ppermute | solution.py:333
  27.4 10.8 %collective-permute-start.11 = (f32[12,16,128]{2,1,0:T(8,128)S(1)}, f32[12,16,128]{2,1,0:T(8,128)S(1)}, u32[]{:S(2)}, u32[]{:S(2)}) collective-permute-start(f32[12,16,128]{2,1,0:T(8,128)S(1)} %get-tuple-element.91), channel_id=1, source_target_pairs={{0,1},{1,0},{2,3},{3,2},{4,5},{5,4},{6,7},{7,6},{8,9},{9,8},{10,11... | collective-permute-start | bytes 294920 | tf_op jit(solution)/shard_map/ppermute | solution.py:328
  27.5 12.9 %collective-permute-start.12 = (f32[12,16,128]{2,1,0:T(8,128)S(1)}, f32[12,16,128]{2,1,0:T(8,128)S(1)}, u32[]{:S(2)}, u32[]{:S(2)}) collective-permute-start(f32[12,16,128]{2,1,0:T(8,128)S(1)} %get-tuple-element.92), channel_id=1, source_target_pairs={{0,2},{1,3},{2,0},{3,1},{4,6},{5,7},{6,4},{7,5},{8,10},{9,11},{10,... | collective-permute-start | bytes 294920 | tf_op jit(solution)/shard_map/ppermute | solution.py:328
  30.5 4.1 %collective-permute-start.1 = (f32[16,640]{1,0:T(8,128)S(1)}, f32[16,640]{1,0:T(8,128)S(1)}, u32[]{:S(2)}, u32[]{:S(2)}) collective-permute-start(f32[16,640]{1,0:T(8,128)S(1)} %add.181), channel_id=1, source_target_pairs={{0,2},{1,3},{2,0},{3,1},{4,6},{5,7},{6,4},{7,5},{8,10},{9,11},{10,... | collective-permute-start | bytes 122888 | tf_op jit(solution)/shard_map/ppermute | solution.py:333
  34.6 6.8 %collective-permute-start.3 = (f32[16,640]{1,0:T(8,128)S(1)}, f32[16,640]{1,0:T(8,128)S(1)}, u32[]{:S(2)}, u32[]{:S(2)}) collective-permute-start(f32[16,640]{1,0:T(8,128)S(1)} %add.182), channel_id=1, source_target_pairs={{0,12},{1,13},{2,14},{3,15},{4,8},{5,9},{6,10},{7,11},{8,4},{9,5},... | collective-permute-start | bytes 122888 | tf_op jit(solution)/shard_map/ppermute | solution.py:333
  38.2 4.4 %collective-permute-start.2 = (f32[16,640]{1,0:T(8,128)S(1)}, f32[16,640]{1,0:T(8,128)S(1)}, u32[]{:S(2)}, u32[]{:S(2)}) collective-permute-start(f32[16,640]{1,0:T(8,128)S(1)} %add.182), channel_id=1, source_target_pairs={{0,4},{1,9},{2,6},{3,11},{4,0},{5,13},{6,2},{7,15},{8,12},{9,1},{1... | collective-permute-start | bytes 122888 | tf_op jit(solution)/shard_map/ppermute | solution.py:333
  38.2 4.5 %collective-permute-start.5 = (f32[296,128]{1,0:T(8,128)S(1)}, f32[296,128]{1,0:T(8,128)S(1)}, u32[]{:S(2)}, u32[]{:S(2)}) collective-permute-start(f32[296,128]{1,0:T(8,128)S(1)} %get-tuple-element.83), channel_id=1, source_target_pairs={{0,1},{1,0},{2,3},{3,2},{4,5},{5,4},{6,7},{7,6},{8,9},{9,8},{10,11... | collective-permute-start | bytes 454664 | tf_op jit(solution)/shard_map/ppermute | solution.py:328
  38.9 6.7 %collective-permute-start.6 = (f32[296,128]{1,0:T(8,128)S(1)}, f32[296,128]{1,0:T(8,128)S(1)}, u32[]{:S(2)}, u32[]{:S(2)}) collective-permute-start(f32[296,128]{1,0:T(8,128)S(1)} %get-tuple-element.84), channel_id=1, source_target_pairs={{0,2},{1,3},{2,0},{3,1},{4,6},{5,7},{6,4},{7,5},{8,10},{9,11},{10,... | collective-permute-start | bytes 454664 | tf_op jit(solution)/shard_map/ppermute | solution.py:328
  41.1 13.3 %collective-permute-start.7 = (f32[296,128]{1,0:T(8,128)S(1)}, f32[296,128]{1,0:T(8,128)S(1)}, u32[]{:S(2)}, u32[]{:S(2)}) collective-permute-start(f32[296,128]{1,0:T(8,128)S(1)} %get-tuple-element.85), channel_id=1, source_target_pairs={{0,3},{1,2},{2,1},{3,0},{4,7},{5,6},{6,5},{7,4},{8,11},{9,10},{10,... | collective-permute-start | bytes 454664 | tf_op jit(solution)/shard_map/ppermute | solution.py:328
  41.4 13.7 %collective-permute-start.8 = (f32[296,128]{1,0:T(8,128)S(1)}, f32[296,128]{1,0:T(8,128)S(1)}, u32[]{:S(2)}, u32[]{:S(2)}) collective-permute-start(f32[296,128]{1,0:T(8,128)S(1)} %get-tuple-element.86), channel_id=1, source_target_pairs={{0,1},{1,0},{2,4},{3,5},{4,2},{5,3},{6,8},{7,9},{8,6},{9,7},{10,12... | collective-permute-start | bytes 454664 | tf_op jit(solution)/shard_map/ppermute | solution.py:328
  42.6 13.6 %collective-permute-start.9 = (f32[296,128]{1,0:T(8,128)S(1)}, f32[296,128]{1,0:T(8,128)S(1)}, u32[]{:S(2)}, u32[]{:S(2)}) collective-permute-start(f32[296,128]{1,0:T(8,128)S(1)} %get-tuple-element.87), channel_id=1, source_target_pairs={{0,1},{1,0},{2,5},{3,4},{4,3},{5,2},{6,9},{7,8},{8,7},{9,6},{10,13... | collective-permute-start | bytes 454664 | tf_op jit(solution)/shard_map/ppermute | solution.py:328
  42.7 18.6 %collective-permute-start.10 = (f32[296,128]{1,0:T(8,128)S(1)}, f32[296,128]{1,0:T(8,128)S(1)}, u32[]{:S(2)}, u32[]{:S(2)}) collective-permute-start(f32[296,128]{1,0:T(8,128)S(1)} %get-tuple-element.88), channel_id=1, source_target_pairs={{0,2},{1,4},{2,0},{3,6},{4,1},{5,8},{6,3},{7,10},{8,5},{9,12},{10,... | collective-permute-start | bytes 454664 | tf_op jit(solution)/shard_map/ppermute | solution.py:328
  46.3 23.1 %collective-permute-start.13 = (f32[12,16,128]{2,1,0:T(8,128)}, f32[12,16,128]{2,1,0:T(8,128)S(1)}, u32[]{:S(2)}, u32[]{:S(2)}) collective-permute-start(f32[12,16,128]{2,1,0:T(8,128)} %get-tuple-element.93), channel_id=1, source_target_pairs={{0,3},{1,2},{2,1},{3,0},{4,7},{5,6},{6,5},{7,4},{8,11},{9,10},{10,... | collective-permute-start | bytes 294920 | tf_op jit(solution)/shard_map/ppermute | solution.py:328
  55.1 14.9 %collective-permute-start.14 = (f32[12,16,128]{2,1,0:T(8,128)}, f32[12,16,128]{2,1,0:T(8,128)S(1)}, u32[]{:S(2)}, u32[]{:S(2)}) collective-permute-start(f32[12,16,128]{2,1,0:T(8,128)} %get-tuple-element.94), channel_id=1, source_target_pairs={{0,1},{1,0},{2,4},{3,5},{4,2},{5,3},{6,8},{7,9},{8,6},{9,7},{10,12... | collective-permute-start | bytes 294920 | tf_op jit(solution)/shard_map/ppermute | solution.py:328
  55.7 14.9 %collective-permute-start.15 = (f32[12,16,128]{2,1,0:T(8,128)}, f32[12,16,128]{2,1,0:T(8,128)S(1)}, u32[]{:S(2)}, u32[]{:S(2)}) collective-permute-start(f32[12,16,128]{2,1,0:T(8,128)} %get-tuple-element.95), channel_id=1, source_target_pairs={{0,1},{1,0},{2,5},{3,4},{4,3},{5,2},{6,9},{7,8},{8,7},{9,6},{10,13... | collective-permute-start | bytes 294920 | tf_op jit(solution)/shard_map/ppermute | solution.py:328
  56.9 14.4 %collective-permute-start.16 = (f32[12,16,128]{2,1,0:T(8,128)}, f32[12,16,128]{2,1,0:T(8,128)S(1)}, u32[]{:S(2)}, u32[]{:S(2)}) collective-permute-start(f32[12,16,128]{2,1,0:T(8,128)} %get-tuple-element.96), channel_id=1, source_target_pairs={{0,2},{1,4},{2,0},{3,6},{4,1},{5,8},{6,3},{7,10},{8,5},{9,12},{10,... | collective-permute-start | bytes 294920 | tf_op jit(solution)/shard_map/ppermute | solution.py:328
  61.3 10.6 %collective-permute-start.4 = (f32[16,640]{1,0:T(8,128)S(1)}, f32[16,640]{1,0:T(8,128)S(1)}, u32[]{:S(2)}, u32[]{:S(2)}) collective-permute-start(f32[16,640]{1,0:T(8,128)S(1)} %select_add_fusion.3.small_a), channel_id=1, source_target_pairs={{0,1},{1,0},{2,3},{3,2},{4,5},{5,4},{6,7},{7,6},{8,9},{9,8},{10,11... | collective-permute-start | bytes 122888 | tf_op jit(solution)/shard_map/ppermute | solution.py:333
  85.0 6.0 %collective-permute-start.18 = (f32[12,16,128]{2,1,0:T(8,128)S(1)}, f32[12,16,128]{2,1,0:T(8,128)S(1)}, u32[]{:S(2)}, u32[]{:S(2)}) collective-permute-start(f32[12,16,128]{2,1,0:T(8,128)S(1)} %get-tuple-element.100), channel_id=1, source_target_pairs={{0,2},{1,3},{2,0},{3,1},{4,6},{5,7},{6,4},{7,5},{8,10},{9,11},{10,... | collective-permute-start | bytes 294920 | tf_op jit(solution)/shard_map/ppermute | solution.py:328
  86.5 9.0 %collective-permute-start.19 = (f32[12,16,128]{2,1,0:T(8,128)S(1)}, f32[12,16,128]{2,1,0:T(8,128)S(1)}, u32[]{:S(2)}, u32[]{:S(2)}) collective-permute-start(f32[12,16,128]{2,1,0:T(8,128)S(1)} %get-tuple-element.101), channel_id=1, source_target_pairs={{0,3},{1,2},{2,1},{3,0},{4,7},{5,6},{6,5},{7,4},{8,11},{9,10},{10,... | collective-permute-start | bytes 294920 | tf_op jit(solution)/shard_map/ppermute | solution.py:328
  86.8 8.7 %collective-permute-start.20 = (f32[12,16,128]{2,1,0:T(8,128)S(1)}, f32[12,16,128]{2,1,0:T(8,128)S(1)}, u32[]{:S(2)}, u32[]{:S(2)}) collective-permute-start(f32[12,16,128]{2,1,0:T(8,128)S(1)} %get-tuple-element.102), channel_id=1, source_target_pairs={{0,1},{1,0},{2,4},{3,5},{4,2},{5,3},{6,8},{7,9},{8,6},{9,7},{10,12... | collective-permute-start | bytes 294920 | tf_op jit(solution)/shard_map/ppermute | solution.py:328
  87.2 8.4 %collective-permute-start.21 = (f32[12,16,128]{2,1,0:T(8,128)S(1)}, f32[12,16,128]{2,1,0:T(8,128)S(1)}, u32[]{:S(2)}, u32[]{:S(2)}) collective-permute-start(f32[12,16,128]{2,1,0:T(8,128)S(1)} %get-tuple-element.103), channel_id=1, source_target_pairs={{0,1},{1,0},{2,5},{3,4},{4,3},{5,2},{6,9},{7,8},{8,7},{9,6},{10,13... | collective-permute-start | bytes 294920 | tf_op jit(solution)/shard_map/ppermute | solution.py:328
  87.3 9.2 %collective-permute-start.22 = (f32[12,16,128]{2,1,0:T(8,128)S(1)}, f32[12,16,128]{2,1,0:T(8,128)S(1)}, u32[]{:S(2)}, u32[]{:S(2)}) collective-permute-start(f32[12,16,128]{2,1,0:T(8,128)S(1)} %get-tuple-element.104), channel_id=1, source_target_pairs={{0,2},{1,4},{2,0},{3,6},{4,1},{5,8},{6,3},{7,10},{8,5},{9,12},{10,... | collective-permute-start | bytes 294920 | tf_op jit(solution)/shard_map/ppermute | solution.py:328
  110.0 7.9 %collective-permute-start.28 = (f32[12,16,128]{2,1,0:T(8,128)S(1)}, f32[12,16,128]{2,1,0:T(8,128)S(1)}, u32[]{:S(2)}, u32[]{:S(2)}) collective-permute-start(f32[12,16,128]{2,1,0:T(8,128)S(1)} %get-tuple-element.108), channel_id=1, source_target_pairs={{0,1},{1,0},{2,3},{3,2},{4,5},{5,4},{6,7},{7,6},{8,9},{9,8},{10,11... | collective-permute-start | bytes 294920 | tf_op jit(solution)/shard_map/ppermute | solution.py:328
  111.3 4.5 %collective-permute-start.24 = (f32[16,640]{1,0:T(8,128)S(1)}, f32[16,640]{1,0:T(8,128)S(1)}, u32[]{:S(2)}, u32[]{:S(2)}) collective-permute-start(f32[16,640]{1,0:T(8,128)S(1)} %add.185), channel_id=1, source_target_pairs={{0,2},{1,3},{2,0},{3,1},{4,6},{5,7},{6,4},{7,5},{8,10},{9,11},{10,... | collective-permute-start | bytes 122888 | tf_op jit(solution)/shard_map/ppermute | solution.py:333
  115.7 5.8 %collective-permute-start.26 = (f32[16,640]{1,0:T(8,128)S(1)}, f32[16,640]{1,0:T(8,128)S(1)}, u32[]{:S(2)}, u32[]{:S(2)}) collective-permute-start(f32[16,640]{1,0:T(8,128)S(1)} %add.186), channel_id=1, source_target_pairs={{0,12},{1,13},{2,14},{3,15},{4,8},{5,9},{6,10},{7,11},{8,4},{9,5},... | collective-permute-start | bytes 122888 | tf_op jit(solution)/shard_map/ppermute | solution.py:333
  116.9 4.7 %collective-permute-start.25 = (f32[16,640]{1,0:T(8,128)S(1)}, f32[16,640]{1,0:T(8,128)S(1)}, u32[]{:S(2)}, u32[]{:S(2)}) collective-permute-start(f32[16,640]{1,0:T(8,128)S(1)} %add.186), channel_id=1, source_target_pairs={{0,4},{1,9},{2,6},{3,11},{4,0},{5,13},{6,2},{7,15},{8,12},{9,1},{1... | collective-permute-start | bytes 122888 | tf_op jit(solution)/shard_map/ppermute | solution.py:333
  116.9 6.7 %collective-permute-start.29 = (f32[12,16,128]{2,1,0:T(8,128)S(1)}, f32[12,16,128]{2,1,0:T(8,128)S(1)}, u32[]{:S(2)}, u32[]{:S(2)}) collective-permute-start(f32[12,16,128]{2,1,0:T(8,128)S(1)} %get-tuple-element.109), channel_id=1, source_target_pairs={{0,2},{1,3},{2,0},{3,1},{4,6},{5,7},{6,4},{7,5},{8,10},{9,11},{10,... | collective-permute-start | bytes 294920 | tf_op jit(solution)/shard_map/ppermute | solution.py:328
  117.9 7.6 %collective-permute-start.30 = (f32[12,16,128]{2,1,0:T(8,128)S(1)}, f32[12,16,128]{2,1,0:T(8,128)S(1)}, u32[]{:S(2)}, u32[]{:S(2)}) collective-permute-start(f32[12,16,128]{2,1,0:T(8,128)S(1)} %get-tuple-element.110), channel_id=1, source_target_pairs={{0,3},{1,2},{2,1},{3,0},{4,7},{5,6},{6,5},{7,4},{8,11},{9,10},{10,... | collective-permute-start | bytes 294920 | tf_op jit(solution)/shard_map/ppermute | solution.py:328
  117.9 7.6 %collective-permute-start.31 = (f32[12,16,128]{2,1,0:T(8,128)S(1)}, f32[12,16,128]{2,1,0:T(8,128)S(1)}, u32[]{:S(2)}, u32[]{:S(2)}) collective-permute-start(f32[12,16,128]{2,1,0:T(8,128)S(1)} %get-tuple-element.111), channel_id=1, source_target_pairs={{0,1},{1,0},{2,4},{3,5},{4,2},{5,3},{6,8},{7,9},{8,6},{9,7},{10,12... | collective-permute-start | bytes 294920 | tf_op jit(solution)/shard_map/ppermute | solution.py:328
  121.5 4.0 %collective-permute-start.32 = (f32[12,16,128]{2,1,0:T(8,128)S(1)}, f32[12,16,128]{2,1,0:T(8,128)S(1)}, u32[]{:S(2)}, u32[]{:S(2)}) collective-permute-start(f32[12,16,128]{2,1,0:T(8,128)S(1)} %get-tuple-element.112), channel_id=1, source_target_pairs={{0,1},{1,0},{2,5},{3,4},{4,3},{5,2},{6,9},{7,8},{8,7},{9,6},{10,13... | collective-permute-start | bytes 294920 | tf_op jit(solution)/shard_map/ppermute | solution.py:328
  121.5 5.9 %collective-permute-start.33 = (f32[12,16,128]{2,1,0:T(8,128)S(1)}, f32[12,16,128]{2,1,0:T(8,128)S(1)}, u32[]{:S(2)}, u32[]{:S(2)}) collective-permute-start(f32[12,16,128]{2,1,0:T(8,128)S(1)} %get-tuple-element.113), channel_id=1, source_target_pairs={{0,2},{1,4},{2,0},{3,6},{4,1},{5,8},{6,3},{7,10},{8,5},{9,12},{10,... | collective-permute-start | bytes 294920 | tf_op jit(solution)/shard_map/ppermute | solution.py:328
  123.6 3.9 %collective-permute-start.27 = (f32[16,640]{1,0:T(8,128)S(1)}, f32[16,640]{1,0:T(8,128)S(1)}, u32[]{:S(2)}, u32[]{:S(2)}) collective-permute-start(f32[16,640]{1,0:T(8,128)S(1)} %select_add_fusion.2.small_a), channel_id=1, source_target_pairs={{0,1},{1,0},{2,3},{3,2},{4,5},{5,4},{6,7},{7,6},{8,9},{9,8},{10,11... | collective-permute-start | bytes 122888 | tf_op jit(solution)/shard_map/ppermute | solution.py:333
  129.9 6.6 %collective-permute-start.35 = (f32[12,16,128]{2,1,0:T(8,128)S(1)}, f32[12,16,128]{2,1,0:T(8,128)S(1)}, u32[]{:S(2)}, u32[]{:S(2)}) collective-permute-start(f32[12,16,128]{2,1,0:T(8,128)S(1)} %get-tuple-element.118), channel_id=1, source_target_pairs={{0,2},{1,3},{2,0},{3,1},{4,6},{5,7},{6,4},{7,5},{8,10},{9,11},{10,... | collective-permute-start | bytes 294920 | tf_op jit(solution)/shard_map/ppermute | solution.py:328
  132.1 9.0 %collective-permute-start.36 = (f32[12,16,128]{2,1,0:T(8,128)S(1)}, f32[12,16,128]{2,1,0:T(8,128)S(1)}, u32[]{:S(2)}, u32[]{:S(2)}) collective-permute-start(f32[12,16,128]{2,1,0:T(8,128)S(1)} %get-tuple-element.119), channel_id=1, source_target_pairs={{0,3},{1,2},{2,1},{3,0},{4,7},{5,6},{6,5},{7,4},{8,11},{9,10},{10,... | collective-permute-start | bytes 294920 | tf_op jit(solution)/shard_map/ppermute | solution.py:328
  132.2 8.9 %collective-permute-start.37 = (f32[12,16,128]{2,1,0:T(8,128)S(1)}, f32[12,16,128]{2,1,0:T(8,128)S(1)}, u32[]{:S(2)}, u32[]{:S(2)}) collective-permute-start(f32[12,16,128]{2,1,0:T(8,128)S(1)} %get-tuple-element.120), channel_id=1, source_target_pairs={{0,1},{1,0},{2,4},{3,5},{4,2},{5,3},{6,8},{7,9},{8,6},{9,7},{10,12... | collective-permute-start | bytes 294920 | tf_op jit(solution)/shard_map/ppermute | solution.py:328
  132.3 8.8 %collective-permute-start.38 = (f32[12,16,128]{2,1,0:T(8,128)S(1)}, f32[12,16,128]{2,1,0:T(8,128)S(1)}, u32[]{:S(2)}, u32[]{:S(2)}) collective-permute-start(f32[12,16,128]{2,1,0:T(8,128)S(1)} %get-tuple-element.121), channel_id=1, source_target_pairs={{0,1},{1,0},{2,5},{3,4},{4,3},{5,2},{6,9},{7,8},{8,7},{9,6},{10,13... | collective-permute-start | bytes 294920 | tf_op jit(solution)/shard_map/ppermute | solution.py:328
  132.7 9.5 %collective-permute-start.39 = (f32[12,16,128]{2,1,0:T(8,128)S(1)}, f32[12,16,128]{2,1,0:T(8,128)S(1)}, u32[]{:S(2)}, u32[]{:S(2)}) collective-permute-start(f32[12,16,128]{2,1,0:T(8,128)S(1)} %get-tuple-element.122), channel_id=1, source_target_pairs={{0,2},{1,4},{2,0},{3,6},{4,1},{5,8},{6,3},{7,10},{8,5},{9,12},{10,... | collective-permute-start | bytes 294920 | tf_op jit(solution)/shard_map/ppermute | solution.py:328
  149.6 9.5 %collective-permute-start.45 = (f32[12,16,128]{2,1,0:T(8,128)S(1)}, f32[12,16,128]{2,1,0:T(8,128)S(1)}, u32[]{:S(2)}, u32[]{:S(2)}) collective-permute-start(f32[12,16,128]{2,1,0:T(8,128)S(1)} %get-tuple-element.129), channel_id=1, source_target_pairs={{0,1},{1,0},{2,3},{3,2},{4,5},{5,4},{6,7},{7,6},{8,9},{9,8},{10,11... | collective-permute-start | bytes 294920 | tf_op jit(solution)/shard_map/ppermute | solution.py:328
  150.8 4.5 %collective-permute-start.41 = (f32[16,640]{1,0:T(8,128)S(1)}, f32[16,640]{1,0:T(8,128)S(1)}, u32[]{:S(2)}, u32[]{:S(2)}) collective-permute-start(f32[16,640]{1,0:T(8,128)S(1)} %add.188), channel_id=1, source_target_pairs={{0,2},{1,3},{2,0},{3,1},{4,6},{5,7},{6,4},{7,5},{8,10},{9,11},{10,... | collective-permute-start | bytes 122888 | tf_op jit(solution)/shard_map/ppermute | solution.py:333
  155.3 5.8 %collective-permute-start.43 = (f32[16,640]{1,0:T(8,128)S(1)}, f32[16,640]{1,0:T(8,128)S(1)}, u32[]{:S(2)}, u32[]{:S(2)}) collective-permute-start(f32[16,640]{1,0:T(8,128)S(1)} %add.189), channel_id=1, source_target_pairs={{0,12},{1,13},{2,14},{3,15},{4,8},{5,9},{6,10},{7,11},{8,4},{9,5},... | collective-permute-start | bytes 122888 | tf_op jit(solution)/shard_map/ppermute | solution.py:333
  157.8 4.0 %collective-permute-start.42 = (f32[16,640]{1,0:T(8,128)S(1)}, f32[16,640]{1,0:T(8,128)S(1)}, u32[]{:S(2)}, u32[]{:S(2)}) collective-permute-start(f32[16,640]{1,0:T(8,128)S(1)} %add.189), channel_id=1, source_target_pairs={{0,4},{1,9},{2,6},{3,11},{4,0},{5,13},{6,2},{7,15},{8,12},{9,1},{1... | collective-permute-start | bytes 122888 | tf_op jit(solution)/shard_map/ppermute | solution.py:333
  157.8 5.7 %collective-permute-start.46 = (f32[12,16,128]{2,1,0:T(8,128)S(1)}, f32[12,16,128]{2,1,0:T(8,128)S(1)}, u32[]{:S(2)}, u32[]{:S(2)}) collective-permute-start(f32[12,16,128]{2,1,0:T(8,128)S(1)} %get-tuple-element.130), channel_id=1, source_target_pairs={{0,2},{1,3},{2,0},{3,1},{4,6},{5,7},{6,4},{7,5},{8,10},{9,11},{10,... | collective-permute-start | bytes 294920 | tf_op jit(solution)/shard_map/ppermute | solution.py:328
  159.1 8.5 %collective-permute-start.47 = (f32[12,16,128]{2,1,0:T(8,128)S(1)}, f32[12,16,128]{2,1,0:T(8,128)S(1)}, u32[]{:S(2)}, u32[]{:S(2)}) collective-permute-start(f32[12,16,128]{2,1,0:T(8,128)S(1)} %get-tuple-element.131), channel_id=1, source_target_pairs={{0,3},{1,2},{2,1},{3,0},{4,7},{5,6},{6,5},{7,4},{8,11},{9,10},{10,... | collective-permute-start | bytes 294920 | tf_op jit(solution)/shard_map/ppermute | solution.py:328
  159.1 8.5 %collective-permute-start.48 = (f32[12,16,128]{2,1,0:T(8,128)S(1)}, f32[12,16,128]{2,1,0:T(8,128)S(1)}, u32[]{:S(2)}, u32[]{:S(2)}) collective-permute-start(f32[12,16,128]{2,1,0:T(8,128)S(1)} %get-tuple-element.132), channel_id=1, source_target_pairs={{0,1},{1,0},{2,4},{3,5},{4,2},{5,3},{6,8},{7,9},{8,6},{9,7},{10,12... | collective-permute-start | bytes 294920 | tf_op jit(solution)/shard_map/ppermute | solution.py:328
  161.1 6.5 %collective-permute-start.49 = (f32[12,16,128]{2,1,0:T(8,128)S(1)}, f32[12,16,128]{2,1,0:T(8,128)S(1)}, u32[]{:S(2)}, u32[]{:S(2)}) collective-permute-start(f32[12,16,128]{2,1,0:T(8,128)S(1)} %get-tuple-element.133), channel_id=1, source_target_pairs={{0,1},{1,0},{2,5},{3,4},{4,3},{5,2},{6,9},{7,8},{8,7},{9,6},{10,13... | collective-permute-start | bytes 294920 | tf_op jit(solution)/shard_map/ppermute | solution.py:328
  161.8 6.8 %collective-permute-start.50 = (f32[12,16,128]{2,1,0:T(8,128)S(1)}, f32[12,16,128]{2,1,0:T(8,128)S(1)}, u32[]{:S(2)}, u32[]{:S(2)}) collective-permute-start(f32[12,16,128]{2,1,0:T(8,128)S(1)} %get-tuple-element.134), channel_id=1, source_target_pairs={{0,2},{1,4},{2,0},{3,6},{4,1},{5,8},{6,3},{7,10},{8,5},{9,12},{10,... | collective-permute-start | bytes 294920 | tf_op jit(solution)/shard_map/ppermute | solution.py:328
  163.6 5.1 %collective-permute-start.44 = (f32[16,640]{1,0:T(8,128)S(1)}, f32[16,640]{1,0:T(8,128)S(1)}, u32[]{:S(2)}, u32[]{:S(2)}) collective-permute-start(f32[16,640]{1,0:T(8,128)S(1)} %select_add_fusion.1.small_a), channel_id=1, source_target_pairs={{0,1},{1,0},{2,3},{3,2},{4,5},{5,4},{6,7},{7,6},{8,9},{9,8},{10,11... | collective-permute-start | bytes 122888 | tf_op jit(solution)/shard_map/ppermute | solution.py:333
  170.7 3.2 %collective-permute-start.51 = (f32[12,16,128]{2,1,0:T(8,128)S(1)}, f32[12,16,128]{2,1,0:T(8,128)S(1)}, u32[]{:S(2)}, u32[]{:S(2)}) collective-permute-start(f32[12,16,128]{2,1,0:T(8,128)S(1)} %get-tuple-element.138), channel_id=1, source_target_pairs={{0,1},{1,0},{2,3},{3,2},{4,5},{5,4},{6,7},{7,6},{8,9},{9,8},{10,11... | collective-permute-start | bytes 294920 | tf_op jit(solution)/shard_map/ppermute | solution.py:328
  170.8 6.9 %collective-permute-start.52 = (f32[12,16,128]{2,1,0:T(8,128)S(1)}, f32[12,16,128]{2,1,0:T(8,128)S(1)}, u32[]{:S(2)}, u32[]{:S(2)}) collective-permute-start(f32[12,16,128]{2,1,0:T(8,128)S(1)} %get-tuple-element.139), channel_id=1, source_target_pairs={{0,2},{1,3},{2,0},{3,1},{4,6},{5,7},{6,4},{7,5},{8,10},{9,11},{10,... | collective-permute-start | bytes 294920 | tf_op jit(solution)/shard_map/ppermute | solution.py:328
  173.3 9.0 %collective-permute-start.53 = (f32[12,16,128]{2,1,0:T(8,128)S(1)}, f32[12,16,128]{2,1,0:T(8,128)S(1)}, u32[]{:S(2)}, u32[]{:S(2)}) collective-permute-start(f32[12,16,128]{2,1,0:T(8,128)S(1)} %get-tuple-element.140), channel_id=1, source_target_pairs={{0,3},{1,2},{2,1},{3,0},{4,7},{5,6},{6,5},{7,4},{8,11},{9,10},{10,... | collective-permute-start | bytes 294920 | tf_op jit(solution)/shard_map/ppermute | solution.py:328
  173.4 8.9 %collective-permute-start.54 = (f32[12,16,128]{2,1,0:T(8,128)S(1)}, f32[12,16,128]{2,1,0:T(8,128)S(1)}, u32[]{:S(2)}, u32[]{:S(2)}) collective-permute-start(f32[12,16,128]{2,1,0:T(8,128)S(1)} %get-tuple-element.141), channel_id=1, source_target_pairs={{0,1},{1,0},{2,4},{3,5},{4,2},{5,3},{6,8},{7,9},{8,6},{9,7},{10,12... | collective-permute-start | bytes 294920 | tf_op jit(solution)/shard_map/ppermute | solution.py:328
  173.5 8.8 %collective-permute-start.55 = (f32[12,16,128]{2,1,0:T(8,128)S(1)}, f32[12,16,128]{2,1,0:T(8,128)S(1)}, u32[]{:S(2)}, u32[]{:S(2)}) collective-permute-start(f32[12,16,128]{2,1,0:T(8,128)S(1)} %get-tuple-element.142), channel_id=1, source_target_pairs={{0,1},{1,0},{2,5},{3,4},{4,3},{5,2},{6,9},{7,8},{8,7},{9,6},{10,13... | collective-permute-start | bytes 294920 | tf_op jit(solution)/shard_map/ppermute | solution.py:328
  173.9 9.5 %collective-permute-start.56 = (f32[12,16,128]{2,1,0:T(8,128)S(1)}, f32[12,16,128]{2,1,0:T(8,128)S(1)}, u32[]{:S(2)}, u32[]{:S(2)}) collective-permute-start(f32[12,16,128]{2,1,0:T(8,128)S(1)} %get-tuple-element.143), channel_id=1, source_target_pairs={{0,2},{1,4},{2,0},{3,6},{4,1},{5,8},{6,3},{7,10},{8,5},{9,12},{10,... | collective-permute-start | bytes 294920 | tf_op jit(solution)/shard_map/ppermute | solution.py:328
  191.1 7.9 %collective-permute-start.62 = (f32[12,16,128]{2,1,0:T(8,128)S(1)}, f32[12,16,128]{2,1,0:T(8,128)S(1)}, u32[]{:S(2)}, u32[]{:S(2)}) collective-permute-start(f32[12,16,128]{2,1,0:T(8,128)S(1)} %get-tuple-element.150), channel_id=1, source_target_pairs={{0,1},{1,0},{2,3},{3,2},{4,5},{5,4},{6,7},{7,6},{8,9},{9,8},{10,11... | collective-permute-start | bytes 294920 | tf_op jit(solution)/shard_map/ppermute | solution.py:328
  192.3 4.5 %collective-permute-start.58 = (f32[16,640]{1,0:T(8,128)S(1)}, f32[16,640]{1,0:T(8,128)S(1)}, u32[]{:S(2)}, u32[]{:S(2)}) collective-permute-start(f32[16,640]{1,0:T(8,128)S(1)} %add.191), channel_id=1, source_target_pairs={{0,2},{1,3},{2,0},{3,1},{4,6},{5,7},{6,4},{7,5},{8,10},{9,11},{10,... | collective-permute-start | bytes 122888 | tf_op jit(solution)/shard_map/ppermute | solution.py:333
  196.8 5.8 %collective-permute-start.60 = (f32[16,640]{1,0:T(8,128)S(1)}, f32[16,640]{1,0:T(8,128)S(1)}, u32[]{:S(2)}, u32[]{:S(2)}) collective-permute-start(f32[16,640]{1,0:T(8,128)S(1)} %add.192), channel_id=1, source_target_pairs={{0,12},{1,13},{2,14},{3,15},{4,8},{5,9},{6,10},{7,11},{8,4},{9,5},... | collective-permute-start | bytes 122888 | tf_op jit(solution)/shard_map/ppermute | solution.py:333
  197.7 4.9 %collective-permute-start.59 = (f32[16,640]{1,0:T(8,128)S(1)}, f32[16,640]{1,0:T(8,128)S(1)}, u32[]{:S(2)}, u32[]{:S(2)}) collective-permute-start(f32[16,640]{1,0:T(8,128)S(1)} %add.192), channel_id=1, source_target_pairs={{0,4},{1,9},{2,6},{3,11},{4,0},{5,13},{6,2},{7,15},{8,12},{9,1},{1... | collective-permute-start | bytes 122888 | tf_op jit(solution)/shard_map/ppermute | solution.py:333
  197.7 7.0 %collective-permute-start.63 = (f32[12,16,128]{2,1,0:T(8,128)S(1)}, f32[12,16,128]{2,1,0:T(8,128)S(1)}, u32[]{:S(2)}, u32[]{:S(2)}) collective-permute-start(f32[12,16,128]{2,1,0:T(8,128)S(1)} %get-tuple-element.151), channel_id=1, source_target_pairs={{0,2},{1,3},{2,0},{3,1},{4,6},{5,7},{6,4},{7,5},{8,10},{9,11},{10,... | collective-permute-start | bytes 294920 | tf_op jit(solution)/shard_map/ppermute | solution.py:328
  199.0 7.6 %collective-permute-start.64 = (f32[12,16,128]{2,1,0:T(8,128)S(1)}, f32[12,16,128]{2,1,0:T(8,128)S(1)}, u32[]{:S(2)}, u32[]{:S(2)}) collective-permute-start(f32[12,16,128]{2,1,0:T(8,128)S(1)} %get-tuple-element.152), channel_id=1, source_target_pairs={{0,3},{1,2},{2,1},{3,0},{4,7},{5,6},{6,5},{7,4},{8,11},{9,10},{10,... | collective-permute-start | bytes 294920 | tf_op jit(solution)/shard_map/ppermute | solution.py:328
  199.0 7.6 %collective-permute-start.65 = (f32[12,16,128]{2,1,0:T(8,128)S(1)}, f32[12,16,128]{2,1,0:T(8,128)S(1)}, u32[]{:S(2)}, u32[]{:S(2)}) collective-permute-start(f32[12,16,128]{2,1,0:T(8,128)S(1)} %get-tuple-element.153), channel_id=1, source_target_pairs={{0,1},{1,0},{2,4},{3,5},{4,2},{5,3},{6,8},{7,9},{8,6},{9,7},{10,12... | collective-permute-start | bytes 294920 | tf_op jit(solution)/shard_map/ppermute | solution.py:328
  202.6 3.9 %collective-permute-start.66 = (f32[12,16,128]{2,1,0:T(8,128)S(1)}, f32[12,16,128]{2,1,0:T(8,128)S(1)}, u32[]{:S(2)}, u32[]{:S(2)}) collective-permute-start(f32[12,16,128]{2,1,0:T(8,128)S(1)} %get-tuple-element.154), channel_id=1, source_target_pairs={{0,1},{1,0},{2,5},{3,4},{4,3},{5,2},{6,9},{7,8},{8,7},{9,6},{10,13... | collective-permute-start | bytes 294920 | tf_op jit(solution)/shard_map/ppermute | solution.py:328
  202.6 5.9 %collective-permute-start.67 = (f32[12,16,128]{2,1,0:T(8,128)S(1)}, f32[12,16,128]{2,1,0:T(8,128)S(1)}, u32[]{:S(2)}, u32[]{:S(2)}) collective-permute-start(f32[12,16,128]{2,1,0:T(8,128)S(1)} %get-tuple-element.155), channel_id=1, source_target_pairs={{0,2},{1,4},{2,0},{3,6},{4,1},{5,8},{6,3},{7,10},{8,5},{9,12},{10,... | collective-permute-start | bytes 294920 | tf_op jit(solution)/shard_map/ppermute | solution.py:328
  204.6 3.9 %collective-permute-start.61 = (f32[16,640]{1,0:T(8,128)S(1)}, f32[16,640]{1,0:T(8,128)S(1)}, u32[]{:S(2)}, u32[]{:S(2)}) collective-permute-start(f32[16,640]{1,0:T(8,128)S(1)} %select_add_fusion.small_a), channel_id=1, source_target_pairs={{0,1},{1,0},{2,3},{3,2},{4,5},{5,4},{6,7},{7,6},{8,9},{9,8},{10,11... | collective-permute-start | bytes 122888 | tf_op jit(solution)/shard_map/ppermute | solution.py:333
  (43 other events, 206.3 us)
Sparse Core Ops, SparseCore 0:
  10.2 43.5 all-gather.1

commit v2 on v1

v2 whole, which is shorter than its diff:
```python
import functools
import jax
import jax.numpy as jnp
from jax import lax
from jax.experimental import pallas as pl
from jax.experimental.pallas import tpu as pltpu
from jax.sharding import PartitionSpec as P

ITERS = 3
LANES = 6
PAD = 32
WIDE = 128
BF = jnp.bfloat16
F32 = jnp.float32
VMEM = pl.BlockSpec(memory_space=pltpu.VMEM)
SMEM = pl.BlockSpec(memory_space=pltpu.SMEM)
HBM = pl.BlockSpec(memory_space=pltpu.HBM)
PARTS = 8
FIRST_LIMIT = 31
NT = (((1,), (1,)), ((), ()))


def matching(pairs, rest):
    both = list(pairs) + list(rest)
    return sorted(both + [(second, first) for first, second in both])


def flipped(mask, devices):
    return [(i, i ^ mask) for i in range(devices)]


def lane_pairs(devices):
    odd = range(2, devices - 2, 4)
    ends = [(0, 1), (devices - 2, devices - 1)]
    return (
        flipped(2, devices),
        flipped(3, devices),
        matching([(i + core, i + 2 + core) for i in odd for core in (0, 1)], ends),
        matching([(i + core, i + 3 - core) for i in odd for core in (0, 1)], ends),
        matching([(i, i + 3) for i in range(1, devices - 3, 2)], [(0, devices - 3), (2, devices - 1)]),
        flipped(1, devices),
    )


def split_hi_lo(value):
    high = value.astype(BF)
    return high, (value - high.astype(F32)).astype(BF)


def routing(partner, capacity):
    face_count = partner.size
    subs = partner.shape[0]
    own = lax.axis_index("sub")
    ids = partner.reshape(face_count)
    peer = ids // face_count
    chip_gap = jnp.abs(peer // 2 - own // 2)
    lowest = jnp.minimum(peer // 2, own // 2)
    crossed = (peer + own) % 2
    lane = jnp.where(chip_gap == 0, 5, jnp.where(chip_gap == 1, 2 * (lowest % 2) + crossed, 4))
    order = jnp.arange(face_count, dtype=jnp.int32)
    same = lane[:, None] == lane[None, :]
    send_pos = jnp.sum(same & (order[None, :] < order[:, None]), axis=1, dtype=jnp.int32)
    recv_pos = jnp.sum(same & (ids[None, :] < ids[:, None]), axis=1, dtype=jnp.int32)
    slots = jnp.arange(LANES * capacity, dtype=jnp.int32)
    hit = slots[:, None] == (lane * capacity + send_pos)[None, :]
    source = jnp.sum(jnp.where(hit, order[None, :], 0), axis=1, dtype=jnp.int32)
    arrival = lane * capacity + recv_pos
    block = (1 + lane) * subs + (ids // partner.shape[1]) % subs
    return jnp.concatenate([source, arrival, block]).astype(jnp.int32)


class Sizes:
    def __init__(self, load, coupling, coarse_inv, devices):
        self.planes = devices // 4
        self.subs, self.faces, self.loads, self.dof = load.shape
        self.total = self.subs * self.faces
        self.unknowns = self.faces * self.dof
        self.slots_per_lane = 3 * self.total // 8
        self.slots = LANES * self.slots_per_lane
        self.primal = coupling.shape[1]
        self.coarse = coarse_inv.shape[1]
        self.own_rows = coarse_inv.shape[0]
        self.blocks = (1 + LANES) * self.subs
        self.pick_width = -(-self.blocks * PAD // WIDE) * WIDE
        self.carry_rows = self.slots_per_lane * (self.loads + self.primal) + 8


def call(kernel, sizes, outs, ins, specs, scratch, limit, name, flops=0, moved=0):
    return pl.pallas_call(
        functools.partial(kernel, sizes),
        out_shape=outs,
        in_specs=specs,
        out_specs=[VMEM] * len(outs),
        scratch_shapes=scratch,
        compiler_params=pltpu.CompilerParams(vmem_limit_bytes=limit * 2**20),
        cost_estimate=pl.CostEstimate(flops=flops, bytes_accessed=moved, transcendentals=0),
        name=name,
    )(*ins)


def shape(*dims, dtype=F32):
    return jax.ShapeDtypeStruct(dims, dtype)


def unpack_kernel(z, tab, coupling, corner_row, *rest):
    arrived, rest = rest[:LANES], rest[LANES:]
    spread, pick, held, names = rest
    per = z.slots_per_lane
    width = z.subs * PAD
    names[...] = jnp.full(names.shape, -1.0, F32)
    names[:, 0:width] = corner_row[:, 0:width]
    for lane in range(LANES):
        names[:, (1 + lane) * width:(2 + lane) * width] = arrived[lane][per * (z.loads + z.primal):per * (z.loads + z.primal) + 8, 0:width]
        for pos in range(per):
            row = per * z.loads + pos * z.primal
            held[lane * per + pos] = arrived[lane][row:row + z.primal, :]
    rows = lax.broadcasted_iota(jnp.int32, pick.shape, 0).astype(F32)
    pick[...] = jnp.where(rows == names[0:1, :], 1.0, 0.0).astype(BF)
    gap = jnp.zeros((PAD - z.primal, z.dof), F32)
    blank = jnp.zeros((PAD, z.dof), BF)
    for face in range(z.total):
        sub, side = face // z.faces, face % z.faces
        own = coupling[sub, :, side * z.dof:(side + 1) * z.dof]
        other = -held[tab[z.slots + face]]
        for place, value in enumerate((own, other)):
            high, low = split_hi_lo(jnp.concatenate([value, gap], axis=0))
            spread[face, place * 4 * PAD:(place + 1) * 4 * PAD, :] = jnp.concatenate([high, low, high, blank], axis=0)


def assemble_kernel(masks, z, own, *rest):
    stacks, (upper, lower) = rest[:len(masks)], rest[len(masks):]
    count = z.own_rows
    for mask, stack in zip(masks, stacks):
        for place, flip in enumerate((mask, mask ^ 2)):
            start = pl.multiple_of((own[0] ^ flip) * count, count)
            high, low = split_hi_lo(stack[place * count:(place + 1) * count, :])
            upper[pl.ds(start, count), :] = high
            lower[pl.ds(start, count), :] = low


def apply_in_kernel(z, vec, scalars, weights, stiff, copies, packed, image, shares):
    for face in range(z.total):
        sub, side = face // z.faces, face % z.faces
        high, low = split_hi_lo(vec[face])
        packed[sub, 0:z.loads, side * z.dof:(side + 1) * z.dof] = high
        packed[sub, z.loads:, side * z.dof:(side + 1) * z.dof] = low
    n = z.loads
    rows = jnp.zeros((2 * n, WIDE), F32)
    for sub in range(z.subs):
        rows = rows + lax.dot_general(packed[sub], weights[sub], NT, preferred_element_type=F32)
    rows = rows[0:n] + rows[n:]
    rows = rows + pltpu.roll(rows, WIDE - PAD, 1)
    step = z.unknowns // PARTS
    kappa = jnp.zeros((n, z.dof), F32)
    for sub in range(z.subs):
        total = jnp.zeros((2 * n, z.unknowns), F32)
        for part in range(PARTS):
            if copies:
                copies[sub * PARTS + part].wait()
            total = total + jnp.dot(
                packed[sub, :, part * step:(part + 1) * step],
                stiff[sub, part * step:(part + 1) * step, :],
                preferred_element_type=F32,
            )
        total = total[0:n] + total[n:]
        for side in range(z.faces):
            piece = total[:, side * z.dof:(side + 1) * z.dof]
            image[sub * z.faces + side] = piece
            kappa = kappa + piece * vec[sub * z.faces + side]
    column = lax.broadcasted_iota(jnp.int32, (n, WIDE), 1)
    share = jnp.where(column % (2 * PAD) < PAD, rows, 0.0)
    for place, value in enumerate([kappa] + scalars):
        share = jnp.where(column == PAD + place, jnp.sum(value, axis=1, keepdims=True), share)
    shares[0:n, :] = share


def fill_lanes(z, tab, field, lanes):
    for lane in range(LANES):
        for pos in range(z.slots_per_lane):
            lanes[lane][pos] = field[tab[lane * z.slots_per_lane + pos]]


def take_lanes(z, arrived, held):
    per = z.slots_per_lane
    for lane in range(LANES):
        held[lane * per:(lane + 1) * per] = arrived[lane][0:per]


def load_kernel(z, tab, load, coupling, corner_row, corner_groups, stiff, image, shares, *rest):
    lanes, (near, weights, packed, sems) = rest[:LANES], rest[LANES:]
    step = z.unknowns // PARTS
    copies = [
        pltpu.make_async_copy(
            stiff.at[sub, pl.ds(part * step, step), :],
            near.at[sub, pl.ds(part * step, step), :],
            sems.at[sub * PARTS + part],
        )
        for sub in range(z.subs)
        for part in range(PARTS)
    ]
    for copy in copies:
        copy.start()
    per = z.slots_per_lane
    base = per * z.loads
    for lane in range(LANES):
        for pos in range(per):
            face = tab[lane * per + pos]
            sub = face // z.faces
            start = pl.multiple_of((face - sub * z.faces) * z.dof, z.dof)
            row = base + pos * z.primal
            lanes[lane][row:row + z.primal, :] = coupling[sub, :, pl.ds(start, z.dof)]
        lanes[lane][base + per * z.primal:z.carry_rows, :] = corner_row[...]
    weights[...] = jnp.zeros_like(weights)
    gap = jnp.zeros((PAD - z.primal, z.unknowns), F32)
    for sub in range(z.subs):
        high, low = split_hi_lo(jnp.concatenate([coupling[sub], gap], axis=0))
        weights[sub, sub * 2 * PAD:sub * 2 * PAD + PAD, :] = high
        weights[sub, sub * 2 * PAD + PAD:sub * 2 * PAD + 2 * PAD, :] = low
    apply_in_kernel(z, load, [], weights, near, copies, packed, image, shares)
    shares[z.loads:, :] = corner_groups[...]
    for lane in range(LANES):
        for pos in range(per):
            lanes[lane][pos * z.loads:(pos + 1) * z.loads, :] = image[tab[lane * per + pos]]


def precond_kernel(z, tab, weighted, residual, old_image, weights, stiff, *rest):
    arrived, rest = rest[:LANES], rest[LANES:]
    vec, image, shares = rest[:3]
    lanes, (packed, held) = rest[3:3 + LANES], rest[3 + LANES:]
    take_lanes(z, arrived, held)
    gamma = jnp.zeros((z.loads, z.dof), F32)
    eta = jnp.zeros((z.loads, z.dof), F32)
    for face in range(z.total):
        value = 0.25 * (weighted[face] - held[tab[z.slots + face]])
        vec[face] = value
        gamma = gamma + residual[face] * value
        eta = eta + old_image[face] * value
    apply_in_kernel(z, vec, [gamma, eta], weights, stiff, None, packed, image, shares)
    fill_lanes(z, tab, image, lanes)


def coarse_in_kernel(z, shares, spot, inv_high, inv_low, pick, picked):
    n = z.loads
    rows = [stack[place, 0:n] for stack in shares for place in range(4)]
    high, low = split_hi_lo(jnp.concatenate(rows, axis=1))
    together = rows
    while len(together) > 1:
        together = [first + second for first, second in zip(together[0::2], together[1::2])]
    primal = jnp.dot(jnp.concatenate([high, low], axis=0), spot[...], preferred_element_type=F32)
    primal = primal[0:n] + primal[n:]
    high, low = split_hi_lo(primal)
    both = jnp.dot(jnp.concatenate([high, low], axis=0), inv_high[...], preferred_element_type=F32)
    lifted = (both[0:n] + both[n:]) + jnp.dot(high, inv_low[...], preferred_element_type=F32)
    energy = jnp.sum(primal * lifted, axis=1, keepdims=True)
    high, low = split_hi_lo(lifted)
    values = jnp.dot(jnp.concatenate([high, low], axis=0), pick[...], preferred_element_type=F32)
    column = lax.broadcasted_iota(jnp.int32, (n, WIDE), 1)
    for block in range(z.blocks):
        group, place = divmod(block * PAD, WIDE)
        upper = values[0:n, group * WIDE:(group + 1) * WIDE]
        lower = values[n:, group * WIDE:(group + 1) * WIDE]
        first = pltpu.roll(upper, (WIDE - place) % WIDE, 1)
        second = pltpu.roll(upper, (WIDE + PAD - place) % WIDE, 1)
        third = pltpu.roll(lower, (WIDE + 2 * PAD - place) % WIDE, 1)
        mixed = jnp.where(column < PAD, first, jnp.where(column < 2 * PAD, second, third))
        picked[block] = jnp.where(column < 3 * PAD, mixed, 0.0).astype(BF)
    return energy, together[0]


def image_of_face(z, tab, face, image, held, picked, spread):
    sides = jnp.concatenate([picked[face // z.faces], picked[tab[z.slots + z.total + face]]], axis=1)
    lift = jnp.dot(sides, spread[face], preferred_element_type=F32)
    return (image[face] - held[tab[z.slots + face]]) + lift


def start_kernel(z, tab, image, spot, upper, lower, pick, spread, blocks, *rest):
    shares, rest = rest[:z.planes], rest[z.planes:]
    arrived, rest = rest[:LANES], rest[LANES:]
    residual, weighted = rest[:2]
    lanes, (held, picked) = rest[2:2 + LANES], rest[2 + LANES:]
    for lane in range(LANES):
        for pos in range(z.slots_per_lane):
            held[lane * z.slots_per_lane + pos] = arrived[lane][pos * z.loads:(pos + 1) * z.loads, :]
    coarse_in_kernel(z, shares, spot, upper, lower, pick, picked)
    for face in range(z.total):
        value = image_of_face(z, tab, face, image, held, picked, spread)
        residual[face] = value
        weighted[face] = jnp.dot(value.astype(BF), blocks[face], preferred_element_type=F32)
    fill_lanes(z, tab, weighted, lanes)


def step_kernel(first, last, z, tab, image, spot, upper, lower, pick, spread, blocks, vec, old_residual, *rest):
    shares, rest = rest[:z.planes], rest[z.planes:]
    if not first:
        old_solution, old_direction, old_image, old_scalars = rest[:4]
        rest = rest[4:]
    arrived, rest = rest[:LANES], rest[LANES:]
    solution_out, residual = rest[:2]
    rest = rest[2:]
    if not last:
        direction, new_image, scalars, weighted = rest[:4]
        lanes, rest = rest[4:4 + LANES], rest[4 + LANES:]
    held, picked = rest
    take_lanes(z, arrived, held)
    energy, together = coarse_in_kernel(z, shares, spot, upper, lower, pick, picked)
    kappa, gamma, eta = [together[:, PAD + place:PAD + place + 1] for place in range(3)]
    curvature = 2.0 * (kappa + energy)
    beta = None
    if not first:
        beta = gamma / old_scalars[:, 0:1]
        curvature = curvature + beta * (2.0 * eta + beta * old_scalars[:, 1:2])
    alpha = gamma / curvature
    if not last:
        column = lax.broadcasted_iota(jnp.int32, (z.loads, WIDE), 1)
        scalars[...] = jnp.where(column == 0, gamma, curvature)
    wide = (z.loads, z.dof)
    alpha_wide = jnp.broadcast_to(alpha, wide)
    beta_wide = None if first else jnp.broadcast_to(beta, wide)
    for face in range(z.total):
        ahead = image_of_face(z, tab, face, image, held, picked, spread)
        along = vec[face]
        if not first:
            ahead = ahead + beta_wide * old_image[face]
            along = along + beta_wide * old_direction[face]
        moved = alpha_wide * along
        solution_out[face] = moved if first else old_solution[face] + moved
        value = old_residual[face] - alpha_wide * ahead
        residual[face] = value
        if not last:
            direction[face] = along
            new_image[face] = ahead
            weighted[face] = jnp.dot(value.astype(BF), blocks[face], preferred_element_type=F32)
    if not last:
        fill_lanes(z, tab, weighted, lanes)


def exchange(lanes, devices):
    return [lax.ppermute(lane, "sub", pairs) for lane, pairs in zip(lanes, lane_pairs(devices))]


def gathered(rows, devices):
    pair = jnp.concatenate([rows, lax.ppermute(rows, "sub", flipped(2, devices))])
    stacks = [(0, pair)] + [(mask, lax.ppermute(pair, "sub", flipped(mask, devices))) for mask in range(4, devices, 4)]
    return stacks + [(mask ^ 1, lax.ppermute(stack, "sub", flipped(1, devices))) for mask, stack in stacks]


def gathered_shares(share, devices):
    def other(value, mask):
        return lax.ppermute(value, "sub", flipped(mask, devices))

    plane = jnp.stack([share, other(share, 1), other(share, 2), other(share, 3)])
    return [plane] + [other(plane, mask) for mask in range(4, devices, 4)]


def on_device(load, stiff_inv, face_blocks, coupling, coarse_inv, corners, partner):
    devices = lax.axis_size("sub")
    z = Sizes(load, coupling, coarse_inv, devices)
    stacks = gathered(coarse_inv, devices)
    masks = tuple(mask for mask, _ in stacks)
    stacks = [stack for _, stack in stacks]
    tab = routing(partner, z.slots_per_lane)

    numbers = jnp.pad(corners.astype(F32), ((0, 0), (0, PAD - z.primal)), constant_values=-1.0)
    row = jnp.pad(numbers.reshape(1, -1), ((0, 0), (0, WIDE - z.subs * PAD)), constant_values=-1.0)
    corner_row = jnp.broadcast_to(row, (8, WIDE))
    apart = jnp.pad(numbers, ((0, 0), (0, WIDE // z.subs - PAD)), constant_values=-1.0)
    corner_groups = jnp.broadcast_to(apart.reshape(1, WIDE), (8, WIDE))

    field = shape(z.total, z.loads, z.dof)
    lane_field = [shape(z.slots_per_lane, z.loads, z.dof)] * LANES
    held = pltpu.VMEM((z.slots, z.loads, z.dof), F32)
    picked = pltpu.VMEM((z.blocks, z.loads, WIDE), BF)
    apply_scratch = [pltpu.VMEM((z.subs, 2 * z.loads, z.unknowns), BF)]
    apply_cost = dict(flops=2 * z.total * z.dof * z.unknowns * z.loads, moved=stiff_inv.size * 2)

    load_faces = load.reshape(z.total, z.loads, z.dof)
    image, shares, *lanes = call(
        load_kernel, z,
        [field, shape(z.loads + 8, WIDE)]
        + [shape(z.carry_rows, z.dof)] * LANES
        + [shape(z.subs, z.unknowns, z.unknowns, dtype=BF), shape(z.subs, 4 * PAD, z.unknowns, dtype=BF)],
        (tab, load_faces, coupling, corner_row, corner_groups, stiff_inv), [SMEM] + [VMEM] * 4 + [HBM],
        apply_scratch + [pltpu.SemaphoreType.DMA((z.subs * PARTS,))], FIRST_LIMIT, "apply_load", **apply_cost,
    )
    near, weights = lanes[LANES:]
    shares = gathered_shares(shares, devices)
    arrived = exchange(lanes[:LANES], devices)
    names = jnp.concatenate([stack[:, z.loads, :] for stack in shares]).reshape(-1)
    spot = (names[:, None] == jnp.arange(z.coarse, dtype=F32)[None, :]).astype(BF)
    spread, pick = call(
        unpack_kernel, z,
        [shape(z.total, 8 * PAD, z.dof, dtype=BF), shape(z.coarse, z.pick_width, dtype=BF)],
        (tab, coupling, corner_row, *arrived), [SMEM] + [VMEM] * (2 + LANES),
        [pltpu.VMEM((z.slots, z.primal, z.dof), F32), pltpu.VMEM((8, z.pick_width), F32)],
        8, "unpack_coupling",
    )
    blocks = face_blocks.reshape(z.total, z.dof, z.dof)
    inv_shape = shape(z.coarse, z.coarse, dtype=BF)
    upper, lower = call(
        functools.partial(assemble_kernel, masks), z, [inv_shape, inv_shape],
        (lax.axis_index("sub").reshape(1).astype(jnp.int32), *stacks),
        [SMEM] + [VMEM] * len(masks), [], 8, "assemble_coarse",
    )
    fixed = (spot, upper, lower, pick, spread, blocks)
    residual, weighted, *lanes = call(
        start_kernel, z, [field, field] + lane_field,
        (tab, image, *fixed, *shares, *arrived), [SMEM] + [VMEM] * (7 + z.planes + LANES),
        [held, picked], 8, "first_residual",
    )
    state = None
    for iteration in range(ITERS):
        first, last = iteration == 0, iteration + 1 == ITERS
        arrived = exchange(lanes, devices)
        old_image = residual if first else state[2]
        vec, image, shares, *lanes = call(
            precond_kernel, z, [field, field, shape(z.loads, WIDE)] + lane_field,
            (tab, weighted, residual, old_image, weights, near, *arrived),
            [SMEM] + [VMEM] * (5 + LANES),
            apply_scratch + [held], 8, "precond_apply", **apply_cost,
        )
        shares = gathered_shares(shares, devices)
        arrived = exchange(lanes, devices)
        ins = [tab, image, *fixed, vec, residual, *shares] + ([] if first else list(state)) + list(arrived)
        outs = [field, field] + ([] if last else [field, field, shape(z.loads, WIDE), field] + lane_field)
        result = call(
            functools.partial(step_kernel, first, last), z, outs, ins, [SMEM] + [VMEM] * (len(ins) - 1),
            [held, picked], 8, "cg_step",
        )
        multipliers, residual = result[:2]
        if not last:
            direction, old, scalars, weighted = result[2:6]
            lanes = result[6:]
            state = (multipliers, direction, old, scalars)
    return multipliers.reshape(load.shape), residual.reshape(load.shape)


def solution(mesh):
    return jax.shard_map(
        on_device,
        mesh=mesh,
        in_specs=(
            P(("parts", "sub"), None, None, None),
            P(("parts", "sub"), None, None),
            P(("parts", "sub"), None, None, None),
            P(("parts", "sub"), None, None),
            P(("parts", "sub"), None),
            P(("parts", "sub"), None),
            P(("parts", "sub"), None),
        ),
        out_specs=(P(("parts", "sub"), None, None, None), P(("parts", "sub"), None, None, None)),
        check_vma=False,
    )
```

time: 219 us -> 171 us (0.78)
  local copies, waits for them, and re-layouts: 38.3 us -> 2.94 us
  between operations: 14.4 us -> 1.01 us
  Pallas kernels: 41.2 us -> 30.1 us
  waiting for transfers between devices: 55.6 us -> 65.4 us
  starting transfers between devices: 67 us -> 70 us
    unnamed x76 -> x9, local copies, waits for them, and re-layouts: 37.4 us -> 1.97 us
    ppermute x20 -> x32, starting transfers between devices: 18.8 us -> 36.6 us  [the longest x24 26.8 us: other(): return lax.ppermute(value, 'sub', flipped(mask, devices))]
    ppermute x48 -> x42, starting transfers between devices: 48.1 us -> 33.4 us  [exchange(): lax.ppermute(lane, 'sub', pairs)]
    pallas_call x10, Pallas kernels: 41.2 us -> 30.1 us  [call(): pl.pallas_call(functools.partial(kernel, sizes), out_shape=outs, in_specs...]
    ppermute x20 -> x32, waiting for transfers between devices: 19.5 us -> 25 us  [the longest x24 16.9 us: other(): return lax.ppermute(value, 'sub', flipped(mask, devices))]
    ppermute x48 -> x42, waiting for transfers between devices: 35.4 us -> 40.4 us  [exchange(): lax.ppermute(lane, 'sub', pairs)]
  transfers between devices with their start and end apart: 69 -> 74, of which waited for: 26 -> 26; matrix products, arithmetic and copies ran while one was open for 1% -> 0% of each run, Pallas kernels for 5% -> 1%
where the time goes in v2:
time: 171 us
  starting transfers between devices  70 us (41%)
  waiting for transfers between devices  65.4 us (38%)
  Pallas kernels  30.1 us (18%)
  local copies, waits for them, and re-layouts  2.94 us (2%)
    ppermute x42, waiting for transfers between devices, exchange(): lax.ppermute(lane, 'sub', pairs)  40.4 us
    ppermute x42, starting transfers between devices, exchange(): lax.ppermute(lane, 'sub', pairs)  33.4 us
    pallas_call x10, Pallas kernels, call(): pl.pallas_call(functools.partial(kernel, sizes), out_shape=outs, in_specs...  30.1 us
    ppermute x24, starting transfers between devices, other(): return lax.ppermute(value, 'sub', flipped(mask, devices))  26.8 us
    ppermute x24, waiting for transfers between devices, other(): return lax.ppermute(value, 'sub', flipped(mask, devices))  16.9 us
    ppermute x3, waiting for transfers between devices, gathered(): lax.ppermute(pair, 'sub', flipped(mask, devices))  8.09 us
    ppermute x3, starting transfers between devices, gathered(): lax.ppermute(pair, 'sub', flipped(mask, devices))  4.45 us
    ppermute x4, starting transfers between devices, gathered(): lax.ppermute(stack, 'sub', flipped(1, devices))  3.57 us
  transfers between devices with their start and end apart: 74, of which 26 were waited for; matrix products, arithmetic and copies ran while one was open for 0% of the time, Pallas kernels for 1%

profile of v2, /device:TPU:0, one launch (start us, length us, event | category | flops | bytes accessed | tf_op | source)
XLA Modules:
  0.0 171.0 jit_solution(9666016168123475956)
XLA Ops:
  0.6 0.7 convert_element_type.14
  1.4 0.8 reshape.193
  2.7 1.0 copy-done.1
  3.7 0.9 copy-done.2
  4.6 7.7 %apply_load.1 = (f32[32,16,128]{2,1,0:T(8,128)S(1)}, f32[24,128]{1,0:T(8,128)S(1)}, f32[488,128]{1,0:T(8,128)S(1)}, f32[488,128]{1,0:T(8,128)S(1)}, f32[488,128]...) custom-call(s32[136]{0:T(256)S(1)} %pad_add_fusion.tab, ...), custom_call_target="tpu_custom_call" | custom-call | flops 268435456 | bytes 16777216 | tf_op jit(solution)/shard_map/apply_load/pallas_call | solution.py:89
  12.3 2.5 %collective-permute-start.2 = (f32[24,128]{1,0:T(8,128)S(1)}, f32[24,128]{1,0:T(8,128)S(1)}, u32[]{:S(2)}, u32[]{:S(2)}) collective-permute-start(f32[24,128]{1,0:T(8,128)S(1)} %get-tuple-element.78), channel_id=1, source_target_pairs={{0,3},{1,2},{2,1},{3,0},{4,7},{5,6},{6,5},{7,4},{8,11},{9,10},{10,... | collective-permute-start | bytes 36872 | tf_op jit(solution)/shard_map/ppermute | solution.py:349
  15.4 1.7 %collective-permute-start.6 = (f32[32,512]{1,0:T(8,128)S(1)}, f32[32,512]{1,0:T(8,128)S(1)}, u32[]{:S(2)}, u32[]{:S(2)}) collective-permute-start(f32[32,512]{1,0:T(8,128)S(1)} %copy-done.3), channel_id=1, source_target_pairs={{0,2},{1,3},{2,0},{3,1},{4,6},{5,7},{6,4},{7,5},{8,10},{9,11},{10,... | collective-permute-start | bytes 196616 | tf_op jit(solution)/shard_map/ppermute | solution.py:342
  17.2 1.3 collective-permute-done.1
  18.5 2.7 %collective-permute-start.4 = (f32[4,24,128]{2,0,1:T(4,128)S(1)}, f32[4,24,128]{2,0,1:T(4,128)S(1)}, u32[]{:S(2)}, u32[]{:S(2)}) collective-permute-start(f32[4,24,128]{2,0,1:T(4,128)S(1)} %pad_maximum_fusion), channel_id=1, source_target_pairs={{0,8},{1,9},{2,10},{3,11},{4,12},{5,13},{6,14},{7,15},{8,0},{9,1},... | collective-permute-start | bytes 147464 | tf_op jit(solution)/shard_map/ppermute | solution.py:349
  21.2 1.6 collective-permute-start.3
  23.0 3.7 %collective-permute-start.9 = (f32[64,512]{1,0:T(8,128)S(1)}, f32[64,512]{1,0:T(8,128)S(1)}, u32[]{:S(2)}, u32[]{:S(2)}) collective-permute-start(f32[64,512]{1,0:T(8,128)S(1)} %constant_dynamic-update-slice_fusion.rest_0_), channel_id=1, source_target_pairs={{0,12},{1,13},{2,14},{3,15},{4,8},{5,9},{6,10},{7,11},{8,4},{9,5},... | collective-permute-start | bytes 393224 | tf_op jit(solution)/shard_map/ppermute | solution.py:343
  26.7 0.8 collective-permute-start.7
  27.5 1.8 %collective-permute-done.5.rest_3_ = f32[4,24,128]{2,1,0:T(8,128)S(1)} collective-permute-done((f32[4,24,128]{2,1,0:T(8,128)S(1)}, f32[4,24,128]{2,1,0:T(8,128)S(1)}, u32[]{:S(2)}, u32[]{:S(2)}) %collective-permute-start.5) | collective-permute-done | bytes 49184 | tf_op jit(solution)/shard_map/ppermute | solution.py:349
  30.0 2.1 %collective-permute-done.9.rest_3_ = f32[64,512]{1,0:T(8,128)S(1)} collective-permute-done((f32[64,512]{1,0:T(8,128)S(1)}, f32[64,512]{1,0:T(8,128)S(1)}, u32[]{:S(2)}, u32[]{:S(2)}) %collective-permute-start.9) | collective-permute-done | bytes 131104 | tf_op jit(solution)/shard_map/ppermute | solution.py:343
  32.1 6.0 %collective-permute-done.8.rest_2_ = f32[64,512]{1,0:T(8,128)S(1)} collective-permute-done((f32[64,512]{1,0:T(8,128)S(1)}, f32[64,512]{1,0:T(8,128)S(1)}, u32[]{:S(2)}, u32[]{:S(2)}) %collective-permute-start.8) | collective-permute-done | bytes 131104 | tf_op jit(solution)/shard_map/ppermute | solution.py:343
  38.1 1.2 collective-permute-start.18
  39.4 9.1 %collective-permute-done.15.rest_1_.rest_5_ = f32[488,128]{1,0:T(8,128)S(1)} collective-permute-done((f32[488,128]{1,0:T(8,128)S(1)}, f32[488,128]{1,0:T(8,128)S(1)}, u32[]{:S(2)}, u32[]{:S(2)}) %collective-permute-start.15) | collective-permute-done | bytes 249888 | tf_op jit(solution)/shard_map/ppermute | solution.py:338
  49.1 1.8 %collective-permute-done.18.rest_4_.rest_8_ = f32[488,128]{1,0:T(8,128)S(1)} collective-permute-done((f32[488,128]{1,0:T(8,128)S(1)}, f32[488,128]{1,0:T(8,128)S(1)}, u32[]{:S(2)}, u32[]{:S(2)}) %collective-permute-start.18) | collective-permute-done | bytes 249888 | tf_op jit(solution)/shard_map/ppermute | solution.py:338
  50.9 3.0 %collective-permute-start.11 = (f32[64,512]{1,0:T(8,128)S(1)}, f32[64,512]{1,0:T(8,128)S(1)}, u32[]{:S(2)}, u32[]{:S(2)}) collective-permute-start(f32[64,512]{1,0:T(8,128)S(1)} %collective-permute-done.7.rest_1_), channel_id=1, source_target_pairs={{0,1},{1,0},{2,3},{3,2},{4,5},{5,4},{6,7},{7,6},{8,9},{9,8},{10,11... | collective-permute-start | bytes 393224 | tf_op jit(solution)/shard_map/ppermute | solution.py:344
  54.3 1.0 unpack_coupling.1
  55.5 2.3 %first_residual.1 = (f32[32,16,128]{2,1,0:T(8,128)S(1)}, f32[32,16,128]{2,1,0:T(8,128)S(1)}, f32[12,16,128]{2,1,0:T(8,128)S(1)}, f32[12,16,128]{2,1,0:T(8,128)S(...) custom-call(s32[136]{0:T(256)S(1)} %pad_add_fusion.tab, ...), custom_call_target="tpu_custom_call" | custom-call | tf_op jit(solution)/shard_map/first_residual/pallas_call | solution.py:89
  57.9 1.3 collective-permute-start.21
  59.3 0.8 collective-permute-start.22
  60.1 4.2 %collective-permute-start.24 = (f32[12,16,128]{2,1,0:T(8,128)S(1)}, f32[12,16,128]{2,1,0:T(8,128)S(1)}, u32[]{:S(2)}, u32[]{:S(2)}) collective-permute-start(f32[12,16,128]{2,1,0:T(8,128)S(1)} %get-tuple-element.97), channel_id=1, source_target_pairs={{0,13},{1,4},{2,15},{3,6},{4,1},{5,8},{6,3},{7,10},{8,5},{9,12},{1... | collective-permute-start | bytes 294920 | tf_op jit(solution)/shard_map/ppermute | solution.py:338
  65.0 5.2 %collective-permute-done.24.rest_4_ = f32[12,16,128]{2,1,0:T(8,128)S(1)} collective-permute-done((f32[12,16,128]{2,1,0:T(8,128)S(1)}, f32[12,16,128]{2,1,0:T(8,128)S(1)}, u32[]{:S(2)}, u32[]{:S(2)}) %collective-permute-start.24) | collective-permute-done | bytes 98336 | tf_op jit(solution)/shard_map/ppermute | solution.py:338
  70.1 3.8 %precond_apply.3 = (f32[32,16,128]{2,1,0:T(8,128)S(1)}, f32[32,16,128]{2,1,0:T(8,128)S(1)}, f32[16,128]{1,0:T(8,128)S(1)}, f32[12,16,128]{2,1,0:T(8,128)S(1)}, f...) custom-call(s32[136]{0:T(256)S(1)} %pad_add_fusion.tab, ...), custom_call_target="tpu_custom_call" | custom-call | flops 268435456 | bytes 16777216 | tf_op jit(solution)/shard_map/precond_apply/pallas_call | solution.py:89
  74.0 1.7 %collective-permute-start.27 = (f32[16,128]{1,0:T(8,128)S(1)}, f32[16,128]{1,0:T(8,128)S(1)}, u32[]{:S(2)}, u32[]{:S(2)}) collective-permute-start(f32[16,128]{1,0:T(8,128)S(1)} %get-tuple-element.101), channel_id=1, source_target_pairs={{0,2},{1,3},{2,0},{3,1},{4,6},{5,7},{6,4},{7,5},{8,10},{9,11},{10,... | collective-permute-start | bytes 24584 | tf_op jit(solution)/shard_map/ppermute | solution.py:349
  76.2 0.8 collective-permute-done.28
  77.7 4.1 %collective-permute-start.31 = (f32[4,16,128]{2,1,0:T(8,128)S(1)}, f32[4,16,128]{2,1,0:T(8,128)S(1)}, u32[]{:S(2)}, u32[]{:S(2)}) collective-permute-start(f32[4,16,128]{2,1,0:T(8,128)S(1)} %pad_maximum_fusion.1.rest_0_), channel_id=1, source_target_pairs={{0,12},{1,13},{2,14},{3,15},{4,8},{5,9},{6,10},{7,11},{8,4},{9,5},... | collective-permute-start | bytes 98312 | tf_op jit(solution)/shard_map/ppermute | solution.py:349
  82.5 1.3 collective-permute-done.31.rest_3_
  84.0 2.7 %collective-permute-done.30.rest_2_ = f32[4,16,128]{2,1,0:T(8,128)S(1)} collective-permute-done((f32[4,16,128]{2,1,0:T(8,128)S(1)}, f32[4,16,128]{2,1,0:T(8,128)S(1)}, u32[]{:S(2)}, u32[]{:S(2)}) %collective-permute-start.30) | collective-permute-done | bytes 32800 | tf_op jit(solution)/shard_map/ppermute | solution.py:349
  86.7 3.5 %collective-permute-start.36 = (f32[12,16,128]{2,1,0:T(8,128)S(1)}, f32[12,16,128]{2,1,0:T(8,128)S(1)}, u32[]{:S(2)}, u32[]{:S(2)}) collective-permute-start(f32[12,16,128]{2,1,0:T(8,128)S(1)} %get-tuple-element.106), channel_id=1, source_target_pairs={{0,13},{1,4},{2,15},{3,6},{4,1},{5,8},{6,3},{7,10},{8,5},{9,12},{1... | collective-permute-start | bytes 294920 | tf_op jit(solution)/shard_map/ppermute | solution.py:338
  90.2 4.5 %collective-permute-done.36.rest_8_ = f32[12,16,128]{2,1,0:T(8,128)S(1)} collective-permute-done((f32[12,16,128]{2,1,0:T(8,128)S(1)}, f32[12,16,128]{2,1,0:T(8,128)S(1)}, u32[]{:S(2)}, u32[]{:S(2)}) %collective-permute-start.36) | collective-permute-done | bytes 98336 | tf_op jit(solution)/shard_map/ppermute | solution.py:338
  94.7 2.3 %cg_step.3 = (f32[32,16,128]{2,1,0:T(8,128)S(1)}, f32[32,16,128]{2,1,0:T(8,128)S(1)}, f32[32,16,128]{2,1,0:T(8,128)S(1)}, f32[32,16,128]{2,1,0:T(8,128)S(1)}, f3...) custom-call(s32[136]{0:T(256)S(1)} %pad_add_fusion.tab, ...), custom_call_target="tpu_custom_call" | custom-call | tf_op jit(solution)/shard_map/cg_step/pallas_call | solution.py:89
  97.2 2.0 %collective-permute-start.40 = (f32[12,16,128]{2,1,0:T(8,128)S(1)}, f32[12,16,128]{2,1,0:T(8,128)S(1)}, u32[]{:S(2)}, u32[]{:S(2)}) collective-permute-start(f32[12,16,128]{2,1,0:T(8,128)S(1)} %get-tuple-element.113), channel_id=1, source_target_pairs={{0,1},{1,0},{2,4},{3,5},{4,2},{5,3},{6,8},{7,9},{8,6},{9,7},{10,12... | collective-permute-start | bytes 294920 | tf_op jit(solution)/shard_map/ppermute | solution.py:338
  99.3 3.7 %collective-permute-start.42 = (f32[12,16,128]{2,1,0:T(8,128)S(1)}, f32[12,16,128]{2,1,0:T(8,128)S(1)}, u32[]{:S(2)}, u32[]{:S(2)}) collective-permute-start(f32[12,16,128]{2,1,0:T(8,128)S(1)} %get-tuple-element.115), channel_id=1, source_target_pairs={{0,13},{1,4},{2,15},{3,6},{4,1},{5,8},{6,3},{7,10},{8,5},{9,12},{1... | collective-permute-start | bytes 294920 | tf_op jit(solution)/shard_map/ppermute | solution.py:338
  103.0 2.0 %collective-permute-done.39.rest_1_ = f32[12,16,128]{2,1,0:T(8,128)S(1)} collective-permute-done((f32[12,16,128]{2,1,0:T(8,128)S(1)}, f32[12,16,128]{2,1,0:T(8,128)S(1)}, u32[]{:S(2)}, u32[]{:S(2)}) %collective-permute-start.39) | collective-permute-done | bytes 98336 | tf_op jit(solution)/shard_map/ppermute | solution.py:338
  105.0 3.0 %collective-permute-done.42.rest_4_ = f32[12,16,128]{2,1,0:T(8,128)S(1)} collective-permute-done((f32[12,16,128]{2,1,0:T(8,128)S(1)}, f32[12,16,128]{2,1,0:T(8,128)S(1)}, u32[]{:S(2)}, u32[]{:S(2)}) %collective-permute-start.42) | collective-permute-done | bytes 98336 | tf_op jit(solution)/shard_map/ppermute | solution.py:338
  108.0 3.8 %precond_apply.4 = (f32[32,16,128]{2,1,0:T(8,128)S(1)}, f32[32,16,128]{2,1,0:T(8,128)S(1)}, f32[16,128]{1,0:T(8,128)S(1)}, f32[12,16,128]{2,1,0:T(8,128)S(1)}, f...) custom-call(s32[136]{0:T(256)S(1)} %pad_add_fusion.tab, ...), custom_call_target="tpu_custom_call" | custom-call | flops 268435456 | bytes 16777216 | tf_op jit(solution)/shard_map/precond_apply/pallas_call | solution.py:89
  111.9 0.7 collective-permute-start.45
  112.6 1.2 collective-permute-start.44
  114.0 0.9 collective-permute-done.46
  115.0 0.7 collective-permute-done.45
  115.6 2.5 %collective-permute-start.49 = (f32[4,16,128]{2,1,0:T(8,128)S(1)}, f32[4,16,128]{2,1,0:T(8,128)S(1)}, u32[]{:S(2)}, u32[]{:S(2)}) collective-permute-start(f32[4,16,128]{2,1,0:T(8,128)S(1)} %pad_maximum_fusion.2.rest_0_), channel_id=1, source_target_pairs={{0,12},{1,13},{2,14},{3,15},{4,8},{5,9},{6,10},{7,11},{8,4},{9,5},... | collective-permute-start | bytes 98312 | tf_op jit(solution)/shard_map/ppermute | solution.py:349
  118.1 1.9 %collective-permute-start.47 = (f32[4,16,128]{2,1,0:T(8,128)S(1)}, f32[4,16,128]{2,1,0:T(8,128)S(1)}, u32[]{:S(2)}, u32[]{:S(2)}) collective-permute-start(f32[4,16,128]{2,1,0:T(8,128)S(1)} %pad_maximum_fusion.2.rest_0_), channel_id=1, source_target_pairs={{0,4},{1,5},{2,6},{3,7},{4,0},{5,1},{6,2},{7,3},{8,12},{9,13},{10,... | collective-permute-start | bytes 98312 | tf_op jit(solution)/shard_map/ppermute | solution.py:349
  120.0 1.6 collective-permute-done.49.rest_3_
  121.6 1.3 collective-permute-done.48.rest_2_
  122.9 3.7 %collective-permute-start.54 = (f32[12,16,128]{2,1,0:T(8,128)S(1)}, f32[12,16,128]{2,1,0:T(8,128)S(1)}, u32[]{:S(2)}, u32[]{:S(2)}) collective-permute-start(f32[12,16,128]{2,1,0:T(8,128)S(1)} %get-tuple-element.127), channel_id=1, source_target_pairs={{0,13},{1,4},{2,15},{3,6},{4,1},{5,8},{6,3},{7,10},{8,5},{9,12},{1... | collective-permute-start | bytes 294920 | tf_op jit(solution)/shard_map/ppermute | solution.py:338
  126.7 4.3 %collective-permute-done.54.rest_12_ = f32[12,16,128]{2,1,0:T(8,128)S(1)} collective-permute-done((f32[12,16,128]{2,1,0:T(8,128)S(1)}, f32[12,16,128]{2,1,0:T(8,128)S(1)}, u32[]{:S(2)}, u32[]{:S(2)}) %collective-permute-start.54) | collective-permute-done | bytes 98336 | tf_op jit(solution)/shard_map/ppermute | solution.py:338
  131.0 2.4 %cg_step.4 = (f32[32,16,128]{2,1,0:T(8,128)S(1)}, f32[32,16,128]{2,1,0:T(8,128)S(1)}, f32[32,16,128]{2,1,0:T(8,128)S(1)}, f32[32,16,128]{2,1,0:T(8,128)S(1)}, f3...) custom-call(s32[136]{0:T(256)S(1)} %pad_add_fusion.tab, ...), custom_call_target="tpu_custom_call" | custom-call | tf_op jit(solution)/shard_map/cg_step/pallas_call | solution.py:89
  133.6 2.0 %collective-permute-start.58 = (f32[12,16,128]{2,1,0:T(8,128)S(1)}, f32[12,16,128]{2,1,0:T(8,128)S(1)}, u32[]{:S(2)}, u32[]{:S(2)}) collective-permute-start(f32[12,16,128]{2,1,0:T(8,128)S(1)} %get-tuple-element.134), channel_id=1, source_target_pairs={{0,1},{1,0},{2,4},{3,5},{4,2},{5,3},{6,8},{7,9},{8,6},{9,7},{10,12... | collective-permute-start | bytes 294920 | tf_op jit(solution)/shard_map/ppermute | solution.py:338
  135.6 4.3 %collective-permute-start.60 = (f32[12,16,128]{2,1,0:T(8,128)S(1)}, f32[12,16,128]{2,1,0:T(8,128)S(1)}, u32[]{:S(2)}, u32[]{:S(2)}) collective-permute-start(f32[12,16,128]{2,1,0:T(8,128)S(1)} %get-tuple-element.136), channel_id=1, source_target_pairs={{0,13},{1,4},{2,15},{3,6},{4,1},{5,8},{6,3},{7,10},{8,5},{9,12},{1... | collective-permute-start | bytes 294920 | tf_op jit(solution)/shard_map/ppermute | solution.py:338
  140.0 1.5 collective-permute-done.57.rest_1_
  141.5 3.6 %collective-permute-done.60.rest_4_ = f32[12,16,128]{2,1,0:T(8,128)S(1)} collective-permute-done((f32[12,16,128]{2,1,0:T(8,128)S(1)}, f32[12,16,128]{2,1,0:T(8,128)S(1)}, u32[]{:S(2)}, u32[]{:S(2)}) %collective-permute-start.60) | collective-permute-done | bytes 98336 | tf_op jit(solution)/shard_map/ppermute | solution.py:338
  145.1 3.8 %precond_apply.5 = (f32[32,16,128]{2,1,0:T(8,128)S(1)}, f32[32,16,128]{2,1,0:T(8,128)S(1)}, f32[16,128]{1,0:T(8,128)S(1)}, f32[12,16,128]{2,1,0:T(8,128)S(1)}, f...) custom-call(s32[136]{0:T(256)S(1)} %pad_add_fusion.tab, ...), custom_call_target="tpu_custom_call" | custom-call | flops 268435456 | bytes 16777216 | tf_op jit(solution)/shard_map/precond_apply/pallas_call | solution.py:89
  149.0 1.8 %collective-permute-start.62 = (f32[16,128]{1,0:T(8,128)S(1)}, f32[16,128]{1,0:T(8,128)S(1)}, u32[]{:S(2)}, u32[]{:S(2)}) collective-permute-start(f32[16,128]{1,0:T(8,128)S(1)} %get-tuple-element.140), channel_id=1, source_target_pairs={{0,1},{1,0},{2,3},{3,2},{4,5},{5,4},{6,7},{7,6},{8,9},{9,8},{10,11... | collective-permute-start | bytes 24584 | tf_op jit(solution)/shard_map/ppermute | solution.py:349
  151.1 0.9 collective-permute-done.64
  152.7 1.8 %collective-permute-start.67 = (f32[4,16,128]{2,1,0:T(8,128)S(1)}, f32[4,16,128]{2,1,0:T(8,128)S(1)}, u32[]{:S(2)}, u32[]{:S(2)}) collective-permute-start(f32[4,16,128]{2,1,0:T(8,128)S(1)} %pad_maximum_fusion.3.rest_0_), channel_id=1, source_target_pairs={{0,12},{1,13},{2,14},{3,15},{4,8},{5,9},{6,10},{7,11},{8,4},{9,5},... | collective-permute-start | bytes 98312 | tf_op jit(solution)/shard_map/ppermute | solution.py:349
  154.4 2.6 %collective-permute-start.65 = (f32[4,16,128]{2,1,0:T(8,128)S(1)}, f32[4,16,128]{2,1,0:T(8,128)S(1)}, u32[]{:S(2)}, u32[]{:S(2)}) collective-permute-start(f32[4,16,128]{2,1,0:T(8,128)S(1)} %pad_maximum_fusion.3.rest_0_), channel_id=1, source_target_pairs={{0,4},{1,5},{2,6},{3,7},{4,0},{5,1},{6,2},{7,3},{8,12},{9,13},{10,... | collective-permute-start | bytes 98312 | tf_op jit(solution)/shard_map/ppermute | solution.py:349
  157.1 1.3 collective-permute-done.67.rest_3_
  158.4 1.0 collective-permute-done.66.rest_2_
  159.4 3.4 %collective-permute-start.72 = (f32[12,16,128]{2,1,0:T(8,128)S(1)}, f32[12,16,128]{2,1,0:T(8,128)S(1)}, u32[]{:S(2)}, u32[]{:S(2)}) collective-permute-start(f32[12,16,128]{2,1,0:T(8,128)S(1)} %get-tuple-element.148), channel_id=1, source_target_pairs={{0,13},{1,4},{2,15},{3,6},{4,1},{5,8},{6,3},{7,10},{8,5},{9,12},{1... | collective-permute-start | bytes 294920 | tf_op jit(solution)/shard_map/ppermute | solution.py:338
  162.8 5.4 %collective-permute-done.72.rest_12_ = f32[12,16,128]{2,1,0:T(8,128)S(1)} collective-permute-done((f32[12,16,128]{2,1,0:T(8,128)S(1)}, f32[12,16,128]{2,1,0:T(8,128)S(1)}, u32[]{:S(2)}, u32[]{:S(2)}) %collective-permute-start.72) | collective-permute-done | bytes 98336 | tf_op jit(solution)/shard_map/ppermute | solution.py:338
  168.2 2.8 %cg_step.5 = (f32[32,16,128]{2,1,0:T(8,128)}, f32[32,16,128]{2,1,0:T(8,128)}) custom-call(s32[136]{0:T(256)S(1)} %pad_add_fusion.tab, f32[32,16,128]{2,1,0:T(8,128)S(1)} %get-tuple-element.138.image, bf16[2048,512]{1,0:T(8,128)(2,1)S(1)} %fusion.spot, bf16[512,512]{1,0:T(8,128)(2,1)S(1)} %get-tuple-element.79.upper, ...), custom_call_target="tpu_custom_call" | custom-call | tf_op jit(solution)/shard_map/cg_step/pallas_call | solution.py:89
  (131 shorter events, 8.0 us)
Async XLA Ops:
  12.3 4.9 %collective-permute-start.2 = (f32[24,128]{1,0:T(8,128)S(1)}, f32[24,128]{1,0:T(8,128)S(1)}, u32[]{:S(2)}, u32[]{:S(2)}) collective-permute-start(f32[24,128]{1,0:T(8,128)S(1)} %get-tuple-element.78), channel_id=1, source_target_pairs={{0,3},{1,2},{2,1},{3,0},{4,7},{5,6},{6,5},{7,4},{8,11},{9,10},{10,... | collective-permute-start | bytes 36872 | tf_op jit(solution)/shard_map/ppermute | solution.py:349
  15.4 7.6 %collective-permute-start.6 = (f32[32,512]{1,0:T(8,128)S(1)}, f32[32,512]{1,0:T(8,128)S(1)}, u32[]{:S(2)}, u32[]{:S(2)}) collective-permute-start(f32[32,512]{1,0:T(8,128)S(1)} %copy-done.3), channel_id=1, source_target_pairs={{0,2},{1,3},{2,0},{3,1},{4,6},{5,7},{6,4},{7,5},{8,10},{9,11},{10,... | collective-permute-start | bytes 196616 | tf_op jit(solution)/shard_map/ppermute | solution.py:342
  18.5 8.1 %collective-permute-start.4 = (f32[4,24,128]{2,0,1:T(4,128)S(1)}, f32[4,24,128]{2,0,1:T(4,128)S(1)}, u32[]{:S(2)}, u32[]{:S(2)}) collective-permute-start(f32[4,24,128]{2,0,1:T(4,128)S(1)} %pad_maximum_fusion), channel_id=1, source_target_pairs={{0,8},{1,9},{2,10},{3,11},{4,12},{5,13},{6,14},{7,15},{8,0},{9,1},... | collective-permute-start | bytes 147464 | tf_op jit(solution)/shard_map/ppermute | solution.py:349
  21.2 8.8 %collective-permute-start.3 = (f32[4,24,128]{2,0,1:T(4,128)S(1)}, f32[4,24,128]{2,0,1:T(4,128)S(1)}, u32[]{:S(2)}, u32[]{:S(2)}) collective-permute-start(f32[4,24,128]{2,0,1:T(4,128)S(1)} %pad_maximum_fusion), channel_id=1, source_target_pairs={{0,4},{1,5},{2,6},{3,7},{4,0},{5,1},{6,2},{7,3},{8,12},{9,13},{10,... | collective-permute-start | bytes 147464 | tf_op jit(solution)/shard_map/ppermute | solution.py:349
  22.8 6.5 %collective-permute-start.5 = (f32[4,24,128]{2,1,0:T(8,128)S(1)}, f32[4,24,128]{2,1,0:T(8,128)S(1)}, u32[]{:S(2)}, u32[]{:S(2)}) collective-permute-start(f32[4,24,128]{2,1,0:T(8,128)S(1)} %copy.13.rest_0_), channel_id=1, source_target_pairs={{0,12},{1,13},{2,14},{3,15},{4,8},{5,9},{6,10},{7,11},{8,4},{9,5},... | collective-permute-start | bytes 147464 | tf_op jit(solution)/shard_map/ppermute | solution.py:349
  23.0 9.1 %collective-permute-start.9 = (f32[64,512]{1,0:T(8,128)S(1)}, f32[64,512]{1,0:T(8,128)S(1)}, u32[]{:S(2)}, u32[]{:S(2)}) collective-permute-start(f32[64,512]{1,0:T(8,128)S(1)} %constant_dynamic-update-slice_fusion.rest_0_), channel_id=1, source_target_pairs={{0,12},{1,13},{2,14},{3,15},{4,8},{5,9},{6,10},{7,11},{8,4},{9,5},... | collective-permute-start | bytes 393224 | tf_op jit(solution)/shard_map/ppermute | solution.py:343
  26.7 11.4 %collective-permute-start.8 = (f32[64,512]{1,0:T(8,128)S(1)}, f32[64,512]{1,0:T(8,128)S(1)}, u32[]{:S(2)}, u32[]{:S(2)}) collective-permute-start(f32[64,512]{1,0:T(8,128)S(1)} %constant_dynamic-update-slice_fusion.rest_0_), channel_id=1, source_target_pairs={{0,8},{1,9},{2,10},{3,11},{4,12},{5,13},{6,14},{7,15},{8,0},{9,1},... | collective-permute-start | bytes 393224 | tf_op jit(solution)/shard_map/ppermute | solution.py:343
  26.7 11.4 %collective-permute-start.7 = (f32[64,512]{1,0:T(8,128)S(1)}, f32[64,512]{1,0:T(8,128)S(1)}, u32[]{:S(2)}, u32[]{:S(2)}) collective-permute-start(f32[64,512]{1,0:T(8,128)S(1)} %constant_dynamic-update-slice_fusion.rest_0_), channel_id=1, source_target_pairs={{0,4},{1,5},{2,6},{3,7},{4,0},{5,1},{6,2},{7,3},{8,12},{9,13},{10,... | collective-permute-start | bytes 393224 | tf_op jit(solution)/shard_map/ppermute | solution.py:343
  29.3 10.0 %collective-permute-start.14 = (f32[488,128]{1,0:T(8,128)S(1)}, f32[488,128]{1,0:T(8,128)S(1)}, u32[]{:S(2)}, u32[]{:S(2)}) collective-permute-start(f32[488,128]{1,0:T(8,128)S(1)} %get-tuple-element.81), channel_id=1, source_target_pairs={{0,2},{1,3},{2,0},{3,1},{4,6},{5,7},{6,4},{7,5},{8,10},{9,11},{10,... | collective-permute-start | bytes 749576 | tf_op jit(solution)/shard_map/ppermute | solution.py:338
  29.9 18.6 %collective-permute-start.15 = (f32[488,128]{1,0:T(8,128)S(1)}, f32[488,128]{1,0:T(8,128)S(1)}, u32[]{:S(2)}, u32[]{:S(2)}) collective-permute-start(f32[488,128]{1,0:T(8,128)S(1)} %get-tuple-element.82), channel_id=1, source_target_pairs={{0,3},{1,2},{2,1},{3,0},{4,7},{5,6},{6,5},{7,4},{8,11},{9,10},{10,... | collective-permute-start | bytes 749576 | tf_op jit(solution)/shard_map/ppermute | solution.py:338
  32.1 16.5 %collective-permute-start.16 = (f32[488,128]{1,0:T(8,128)S(1)}, f32[488,128]{1,0:T(8,128)S(1)}, u32[]{:S(2)}, u32[]{:S(2)}) collective-permute-start(f32[488,128]{1,0:T(8,128)S(1)} %get-tuple-element.83), channel_id=1, source_target_pairs={{0,1},{1,0},{2,4},{3,5},{4,2},{5,3},{6,8},{7,9},{8,6},{9,7},{10,12... | collective-permute-start | bytes 749576 | tf_op jit(solution)/shard_map/ppermute | solution.py:338
  38.0 11.0 %collective-permute-start.17 = (f32[488,128]{1,0:T(8,128)S(1)}, f32[488,128]{1,0:T(8,128)S(1)}, u32[]{:S(2)}, u32[]{:S(2)}) collective-permute-start(f32[488,128]{1,0:T(8,128)S(1)} %get-tuple-element.84), channel_id=1, source_target_pairs={{0,1},{1,0},{2,5},{3,4},{4,3},{5,2},{6,9},{7,8},{8,7},{9,6},{10,13... | collective-permute-start | bytes 749576 | tf_op jit(solution)/shard_map/ppermute | solution.py:338
  38.1 12.8 %collective-permute-start.18 = (f32[488,128]{1,0:T(8,128)S(1)}, f32[488,128]{1,0:T(8,128)S(1)}, u32[]{:S(2)}, u32[]{:S(2)}) collective-permute-start(f32[488,128]{1,0:T(8,128)S(1)} %get-tuple-element.85), channel_id=1, source_target_pairs={{0,13},{1,4},{2,15},{3,6},{4,1},{5,8},{6,3},{7,10},{8,5},{9,12},{1... | collective-permute-start | bytes 749576 | tf_op jit(solution)/shard_map/ppermute | solution.py:338
  39.3 15.0 %collective-permute-start.19 = (f32[488,128]{1,0:T(8,128)S(1)}, f32[488,128]{1,0:T(8,128)S(1)}, u32[]{:S(2)}, u32[]{:S(2)}) collective-permute-start(f32[488,128]{1,0:T(8,128)S(1)} %get-tuple-element.86), channel_id=1, source_target_pairs={{0,1},{1,0},{2,3},{3,2},{4,5},{5,4},{6,7},{7,6},{8,9},{9,8},{10,11... | collective-permute-start | bytes 749576 | tf_op jit(solution)/shard_map/ppermute | solution.py:338
  48.5 6.8 %collective-permute-start.10 = (f32[64,512]{1,0:T(8,128)S(1)}, f32[64,512]{1,0:T(8,128)S(1)}, u32[]{:S(2)}, u32[]{:S(2)}) collective-permute-start(f32[64,512]{1,0:T(8,128)S(1)} %constant_dynamic-update-slice_fusion.rest_0_), channel_id=1, source_target_pairs={{0,1},{1,0},{2,3},{3,2},{4,5},{5,4},{6,7},{7,6},{8,9},{9,8},{10,11... | collective-permute-start | bytes 393224 | tf_op jit(solution)/shard_map/ppermute | solution.py:344
  48.5 6.8 %collective-permute-start.13 = (f32[64,512]{1,0:T(8,128)S(1)}, f32[64,512]{1,0:T(8,128)S(1)}, u32[]{:S(2)}, u32[]{:S(2)}) collective-permute-start(f32[64,512]{1,0:T(8,128)S(1)} %collective-permute-done.9.rest_3_), channel_id=1, source_target_pairs={{0,1},{1,0},{2,3},{3,2},{4,5},{5,4},{6,7},{7,6},{8,9},{9,8},{10,11... | collective-permute-start | bytes 393224 | tf_op jit(solution)/shard_map/ppermute | solution.py:344
  49.1 6.3 %collective-permute-start.12 = (f32[64,512]{1,0:T(8,128)S(1)}, f32[64,512]{1,0:T(8,128)S(1)}, u32[]{:S(2)}, u32[]{:S(2)}) collective-permute-start(f32[64,512]{1,0:T(8,128)S(1)} %collective-permute-done.8.rest_2_), channel_id=1, source_target_pairs={{0,1},{1,0},{2,3},{3,2},{4,5},{5,4},{6,7},{7,6},{8,9},{9,8},{10,11... | collective-permute-start | bytes 393224 | tf_op jit(solution)/shard_map/ppermute | solution.py:344
  50.9 4.5 %collective-permute-start.11 = (f32[64,512]{1,0:T(8,128)S(1)}, f32[64,512]{1,0:T(8,128)S(1)}, u32[]{:S(2)}, u32[]{:S(2)}) collective-permute-start(f32[64,512]{1,0:T(8,128)S(1)} %collective-permute-done.7.rest_1_), channel_id=1, source_target_pairs={{0,1},{1,0},{2,3},{3,2},{4,5},{5,4},{6,7},{7,6},{8,9},{9,8},{10,11... | collective-permute-start | bytes 393224 | tf_op jit(solution)/shard_map/ppermute | solution.py:344
  57.9 6.5 %collective-permute-start.20 = (f32[12,16,128]{2,1,0:T(8,128)S(1)}, f32[12,16,128]{2,1,0:T(8,128)S(1)}, u32[]{:S(2)}, u32[]{:S(2)}) collective-permute-start(f32[12,16,128]{2,1,0:T(8,128)S(1)} %get-tuple-element.93), channel_id=1, source_target_pairs={{0,2},{1,3},{2,0},{3,1},{4,6},{5,7},{6,4},{7,5},{8,10},{9,11},{10,... | collective-permute-start | bytes 294920 | tf_op jit(solution)/shard_map/ppermute | solution.py:338
  57.9 7.0 %collective-permute-start.21 = (f32[12,16,128]{2,1,0:T(8,128)S(1)}, f32[12,16,128]{2,1,0:T(8,128)S(1)}, u32[]{:S(2)}, u32[]{:S(2)}) collective-permute-start(f32[12,16,128]{2,1,0:T(8,128)S(1)} %get-tuple-element.94), channel_id=1, source_target_pairs={{0,3},{1,2},{2,1},{3,0},{4,7},{5,6},{6,5},{7,4},{8,11},{9,10},{10,... | collective-permute-start | bytes 294920 | tf_op jit(solution)/shard_map/ppermute | solution.py:338
  59.3 5.7 %collective-permute-start.22 = (f32[12,16,128]{2,1,0:T(8,128)S(1)}, f32[12,16,128]{2,1,0:T(8,128)S(1)}, u32[]{:S(2)}, u32[]{:S(2)}) collective-permute-start(f32[12,16,128]{2,1,0:T(8,128)S(1)} %get-tuple-element.95), channel_id=1, source_target_pairs={{0,1},{1,0},{2,4},{3,5},{4,2},{5,3},{6,8},{7,9},{8,6},{9,7},{10,12... | collective-permute-start | bytes 294920 | tf_op jit(solution)/shard_map/ppermute | solution.py:338
  60.1 4.9 %collective-permute-start.23 = (f32[12,16,128]{2,1,0:T(8,128)S(1)}, f32[12,16,128]{2,1,0:T(8,128)S(1)}, u32[]{:S(2)}, u32[]{:S(2)}) collective-permute-start(f32[12,16,128]{2,1,0:T(8,128)S(1)} %get-tuple-element.96), channel_id=1, source_target_pairs={{0,1},{1,0},{2,5},{3,4},{4,3},{5,2},{6,9},{7,8},{8,7},{9,6},{10,13... | collective-permute-start | bytes 294920 | tf_op jit(solution)/shard_map/ppermute | solution.py:338
  60.1 10.1 %collective-permute-start.24 = (f32[12,16,128]{2,1,0:T(8,128)S(1)}, f32[12,16,128]{2,1,0:T(8,128)S(1)}, u32[]{:S(2)}, u32[]{:S(2)}) collective-permute-start(f32[12,16,128]{2,1,0:T(8,128)S(1)} %get-tuple-element.97), channel_id=1, source_target_pairs={{0,13},{1,4},{2,15},{3,6},{4,1},{5,8},{6,3},{7,10},{8,5},{9,12},{1... | collective-permute-start | bytes 294920 | tf_op jit(solution)/shard_map/ppermute | solution.py:338
  64.3 5.8 %collective-permute-start.25 = (f32[12,16,128]{2,1,0:T(8,128)S(1)}, f32[12,16,128]{2,1,0:T(8,128)S(1)}, u32[]{:S(2)}, u32[]{:S(2)}) collective-permute-start(f32[12,16,128]{2,1,0:T(8,128)S(1)} %get-tuple-element.98), channel_id=1, source_target_pairs={{0,1},{1,0},{2,3},{3,2},{4,5},{5,4},{6,7},{7,6},{8,9},{9,8},{10,11... | collective-permute-start | bytes 294920 | tf_op jit(solution)/shard_map/ppermute | solution.py:338
  74.0 3.7 %collective-permute-start.27 = (f32[16,128]{1,0:T(8,128)S(1)}, f32[16,128]{1,0:T(8,128)S(1)}, u32[]{:S(2)}, u32[]{:S(2)}) collective-permute-start(f32[16,128]{1,0:T(8,128)S(1)} %get-tuple-element.101), channel_id=1, source_target_pairs={{0,2},{1,3},{2,0},{3,1},{4,6},{5,7},{6,4},{7,5},{8,10},{9,11},{10,... | collective-permute-start | bytes 24584 | tf_op jit(solution)/shard_map/ppermute | solution.py:349
  75.9 14.3 %collective-permute-start.32 = (f32[12,16,128]{2,1,0:T(8,128)S(1)}, f32[12,16,128]{2,1,0:T(8,128)S(1)}, u32[]{:S(2)}, u32[]{:S(2)}) collective-permute-start(f32[12,16,128]{2,1,0:T(8,128)S(1)} %get-tuple-element.102), channel_id=1, source_target_pairs={{0,2},{1,3},{2,0},{3,1},{4,6},{5,7},{6,4},{7,5},{8,10},{9,11},{10,... | collective-permute-start | bytes 294920 | tf_op jit(solution)/shard_map/ppermute | solution.py:338
  77.7 6.0 %collective-permute-start.31 = (f32[4,16,128]{2,1,0:T(8,128)S(1)}, f32[4,16,128]{2,1,0:T(8,128)S(1)}, u32[]{:S(2)}, u32[]{:S(2)}) collective-permute-start(f32[4,16,128]{2,1,0:T(8,128)S(1)} %pad_maximum_fusion.1.rest_0_), channel_id=1, source_target_pairs={{0,12},{1,13},{2,14},{3,15},{4,8},{5,9},{6,10},{7,11},{8,4},{9,5},... | collective-permute-start | bytes 98312 | tf_op jit(solution)/shard_map/ppermute | solution.py:349
  81.8 4.8 %collective-permute-start.30 = (f32[4,16,128]{2,1,0:T(8,128)S(1)}, f32[4,16,128]{2,1,0:T(8,128)S(1)}, u32[]{:S(2)}, u32[]{:S(2)}) collective-permute-start(f32[4,16,128]{2,1,0:T(8,128)S(1)} %pad_maximum_fusion.1.rest_0_), channel_id=1, source_target_pairs={{0,8},{1,9},{2,10},{3,11},{4,12},{5,13},{6,14},{7,15},{8,0},{9,1},... | collective-permute-start | bytes 98312 | tf_op jit(solution)/shard_map/ppermute | solution.py:349
  81.8 4.8 %collective-permute-start.29 = (f32[4,16,128]{2,1,0:T(8,128)S(1)}, f32[4,16,128]{2,1,0:T(8,128)S(1)}, u32[]{:S(2)}, u32[]{:S(2)}) collective-permute-start(f32[4,16,128]{2,1,0:T(8,128)S(1)} %pad_maximum_fusion.1.rest_0_), channel_id=1, source_target_pairs={{0,4},{1,5},{2,6},{3,7},{4,0},{5,1},{6,2},{7,3},{8,12},{9,13},{10,... | collective-permute-start | bytes 98312 | tf_op jit(solution)/shard_map/ppermute | solution.py:349
  82.5 7.7 %collective-permute-start.33 = (f32[12,16,128]{2,1,0:T(8,128)S(1)}, f32[12,16,128]{2,1,0:T(8,128)S(1)}, u32[]{:S(2)}, u32[]{:S(2)}) collective-permute-start(f32[12,16,128]{2,1,0:T(8,128)S(1)} %get-tuple-element.103), channel_id=1, source_target_pairs={{0,3},{1,2},{2,1},{3,0},{4,7},{5,6},{6,5},{7,4},{8,11},{9,10},{10,... | collective-permute-start | bytes 294920 | tf_op jit(solution)/shard_map/ppermute | solution.py:338
  83.7 6.5 %collective-permute-start.34 = (f32[12,16,128]{2,1,0:T(8,128)S(1)}, f32[12,16,128]{2,1,0:T(8,128)S(1)}, u32[]{:S(2)}, u32[]{:S(2)}) collective-permute-start(f32[12,16,128]{2,1,0:T(8,128)S(1)} %get-tuple-element.104), channel_id=1, source_target_pairs={{0,1},{1,0},{2,4},{3,5},{4,2},{5,3},{6,8},{7,9},{8,6},{9,7},{10,12... | collective-permute-start | bytes 294920 | tf_op jit(solution)/shard_map/ppermute | solution.py:338
  86.7 8.0 %collective-permute-start.36 = (f32[12,16,128]{2,1,0:T(8,128)S(1)}, f32[12,16,128]{2,1,0:T(8,128)S(1)}, u32[]{:S(2)}, u32[]{:S(2)}) collective-permute-start(f32[12,16,128]{2,1,0:T(8,128)S(1)} %get-tuple-element.106), channel_id=1, source_target_pairs={{0,13},{1,4},{2,15},{3,6},{4,1},{5,8},{6,3},{7,10},{8,5},{9,12},{1... | collective-permute-start | bytes 294920 | tf_op jit(solution)/shard_map/ppermute | solution.py:338
  90.2 4.5 %collective-permute-start.37 = (f32[12,16,128]{2,1,0:T(8,128)S(1)}, f32[12,16,128]{2,1,0:T(8,128)S(1)}, u32[]{:S(2)}, u32[]{:S(2)}) collective-permute-start(f32[12,16,128]{2,1,0:T(8,128)S(1)} %get-tuple-element.107), channel_id=1, source_target_pairs={{0,1},{1,0},{2,3},{3,2},{4,5},{5,4},{6,7},{7,6},{8,9},{9,8},{10,11... | collective-permute-start | bytes 294920 | tf_op jit(solution)/shard_map/ppermute | solution.py:338
  97.1 5.9 %collective-permute-start.38 = (f32[12,16,128]{2,1,0:T(8,128)S(1)}, f32[12,16,128]{2,1,0:T(8,128)S(1)}, u32[]{:S(2)}, u32[]{:S(2)}) collective-permute-start(f32[12,16,128]{2,1,0:T(8,128)S(1)} %get-tuple-element.111), channel_id=1, source_target_pairs={{0,2},{1,3},{2,0},{3,1},{4,6},{5,7},{6,4},{7,5},{8,10},{9,11},{10,... | collective-permute-start | bytes 294920 | tf_op jit(solution)/shard_map/ppermute | solution.py:338
  97.1 7.8 %collective-permute-start.39 = (f32[12,16,128]{2,1,0:T(8,128)S(1)}, f32[12,16,128]{2,1,0:T(8,128)S(1)}, u32[]{:S(2)}, u32[]{:S(2)}) collective-permute-start(f32[12,16,128]{2,1,0:T(8,128)S(1)} %get-tuple-element.112), channel_id=1, source_target_pairs={{0,3},{1,2},{2,1},{3,0},{4,7},{5,6},{6,5},{7,4},{8,11},{9,10},{10,... | collective-permute-start | bytes 294920 | tf_op jit(solution)/shard_map/ppermute | solution.py:338
  97.2 7.8 %collective-permute-start.40 = (f32[12,16,128]{2,1,0:T(8,128)S(1)}, f32[12,16,128]{2,1,0:T(8,128)S(1)}, u32[]{:S(2)}, u32[]{:S(2)}) collective-permute-start(f32[12,16,128]{2,1,0:T(8,128)S(1)} %get-tuple-element.113), channel_id=1, source_target_pairs={{0,1},{1,0},{2,4},{3,5},{4,2},{5,3},{6,8},{7,9},{8,6},{9,7},{10,12... | collective-permute-start | bytes 294920 | tf_op jit(solution)/shard_map/ppermute | solution.py:338
  99.3 5.7 %collective-permute-start.41 = (f32[12,16,128]{2,1,0:T(8,128)S(1)}, f32[12,16,128]{2,1,0:T(8,128)S(1)}, u32[]{:S(2)}, u32[]{:S(2)}) collective-permute-start(f32[12,16,128]{2,1,0:T(8,128)S(1)} %get-tuple-element.114), channel_id=1, source_target_pairs={{0,1},{1,0},{2,5},{3,4},{4,3},{5,2},{6,9},{7,8},{8,7},{9,6},{10,13... | collective-permute-start | bytes 294920 | tf_op jit(solution)/shard_map/ppermute | solution.py:338
  99.3 8.8 %collective-permute-start.42 = (f32[12,16,128]{2,1,0:T(8,128)S(1)}, f32[12,16,128]{2,1,0:T(8,128)S(1)}, u32[]{:S(2)}, u32[]{:S(2)}) collective-permute-start(f32[12,16,128]{2,1,0:T(8,128)S(1)} %get-tuple-element.115), channel_id=1, source_target_pairs={{0,13},{1,4},{2,15},{3,6},{4,1},{5,8},{6,3},{7,10},{8,5},{9,12},{1... | collective-permute-start | bytes 294920 | tf_op jit(solution)/shard_map/ppermute | solution.py:338
  103.0 5.1 %collective-permute-start.43 = (f32[12,16,128]{2,1,0:T(8,128)S(1)}, f32[12,16,128]{2,1,0:T(8,128)S(1)}, u32[]{:S(2)}, u32[]{:S(2)}) collective-permute-start(f32[12,16,128]{2,1,0:T(8,128)S(1)} %get-tuple-element.116), channel_id=1, source_target_pairs={{0,1},{1,0},{2,3},{3,2},{4,5},{5,4},{6,7},{7,6},{8,9},{9,8},{10,11... | collective-permute-start | bytes 294920 | tf_op jit(solution)/shard_map/ppermute | solution.py:338
  111.9 3.7 %collective-permute-start.45 = (f32[16,128]{1,0:T(8,128)S(1)}, f32[16,128]{1,0:T(8,128)S(1)}, u32[]{:S(2)}, u32[]{:S(2)}) collective-permute-start(f32[16,128]{1,0:T(8,128)S(1)} %get-tuple-element.119), channel_id=1, source_target_pairs={{0,2},{1,3},{2,0},{3,1},{4,6},{5,7},{6,4},{7,5},{8,10},{9,11},{10,... | collective-permute-start | bytes 24584 | tf_op jit(solution)/shard_map/ppermute | solution.py:349
  113.8 12.9 %collective-permute-start.50 = (f32[12,16,128]{2,1,0:T(8,128)S(1)}, f32[12,16,128]{2,1,0:T(8,128)S(1)}, u32[]{:S(2)}, u32[]{:S(2)}) collective-permute-start(f32[12,16,128]{2,1,0:T(8,128)S(1)} %get-tuple-element.123), channel_id=1, source_target_pairs={{0,2},{1,3},{2,0},{3,1},{4,6},{5,7},{6,4},{7,5},{8,10},{9,11},{10,... | collective-permute-start | bytes 294920 | tf_op jit(solution)/shard_map/ppermute | solution.py:338
  115.6 6.0 %collective-permute-start.49 = (f32[4,16,128]{2,1,0:T(8,128)S(1)}, f32[4,16,128]{2,1,0:T(8,128)S(1)}, u32[]{:S(2)}, u32[]{:S(2)}) collective-permute-start(f32[4,16,128]{2,1,0:T(8,128)S(1)} %pad_maximum_fusion.2.rest_0_), channel_id=1, source_target_pairs={{0,12},{1,13},{2,14},{3,15},{4,8},{5,9},{6,10},{7,11},{8,4},{9,5},... | collective-permute-start | bytes 98312 | tf_op jit(solution)/shard_map/ppermute | solution.py:349
  118.1 4.8 %collective-permute-start.48 = (f32[4,16,128]{2,1,0:T(8,128)S(1)}, f32[4,16,128]{2,1,0:T(8,128)S(1)}, u32[]{:S(2)}, u32[]{:S(2)}) collective-permute-start(f32[4,16,128]{2,1,0:T(8,128)S(1)} %pad_maximum_fusion.2.rest_0_), channel_id=1, source_target_pairs={{0,8},{1,9},{2,10},{3,11},{4,12},{5,13},{6,14},{7,15},{8,0},{9,1},... | collective-permute-start | bytes 98312 | tf_op jit(solution)/shard_map/ppermute | solution.py:349
  118.1 4.8 %collective-permute-start.47 = (f32[4,16,128]{2,1,0:T(8,128)S(1)}, f32[4,16,128]{2,1,0:T(8,128)S(1)}, u32[]{:S(2)}, u32[]{:S(2)}) collective-permute-start(f32[4,16,128]{2,1,0:T(8,128)S(1)} %pad_maximum_fusion.2.rest_0_), channel_id=1, source_target_pairs={{0,4},{1,5},{2,6},{3,7},{4,0},{5,1},{6,2},{7,3},{8,12},{9,13},{10,... | collective-permute-start | bytes 98312 | tf_op jit(solution)/shard_map/ppermute | solution.py:349
  120.0 6.7 %collective-permute-start.51 = (f32[12,16,128]{2,1,0:T(8,128)S(1)}, f32[12,16,128]{2,1,0:T(8,128)S(1)}, u32[]{:S(2)}, u32[]{:S(2)}) collective-permute-start(f32[12,16,128]{2,1,0:T(8,128)S(1)} %get-tuple-element.124), channel_id=1, source_target_pairs={{0,3},{1,2},{2,1},{3,0},{4,7},{5,6},{6,5},{7,4},{8,11},{9,10},{10,... | collective-permute-start | bytes 294920 | tf_op jit(solution)/shard_map/ppermute | solution.py:338
  121.6 5.1 %collective-permute-start.52 = (f32[12,16,128]{2,1,0:T(8,128)S(1)}, f32[12,16,128]{2,1,0:T(8,128)S(1)}, u32[]{:S(2)}, u32[]{:S(2)}) collective-permute-start(f32[12,16,128]{2,1,0:T(8,128)S(1)} %get-tuple-element.125), channel_id=1, source_target_pairs={{0,1},{1,0},{2,4},{3,5},{4,2},{5,3},{6,8},{7,9},{8,6},{9,7},{10,12... | collective-permute-start | bytes 294920 | tf_op jit(solution)/shard_map/ppermute | solution.py:338
  122.9 3.8 %collective-permute-start.53 = (f32[12,16,128]{2,1,0:T(8,128)S(1)}, f32[12,16,128]{2,1,0:T(8,128)S(1)}, u32[]{:S(2)}, u32[]{:S(2)}) collective-permute-start(f32[12,16,128]{2,1,0:T(8,128)S(1)} %get-tuple-element.126), channel_id=1, source_target_pairs={{0,1},{1,0},{2,5},{3,4},{4,3},{5,2},{6,9},{7,8},{8,7},{9,6},{10,13... | collective-permute-start | bytes 294920 | tf_op jit(solution)/shard_map/ppermute | solution.py:338
  122.9 8.0 %collective-permute-start.54 = (f32[12,16,128]{2,1,0:T(8,128)S(1)}, f32[12,16,128]{2,1,0:T(8,128)S(1)}, u32[]{:S(2)}, u32[]{:S(2)}) collective-permute-start(f32[12,16,128]{2,1,0:T(8,128)S(1)} %get-tuple-element.127), channel_id=1, source_target_pairs={{0,13},{1,4},{2,15},{3,6},{4,1},{5,8},{6,3},{7,10},{8,5},{9,12},{1... | collective-permute-start | bytes 294920 | tf_op jit(solution)/shard_map/ppermute | solution.py:338
  126.7 4.3 %collective-permute-start.55 = (f32[12,16,128]{2,1,0:T(8,128)S(1)}, f32[12,16,128]{2,1,0:T(8,128)S(1)}, u32[]{:S(2)}, u32[]{:S(2)}) collective-permute-start(f32[12,16,128]{2,1,0:T(8,128)S(1)} %get-tuple-element.128), channel_id=1, source_target_pairs={{0,1},{1,0},{2,3},{3,2},{4,5},{5,4},{6,7},{7,6},{8,9},{9,8},{10,11... | collective-permute-start | bytes 294920 | tf_op jit(solution)/shard_map/ppermute | solution.py:338
  133.4 6.5 %collective-permute-start.56 = (f32[12,16,128]{2,1,0:T(8,128)S(1)}, f32[12,16,128]{2,1,0:T(8,128)S(1)}, u32[]{:S(2)}, u32[]{:S(2)}) collective-permute-start(f32[12,16,128]{2,1,0:T(8,128)S(1)} %get-tuple-element.132), channel_id=1, source_target_pairs={{0,2},{1,3},{2,0},{3,1},{4,6},{5,7},{6,4},{7,5},{8,10},{9,11},{10,... | collective-permute-start | bytes 294920 | tf_op jit(solution)/shard_map/ppermute | solution.py:338
  133.6 7.9 %collective-permute-start.57 = (f32[12,16,128]{2,1,0:T(8,128)S(1)}, f32[12,16,128]{2,1,0:T(8,128)S(1)}, u32[]{:S(2)}, u32[]{:S(2)}) collective-permute-start(f32[12,16,128]{2,1,0:T(8,128)S(1)} %get-tuple-element.133), channel_id=1, source_target_pairs={{0,3},{1,2},{2,1},{3,0},{4,7},{5,6},{6,5},{7,4},{8,11},{9,10},{10,... | collective-permute-start | bytes 294920 | tf_op jit(solution)/shard_map/ppermute | solution.py:338
  133.6 7.9 %collective-permute-start.58 = (f32[12,16,128]{2,1,0:T(8,128)S(1)}, f32[12,16,128]{2,1,0:T(8,128)S(1)}, u32[]{:S(2)}, u32[]{:S(2)}) collective-permute-start(f32[12,16,128]{2,1,0:T(8,128)S(1)} %get-tuple-element.134), channel_id=1, source_target_pairs={{0,1},{1,0},{2,4},{3,5},{4,2},{5,3},{6,8},{7,9},{8,6},{9,7},{10,12... | collective-permute-start | bytes 294920 | tf_op jit(solution)/shard_map/ppermute | solution.py:338
  135.6 5.9 %collective-permute-start.59 = (f32[12,16,128]{2,1,0:T(8,128)S(1)}, f32[12,16,128]{2,1,0:T(8,128)S(1)}, u32[]{:S(2)}, u32[]{:S(2)}) collective-permute-start(f32[12,16,128]{2,1,0:T(8,128)S(1)} %get-tuple-element.135), channel_id=1, source_target_pairs={{0,1},{1,0},{2,5},{3,4},{4,3},{5,2},{6,9},{7,8},{8,7},{9,6},{10,13... | collective-permute-start | bytes 294920 | tf_op jit(solution)/shard_map/ppermute | solution.py:338
  135.6 9.4 %collective-permute-start.60 = (f32[12,16,128]{2,1,0:T(8,128)S(1)}, f32[12,16,128]{2,1,0:T(8,128)S(1)}, u32[]{:S(2)}, u32[]{:S(2)}) collective-permute-start(f32[12,16,128]{2,1,0:T(8,128)S(1)} %get-tuple-element.136), channel_id=1, source_target_pairs={{0,13},{1,4},{2,15},{3,6},{4,1},{5,8},{6,3},{7,10},{8,5},{9,12},{1... | collective-permute-start | bytes 294920 | tf_op jit(solution)/shard_map/ppermute | solution.py:338
  140.0 5.1 %collective-permute-start.61 = (f32[12,16,128]{2,1,0:T(8,128)S(1)}, f32[12,16,128]{2,1,0:T(8,128)S(1)}, u32[]{:S(2)}, u32[]{:S(2)}) collective-permute-start(f32[12,16,128]{2,1,0:T(8,128)S(1)} %get-tuple-element.137), channel_id=1, source_target_pairs={{0,1},{1,0},{2,3},{3,2},{4,5},{5,4},{6,7},{7,6},{8,9},{9,8},{10,11... | collective-permute-start | bytes 294920 | tf_op jit(solution)/shard_map/ppermute | solution.py:338
  148.9 3.7 %collective-permute-start.63 = (f32[16,128]{1,0:T(8,128)S(1)}, f32[16,128]{1,0:T(8,128)S(1)}, u32[]{:S(2)}, u32[]{:S(2)}) collective-permute-start(f32[16,128]{1,0:T(8,128)S(1)} %get-tuple-element.140), channel_id=1, source_target_pairs={{0,2},{1,3},{2,0},{3,1},{4,6},{5,7},{6,4},{7,5},{8,10},{9,11},{10,... | collective-permute-start | bytes 24584 | tf_op jit(solution)/shard_map/ppermute | solution.py:349
  150.8 12.0 %collective-permute-start.68 = (f32[12,16,128]{2,1,0:T(8,128)S(1)}, f32[12,16,128]{2,1,0:T(8,128)S(1)}, u32[]{:S(2)}, u32[]{:S(2)}) collective-permute-start(f32[12,16,128]{2,1,0:T(8,128)S(1)} %get-tuple-element.144), channel_id=1, source_target_pairs={{0,2},{1,3},{2,0},{3,1},{4,6},{5,7},{6,4},{7,5},{8,10},{9,11},{10,... | collective-permute-start | bytes 294920 | tf_op jit(solution)/shard_map/ppermute | solution.py:338
  152.7 5.7 %collective-permute-start.67 = (f32[4,16,128]{2,1,0:T(8,128)S(1)}, f32[4,16,128]{2,1,0:T(8,128)S(1)}, u32[]{:S(2)}, u32[]{:S(2)}) collective-permute-start(f32[4,16,128]{2,1,0:T(8,128)S(1)} %pad_maximum_fusion.3.rest_0_), channel_id=1, source_target_pairs={{0,12},{1,13},{2,14},{3,15},{4,8},{5,9},{6,10},{7,11},{8,4},{9,5},... | collective-permute-start | bytes 98312 | tf_op jit(solution)/shard_map/ppermute | solution.py:349
  154.4 4.9 %collective-permute-start.66 = (f32[4,16,128]{2,1,0:T(8,128)S(1)}, f32[4,16,128]{2,1,0:T(8,128)S(1)}, u32[]{:S(2)}, u32[]{:S(2)}) collective-permute-start(f32[4,16,128]{2,1,0:T(8,128)S(1)} %pad_maximum_fusion.3.rest_0_), channel_id=1, source_target_pairs={{0,8},{1,9},{2,10},{3,11},{4,12},{5,13},{6,14},{7,15},{8,0},{9,1},... | collective-permute-start | bytes 98312 | tf_op jit(solution)/shard_map/ppermute | solution.py:349
  154.4 4.9 %collective-permute-start.65 = (f32[4,16,128]{2,1,0:T(8,128)S(1)}, f32[4,16,128]{2,1,0:T(8,128)S(1)}, u32[]{:S(2)}, u32[]{:S(2)}) collective-permute-start(f32[4,16,128]{2,1,0:T(8,128)S(1)} %pad_maximum_fusion.3.rest_0_), channel_id=1, source_target_pairs={{0,4},{1,5},{2,6},{3,7},{4,0},{5,1},{6,2},{7,3},{8,12},{9,13},{10,... | collective-permute-start | bytes 98312 | tf_op jit(solution)/shard_map/ppermute | solution.py:349
  157.1 5.7 %collective-permute-start.69 = (f32[12,16,128]{2,1,0:T(8,128)S(1)}, f32[12,16,128]{2,1,0:T(8,128)S(1)}, u32[]{:S(2)}, u32[]{:S(2)}) collective-permute-start(f32[12,16,128]{2,1,0:T(8,128)S(1)} %get-tuple-element.145), channel_id=1, source_target_pairs={{0,3},{1,2},{2,1},{3,0},{4,7},{5,6},{6,5},{7,4},{8,11},{9,10},{10,... | collective-permute-start | bytes 294920 | tf_op jit(solution)/shard_map/ppermute | solution.py:338
  158.4 4.4 %collective-permute-start.70 = (f32[12,16,128]{2,1,0:T(8,128)S(1)}, f32[12,16,128]{2,1,0:T(8,128)S(1)}, u32[]{:S(2)}, u32[]{:S(2)}) collective-permute-start(f32[12,16,128]{2,1,0:T(8,128)S(1)} %get-tuple-element.146), channel_id=1, source_target_pairs={{0,1},{1,0},{2,4},{3,5},{4,2},{5,3},{6,8},{7,9},{8,6},{9,7},{10,12... | collective-permute-start | bytes 294920 | tf_op jit(solution)/shard_map/ppermute | solution.py:338
  159.4 8.8 %collective-permute-start.72 = (f32[12,16,128]{2,1,0:T(8,128)S(1)}, f32[12,16,128]{2,1,0:T(8,128)S(1)}, u32[]{:S(2)}, u32[]{:S(2)}) collective-permute-start(f32[12,16,128]{2,1,0:T(8,128)S(1)} %get-tuple-element.148), channel_id=1, source_target_pairs={{0,13},{1,4},{2,15},{3,6},{4,1},{5,8},{6,3},{7,10},{8,5},{9,12},{1... | collective-permute-start | bytes 294920 | tf_op jit(solution)/shard_map/ppermute | solution.py:338
  162.8 5.4 %collective-permute-start.73 = (f32[12,16,128]{2,1,0:T(8,128)S(1)}, f32[12,16,128]{2,1,0:T(8,128)S(1)}, u32[]{:S(2)}, u32[]{:S(2)}) collective-permute-start(f32[12,16,128]{2,1,0:T(8,128)S(1)} %get-tuple-element.149), channel_id=1, source_target_pairs={{0,1},{1,0},{2,3},{3,2},{4,5},{5,4},{6,7},{7,6},{8,9},{9,8},{10,11... | collective-permute-start | bytes 294920 | tf_op jit(solution)/shard_map/ppermute | solution.py:338
  (14 other events, 87.8 us)

commit v3 on v2

--- a/solution.py
+++ b/solution.py
@@ -8,6 +8,7 @@
 
 ITERS = 3
 LANES = 6
+EARLY = (0, 1, 5)
 PAD = 32
 WIDE = 128
 BF = jnp.bfloat16
@@ -71,7 +72,6 @@
 
 class Sizes:
     def __init__(self, load, coupling, coarse_inv, devices):
-        self.planes = devices // 4
         self.subs, self.faces, self.loads, self.dof = load.shape
         self.total = self.subs * self.faces
         self.unknowns = self.faces * self.dof
@@ -80,6 +80,7 @@
         self.primal = coupling.shape[1]
         self.coarse = coarse_inv.shape[1]
         self.own_rows = coarse_inv.shape[0]
+        self.groups = self.coarse // WIDE
         self.blocks = (1 + LANES) * self.subs
         self.pick_width = -(-self.blocks * PAD // WIDE) * WIDE
         self.carry_rows = self.slots_per_lane * (self.loads + self.primal) + 8
@@ -138,7 +139,7 @@
             lower[pl.ds(start, count), :] = low
 
 
-def apply_in_kernel(z, vec, scalars, weights, stiff, copies, packed, image, shares):
+def apply_in_kernel(z, vec, scalars, weights, spot, stiff, copies, packed, image, small):
     for face in range(z.total):
         sub, side = face // z.faces, face % z.faces
         high, low = split_hi_lo(vec[face])
@@ -150,6 +151,12 @@
         rows = rows + lax.dot_general(packed[sub], weights[sub], NT, preferred_element_type=F32)
     rows = rows[0:n] + rows[n:]
     rows = rows + pltpu.roll(rows, WIDE - PAD, 1)
+    column = lax.broadcasted_iota(jnp.int32, (n, WIDE), 1)
+    rows = jnp.where(column % (2 * PAD) < PAD, rows, 0.0)
+    summed = jnp.dot(jnp.concatenate(split_hi_lo(rows), axis=0), spot[...], preferred_element_type=F32)
+    summed = summed[0:n] + summed[n:]
+    for group in range(z.groups):
+        small[group] = summed[:, group * WIDE:(group + 1) * WIDE]
     step = z.unknowns // PARTS
     kappa = jnp.zeros((n, z.dof), F32)
     for sub in range(z.subs):
@@ -167,11 +174,10 @@
             piece = total[:, side * z.dof:(side + 1) * z.dof]
             image[sub * z.faces + side] = piece
             kappa = kappa + piece * vec[sub * z.faces + side]
-    column = lax.broadcasted_iota(jnp.int32, (n, WIDE), 1)
-    share = jnp.where(column % (2 * PAD) < PAD, rows, 0.0)
+    tail = jnp.zeros((n, WIDE), F32)
     for place, value in enumerate([kappa] + scalars):
-        share = jnp.where(column == PAD + place, jnp.sum(value, axis=1, keepdims=True), share)
-    shares[0:n, :] = share
+        tail = jnp.where(column == place, jnp.sum(value, axis=1, keepdims=True), tail)
+    small[z.groups] = tail
 
 
 def fill_lanes(z, tab, field, lanes):
@@ -186,7 +192,7 @@
         held[lane * per:(lane + 1) * per] = arrived[lane][0:per]
 
 
-def load_kernel(z, tab, load, coupling, corner_row, corner_groups, stiff, image, shares, *rest):
+def load_kernel(z, tab, load, coupling, corner_row, spot, stiff, image, small, *rest):
     lanes, (near, weights, packed, sems) = rest[:LANES], rest[LANES:]
     step = z.unknowns // PARTS
     copies = [
@@ -216,16 +222,19 @@
         high, low = split_hi_lo(jnp.concatenate([coupling[sub], gap], axis=0))
         weights[sub, sub * 2 * PAD:sub * 2 * PAD + PAD, :] = high
         weights[sub, sub * 2 * PAD + PAD:sub * 2 * PAD + 2 * PAD, :] = low
-    apply_in_kernel(z, load, [], weights, near, copies, packed, image, shares)
-    shares[z.loads:, :] = corner_groups[...]
+    apply_in_kernel(z, load, [], weights, spot, near, copies, packed, image, small)
     for lane in range(LANES):
         for pos in range(per):
             lanes[lane][pos * z.loads:(pos + 1) * z.loads, :] = image[tab[lane * per + pos]]
-
-
-def precond_kernel(z, tab, weighted, residual, old_image, weights, stiff, *rest):
+    for lane in EARLY:
+        for group in range(z.groups + 1):
+            row = z.carry_rows + group * z.loads
+            lanes[lane][row:row + z.loads, :] = small[group]
+
+
+def precond_kernel(z, tab, weighted, residual, old_image, weights, spot, stiff, *rest):
     arrived, rest = rest[:LANES], rest[LANES:]
-    vec, image, shares = rest[:3]
+    vec, image, small = rest[:3]
     lanes, (packed, held) = rest[3:3 + LANES], rest[3 + LANES:]
     take_lanes(z, arrived, held)
     gamma = jnp.zeros((z.loads, z.dof), F32)
@@ -235,19 +244,13 @@
         vec[face] = value
         gamma = gamma + residual[face] * value
         eta = eta + old_image[face] * value
-    apply_in_kernel(z, vec, [gamma, eta], weights, stiff, None, packed, image, shares)
+    apply_in_kernel(z, vec, [gamma, eta], weights, spot, stiff, None, packed, image, small)
     fill_lanes(z, tab, image, lanes)
 
 
-def coarse_in_kernel(z, shares, spot, inv_high, inv_low, pick, picked):
+def coarse_in_kernel(z, summed, inv_high, inv_low, pick, picked):
     n = z.loads
-    rows = [stack[place, 0:n] for stack in shares for place in range(4)]
-    high, low = split_hi_lo(jnp.concatenate(rows, axis=1))
-    together = rows
-    while len(together) > 1:
-        together = [first + second for first, second in zip(together[0::2], together[1::2])]
-    primal = jnp.dot(jnp.concatenate([high, low], axis=0), spot[...], preferred_element_type=F32)
-    primal = primal[0:n] + primal[n:]
+    primal = jnp.concatenate([summed[group] for group in range(z.groups)], axis=1)
     high, low = split_hi_lo(primal)
     both = jnp.dot(jnp.concatenate([high, low], axis=0), inv_high[...], preferred_element_type=F32)
     lifted = (both[0:n] + both[n:]) + jnp.dot(high, inv_low[...], preferred_element_type=F32)
@@ -264,7 +267,7 @@
         third = pltpu.roll(lower, (WIDE + 2 * PAD - place) % WIDE, 1)
         mixed = jnp.where(column < PAD, first, jnp.where(column < 2 * PAD, second, third))
         picked[block] = jnp.where(column < 3 * PAD, mixed, 0.0).astype(BF)
-    return energy, together[0]
+    return energy
 
 
 def image_of_face(z, tab, face, image, held, picked, spread):
@@ -273,15 +276,14 @@
     return (image[face] - held[tab[z.slots + face]]) + lift
 
 
-def start_kernel(z, tab, image, spot, upper, lower, pick, spread, blocks, *rest):
-    shares, rest = rest[:z.planes], rest[z.planes:]
+def start_kernel(z, tab, image, summed, upper, lower, pick, spread, blocks, *rest):
     arrived, rest = rest[:LANES], rest[LANES:]
     residual, weighted = rest[:2]
     lanes, (held, picked) = rest[2:2 + LANES], rest[2 + LANES:]
     for lane in range(LANES):
         for pos in range(z.slots_per_lane):
             held[lane * z.slots_per_lane + pos] = arrived[lane][pos * z.loads:(pos + 1) * z.loads, :]
-    coarse_in_kernel(z, shares, spot, upper, lower, pick, picked)
+    coarse_in_kernel(z, summed, upper, lower, pick, picked)
     for face in range(z.total):
         value = image_of_face(z, tab, face, image, held, picked, spread)
         residual[face] = value
@@ -289,8 +291,7 @@
     fill_lanes(z, tab, weighted, lanes)
 
 
-def step_kernel(first, last, z, tab, image, spot, upper, lower, pick, spread, blocks, vec, old_residual, *rest):
-    shares, rest = rest[:z.planes], rest[z.planes:]
+def step_kernel(first, last, z, tab, image, summed, upper, lower, pick, spread, blocks, vec, old_residual, *rest):
     if not first:
         old_solution, old_direction, old_image, old_scalars = rest[:4]
         rest = rest[4:]
@@ -302,8 +303,9 @@
         lanes, rest = rest[4:4 + LANES], rest[4 + LANES:]
     held, picked = rest
     take_lanes(z, arrived, held)
-    energy, together = coarse_in_kernel(z, shares, spot, upper, lower, pick, picked)
-    kappa, gamma, eta = [together[:, PAD + place:PAD + place + 1] for place in range(3)]
+    energy = coarse_in_kernel(z, summed, upper, lower, pick, picked)
+    scalar = summed[z.groups]
+    kappa, gamma, eta = [scalar[:, place:place + 1] for place in range(3)]
     curvature = 2.0 * (kappa + energy)
     beta = None
     if not first:
@@ -338,18 +340,47 @@
     return [lax.ppermute(lane, "sub", pairs) for lane, pairs in zip(lanes, lane_pairs(devices))]
 
 
+def exchange_in_turn(lanes, devices):
+    pairs = lane_pairs(devices)
+    early = {lane: lax.ppermute(lanes[lane], "sub", pairs[lane]) for lane in EARLY}
+    late = [lane for lane in range(LANES) if lane not in EARLY]
+    near, waiting = lax.optimization_barrier(([early[0], early[1]], [lanes[lane] for lane in late]))
+    early[0], early[1] = near
+    early.update({lane: lax.ppermute(value, "sub", pairs[lane]) for lane, value in zip(late, waiting)})
+    return [early[lane] for lane in range(LANES)]
+
+
 def gathered(rows, devices):
     pair = jnp.concatenate([rows, lax.ppermute(rows, "sub", flipped(2, devices))])
     stacks = [(0, pair)] + [(mask, lax.ppermute(pair, "sub", flipped(mask, devices))) for mask in range(4, devices, 4)]
     return stacks + [(mask ^ 1, lax.ppermute(stack, "sub", flipped(1, devices))) for mask, stack in stacks]
 
 
-def gathered_shares(share, devices):
-    def other(value, mask):
-        return lax.ppermute(value, "sub", flipped(mask, devices))
-
-    plane = jnp.stack([share, other(share, 1), other(share, 2), other(share, 3)])
-    return [plane] + [other(plane, mask) for mask in range(4, devices, 4)]
+def first_exchange(lanes, small, devices):
+    pairs = lane_pairs(devices)
+    arrived = {lane: lax.ppermute(lanes[lane], "sub", pairs[lane]) for lane in EARLY}
+    across, crossed, beside = [
+        lax.optimization_barrier(arrived[lane])[-small.size // WIDE:].reshape(small.shape) for lane in EARLY
+    ]
+    plane = (small + beside) + (across + crossed)
+    late = [lane for lane in range(LANES) if lane not in EARLY]
+    plane, waiting = lax.optimization_barrier((plane, [lanes[lane] for lane in late]))
+    arrived.update({lane: lax.ppermute(value, "sub", pairs[lane]) for lane, value in zip(late, waiting)})
+    parts = [plane] + [lax.ppermute(plane, "sub", flipped(mask, devices)) for mask in range(4, devices, 4)]
+    while len(parts) > 1:
+        parts = [first + second for first, second in zip(parts[0::2], parts[1::2])]
+    return [arrived[lane] for lane in range(LANES)], parts[0]
+
+
+def over_devices(value, devices):
+    masks = []
+    mask = 4
+    while mask < devices:
+        masks.append(mask)
+        mask *= 2
+    for mask in masks + [1, 2]:
+        value = value + lax.ppermute(value, "sub", flipped(mask, devices))
+    return value
 
 
 def on_device(load, stiff_inv, face_blocks, coupling, coarse_inv, corners, partner):
@@ -364,7 +395,7 @@
     row = jnp.pad(numbers.reshape(1, -1), ((0, 0), (0, WIDE - z.subs * PAD)), constant_values=-1.0)
     corner_row = jnp.broadcast_to(row, (8, WIDE))
     apart = jnp.pad(numbers, ((0, 0), (0, WIDE // z.subs - PAD)), constant_values=-1.0)
-    corner_groups = jnp.broadcast_to(apart.reshape(1, WIDE), (8, WIDE))
+    spot = (apart.reshape(WIDE)[:, None] == jnp.arange(z.coarse, dtype=F32)[None, :]).astype(BF)
 
     field = shape(z.total, z.loads, z.dof)
     lane_field = [shape(z.slots_per_lane, z.loads, z.dof)] * LANES
@@ -374,19 +405,17 @@
     apply_cost = dict(flops=2 * z.total * z.dof * z.unknowns * z.loads, moved=stiff_inv.size * 2)
 
     load_faces = load.reshape(z.total, z.loads, z.dof)
-    image, shares, *lanes = call(
+    small_shape = shape(z.groups + 1, z.loads, WIDE)
+    image, small, *lanes = call(
         load_kernel, z,
-        [field, shape(z.loads + 8, WIDE)]
-        + [shape(z.carry_rows, z.dof)] * LANES
+        [field, small_shape]
+        + [shape(z.carry_rows + (z.groups + 1) * z.loads * (lane in EARLY), z.dof) for lane in range(LANES)]
         + [shape(z.subs, z.unknowns, z.unknowns, dtype=BF), shape(z.subs, 4 * PAD, z.unknowns, dtype=BF)],
-        (tab, load_faces, coupling, corner_row, corner_groups, stiff_inv), [SMEM] + [VMEM] * 4 + [HBM],
+        (tab, load_faces, coupling, corner_row, spot, stiff_inv), [SMEM] + [VMEM] * 4 + [HBM],
         apply_scratch + [pltpu.SemaphoreType.DMA((z.subs * PARTS,))], FIRST_LIMIT, "apply_load", **apply_cost,
     )
     near, weights = lanes[LANES:]
-    shares = gathered_shares(shares, devices)
-    arrived = exchange(lanes[:LANES], devices)
-    names = jnp.concatenate([stack[:, z.loads, :] for stack in shares]).reshape(-1)
-    spot = (names[:, None] == jnp.arange(z.coarse, dtype=F32)[None, :]).astype(BF)
+    arrived, summed = first_exchange(lanes[:LANES], small, devices)
     spread, pick = call(
         unpack_kernel, z,
         [shape(z.total, 8 * PAD, z.dof, dtype=BF), shape(z.coarse, z.pick_width, dtype=BF)],
@@ -401,10 +430,10 @@
         (lax.axis_index("sub").reshape(1).astype(jnp.int32), *stacks),
         [SMEM] + [VMEM] * len(masks), [], 8, "assemble_coarse",
     )
-    fixed = (spot, upper, lower, pick, spread, blocks)
+    fixed = (upper, lower, pick, spread, blocks)
     residual, weighted, *lanes = call(
         start_kernel, z, [field, field] + lane_field,
-        (tab, image, *fixed, *shares, *arrived), [SMEM] + [VMEM] * (7 + z.planes + LANES),
+        (tab, image, summed, *fixed, *arrived), [SMEM] + [VMEM] * (7 + LANES),
         [held, picked], 8, "first_residual",
     )
     state = None
@@ -412,15 +441,15 @@
         first, last = iteration == 0, iteration + 1 == ITERS
         arrived = exchange(lanes, devices)
         old_image = residual if first else state[2]
-        vec, image, shares, *lanes = call(
-            precond_kernel, z, [field, field, shape(z.loads, WIDE)] + lane_field,
-            (tab, weighted, residual, old_image, weights, near, *arrived),
-            [SMEM] + [VMEM] * (5 + LANES),
+        vec, image, small, *lanes = call(
+            precond_kernel, z, [field, field, small_shape] + lane_field,
+            (tab, weighted, residual, old_image, weights, spot, near, *arrived),
+            [SMEM] + [VMEM] * (6 + LANES),
             apply_scratch + [held], 8, "precond_apply", **apply_cost,
         )
-        shares = gathered_shares(shares, devices)
-        arrived = exchange(lanes, devices)
-        ins = [tab, image, *fixed, vec, residual, *shares] + ([] if first else list(state)) + list(arrived)
+        summed = over_devices(small, devices)
+        arrived = exchange_in_turn(lanes, devices)
+        ins = [tab, image, summed, *fixed, vec, residual] + ([] if first else list(state)) + list(arrived)
         outs = [field, field] + ([] if last else [field, field, shape(z.loads, WIDE), field] + lane_field)
         result = call(
             functools.partial(step_kernel, first, last), z, outs, ins, [SMEM] + [VMEM] * (len(ins) - 1),

time: 171 us -> 163 us (0.953)
  starting transfers between devices: 70 us -> 57.4 us
  waiting for transfers between devices: 65.4 us -> 72.4 us
  Pallas kernels: 30.1 us -> 28.2 us
    ppermute x24 -> x39, waiting for transfers between devices: 16.9 us -> 42.4 us  [the longest x12 23.8 us: over_devices(): value = value + lax.ppermute(value, 'sub', flipped(mask, devices))]
    ppermute x42 -> x18, waiting for transfers between devices: 40.4 us -> 18.8 us  [exchange(): lax.ppermute(lane, 'sub', pairs)]
    ppermute x42 -> x18, starting transfers between devices: 33.4 us -> 15.5 us  [exchange(): lax.ppermute(lane, 'sub', pairs)]
    ppermute x24 -> x39, starting transfers between devices: 26.8 us -> 34 us  [the longest x9 13.3 us: exchange_in_turn(): lax.ppermute(value, 'sub', pairs[lane])]
    ppermute x4, starting transfers between devices: 3.57 us -> 0.58 us  [gathered(): lax.ppermute(stack, 'sub', flipped(1, devices))]
    ppermute x3, waiting for transfers between devices: 8.09 us -> 10 us  [gathered(): lax.ppermute(pair, 'sub', flipped(mask, devices))]
    pallas_call x10, Pallas kernels: 30.1 us -> 28.2 us  [call(): pl.pallas_call(functools.partial(kernel, sizes), out_shape=outs, in_specs...]
  transfers between devices with their start and end apart: 74 -> 65, of which waited for: 26 -> 25; matrix products, arithmetic and copies ran while one was open for 0% -> 0% of each run, Pallas kernels for 1% -> 0%
where the time goes in v3:
time: 163 us
  waiting for transfers between devices  72.4 us (44%)
  starting transfers between devices  57.4 us (35%)
  Pallas kernels  28.2 us (17%)
  local copies, waits for them, and re-layouts  2.91 us (2%)
    pallas_call x10, Pallas kernels, call(): pl.pallas_call(functools.partial(kernel, sizes), out_shape=outs, in_specs...  28.2 us
    ppermute x12, waiting for transfers between devices, over_devices(): value = value + lax.ppermute(value, 'sub', flipped(mask, devices))  23.8 us
    ppermute x18, waiting for transfers between devices, exchange(): lax.ppermute(lane, 'sub', pairs)  18.8 us
    ppermute x18, starting transfers between devices, exchange(): lax.ppermute(lane, 'sub', pairs)  15.5 us
    ppermute x3, waiting for transfers between devices, first_exchange(): lax.ppermute(value, 'sub', pairs[lane])  14.5 us
    ppermute x9, starting transfers between devices, exchange_in_turn(): lax.ppermute(value, 'sub', pairs[lane])  13.3 us
    ppermute x3, waiting for transfers between devices, gathered(): lax.ppermute(pair, 'sub', flipped(mask, devices))  10 us
    ppermute x12, starting transfers between devices, over_devices(): value = value + lax.ppermute(value, 'sub', flipped(mask, devices))  9.9 us
  transfers between devices with their start and end apart: 65, of which 25 were waited for; matrix products, arithmetic and copies ran while one was open for 0% of the time, Pallas kernels for 0%

profile of v3, /device:TPU:0, one launch (start us, length us, event | category | flops | bytes accessed | tf_op | source)
XLA Modules:
  0.0 163.2 jit_solution(3311357695241322575)
XLA Ops:
  0.6 0.8 convert_element_type.14
  1.5 0.8 reshape.197
  2.9 1.0 copy-done.1
  3.9 0.9 copy-done.2
  4.8 7.7 %apply_load.1 = (f32[32,16,128]{2,1,0:T(8,128)S(1)}, f32[5,16,128]{2,1,0:T(8,128)S(1)}, f32[568,128]{1,0:T(8,128)S(1)}, f32[568,128]{1,0:T(8,128)S(1)}, f32[488,...) custom-call(s32[136]{0:T(256)S(1)} %pad_add_fusion.tab, ...), custom_call_target="tpu_custom_call" | custom-call | flops 268435456 | bytes 16777216 | tf_op jit(solution)/shard_map/apply_load/pallas_call | solution.py:90
  12.5 0.5 collective-permute-start
  13.0 2.6 %collective-permute-start.6 = (f32[32,512]{1,0:T(8,128)S(1)}, f32[32,512]{1,0:T(8,128)S(1)}, u32[]{:S(2)}, u32[]{:S(2)}) collective-permute-start(f32[32,512]{1,0:T(8,128)S(1)} %copy-done.3), channel_id=1, source_target_pairs={{0,2},{1,3},{2,0},{3,1},{4,6},{5,7},{6,4},{7,5},{8,10},{9,11},{10,... | collective-permute-start | bytes 196616 | tf_op jit(solution)/shard_map/ppermute | solution.py:354
  15.7 1.4 collective-permute-start.2
  17.2 1.2 collective-permute-done.6
  18.3 4.0 %collective-permute-start.9 = (f32[64,512]{1,0:T(8,128)S(1)}, f32[64,512]{1,0:T(8,128)S(1)}, u32[]{:S(2)}, u32[]{:S(2)}) collective-permute-start(f32[64,512]{1,0:T(8,128)S(1)} %constant_dynamic-update-slice_fusion.rest_0_), channel_id=1, source_target_pairs={{0,12},{1,13},{2,14},{3,15},{4,8},{5,9},{6,10},{7,11},{8,4},{9,5},... | collective-permute-start | bytes 393224 | tf_op jit(solution)/shard_map/ppermute | solution.py:355
  22.4 0.6 collective-permute-start.7
  23.0 3.8 %collective-permute-done.9.rest_3_ = f32[64,512]{1,0:T(8,128)S(1)} collective-permute-done((f32[64,512]{1,0:T(8,128)S(1)}, f32[64,512]{1,0:T(8,128)S(1)}, u32[]{:S(2)}, u32[]{:S(2)}) %collective-permute-start.9) | collective-permute-done | bytes 131104 | tf_op jit(solution)/shard_map/ppermute | solution.py:355
  26.8 6.2 %collective-permute-done.8.rest_2_ = f32[64,512]{1,0:T(8,128)S(1)} collective-permute-done((f32[64,512]{1,0:T(8,128)S(1)}, f32[64,512]{1,0:T(8,128)S(1)}, u32[]{:S(2)}, u32[]{:S(2)}) %collective-permute-start.8) | collective-permute-done | bytes 131104 | tf_op jit(solution)/shard_map/ppermute | solution.py:355
  33.1 0.5 collective-permute-start.12
  33.7 2.5 %collective-permute-start.5 = (f32[5,16,128]{2,1,0:T(8,128)S(1)}, f32[5,16,128]{2,1,0:T(8,128)S(1)}, u32[]{:S(2)}, u32[]{:S(2)}) collective-permute-start(f32[5,16,128]{2,1,0:T(8,128)S(1)} %add_add_fusion.1), channel_id=1, source_target_pairs={{0,12},{1,13},{2,14},{3,15},{4,8},{5,9},{6,10},{7,11},{8,4},{9,5},... | collective-permute-start | bytes 122888 | tf_op jit(solution)/shard_map/ppermute | solution.py:369
  36.2 1.9 %collective-permute-start.3 = (f32[5,16,128]{2,1,0:T(8,128)S(1)}, f32[5,16,128]{2,1,0:T(8,128)S(1)}, u32[]{:S(2)}, u32[]{:S(2)}) collective-permute-start(f32[5,16,128]{2,1,0:T(8,128)S(1)} %add_add_fusion.1), channel_id=1, source_target_pairs={{0,4},{1,5},{2,6},{3,7},{4,0},{5,1},{6,2},{7,3},{8,12},{9,13},{10,... | collective-permute-start | bytes 122888 | tf_op jit(solution)/shard_map/ppermute | solution.py:369
  38.6 1.2 collective-permute-done.5
  39.9 3.4 %collective-permute-start.16 = (f32[488,128]{1,0:T(8,128)S(1)}, f32[488,128]{1,0:T(8,128)S(1)}, u32[]{:S(2)}, u32[]{:S(2)}) collective-permute-start(f32[488,128]{1,0:T(8,128)S(1)} %get-tuple-element.109), channel_id=1, source_target_pairs={{0,13},{1,4},{2,15},{3,6},{4,1},{5,8},{6,3},{7,10},{8,5},{9,12},{1... | collective-permute-start | bytes 749576 | tf_op jit(solution)/shard_map/ppermute | solution.py:368
  43.5 14.5 %collective-permute-done.16.rest_4_ = f32[488,128]{1,0:T(8,128)S(1)} collective-permute-done((f32[488,128]{1,0:T(8,128)S(1)}, f32[488,128]{1,0:T(8,128)S(1)}, u32[]{:S(2)}, u32[]{:S(2)}) %collective-permute-start.16) | collective-permute-done | bytes 249888 | tf_op jit(solution)/shard_map/ppermute | solution.py:368
  57.9 1.0 unpack_coupling.1
  58.9 1.9 %first_residual.1 = (f32[32,16,128]{2,1,0:T(8,128)S(1)}, f32[32,16,128]{2,1,0:T(8,128)S(1)}, f32[12,16,128]{2,1,0:T(8,128)S(1)}, f32[12,16,128]{2,1,0:T(8,128)S(...) custom-call(s32[136]{0:T(256)S(1)} %pad_add_fusion.tab, ...), custom_call_target="tpu_custom_call" | custom-call | tf_op jit(solution)/shard_map/first_residual/pallas_call | solution.py:90
  61.2 1.8 %collective-permute-start.19 = (f32[12,16,128]{2,1,0:T(8,128)S(1)}, f32[12,16,128]{2,1,0:T(8,128)S(1)}, u32[]{:S(2)}, u32[]{:S(2)}) collective-permute-start(f32[12,16,128]{2,1,0:T(8,128)S(1)} %get-tuple-element.118), channel_id=1, source_target_pairs={{0,1},{1,0},{2,4},{3,5},{4,2},{5,3},{6,8},{7,9},{8,6},{9,7},{10,12... | collective-permute-start | bytes 294920 | tf_op jit(solution)/shard_map/ppermute | solution.py:340
  63.1 3.3 %collective-permute-start.21 = (f32[12,16,128]{2,1,0:T(8,128)S(1)}, f32[12,16,128]{2,1,0:T(8,128)S(1)}, u32[]{:S(2)}, u32[]{:S(2)}) collective-permute-start(f32[12,16,128]{2,1,0:T(8,128)S(1)} %get-tuple-element.120), channel_id=1, source_target_pairs={{0,13},{1,4},{2,15},{3,6},{4,1},{5,8},{6,3},{7,10},{8,5},{9,12},{1... | collective-permute-start | bytes 294920 | tf_op jit(solution)/shard_map/ppermute | solution.py:340
  66.4 2.4 %collective-permute-done.18.rest_1_ = f32[12,16,128]{2,1,0:T(8,128)S(1)} collective-permute-done((f32[12,16,128]{2,1,0:T(8,128)S(1)}, f32[12,16,128]{2,1,0:T(8,128)S(1)}, u32[]{:S(2)}, u32[]{:S(2)}) %collective-permute-start.18) | collective-permute-done | bytes 98336 | tf_op jit(solution)/shard_map/ppermute | solution.py:340
  68.8 3.7 %collective-permute-done.21.rest_4_ = f32[12,16,128]{2,1,0:T(8,128)S(1)} collective-permute-done((f32[12,16,128]{2,1,0:T(8,128)S(1)}, f32[12,16,128]{2,1,0:T(8,128)S(1)}, u32[]{:S(2)}, u32[]{:S(2)}) %collective-permute-start.21) | collective-permute-done | bytes 98336 | tf_op jit(solution)/shard_map/ppermute | solution.py:340
  72.5 3.7 %precond_apply.3 = (f32[32,16,128]{2,1,0:T(8,128)S(1)}, f32[32,16,128]{2,1,0:T(8,128)S(1)}, f32[5,16,128]{2,1,0:T(8,128)S(1)}, f32[12,16,128]{2,1,0:T(8,128)S(1)...) custom-call(s32[136]{0:T(256)S(1)} %pad_add_fusion.tab, ...), custom_call_target="tpu_custom_call" | custom-call | flops 268435456 | bytes 16777216 | tf_op jit(solution)/shard_map/precond_apply/pallas_call | solution.py:90
  76.8 3.6 %collective-permute-done.23 = f32[5,16,128]{2,1,0:T(8,128)S(1)} collective-permute-done((f32[5,16,128]{2,1,0:T(8,128)S(1)}, f32[5,16,128]{2,1,0:T(8,128)S(1)}, u32[]{:S(2)}, u32[]{:S(2)}) %collective-permute-start.23) | collective-permute-done | bytes 40992 | tf_op jit(solution)/shard_map/ppermute | solution.py:382
  80.4 1.6 collective-permute-start.24
  82.0 0.5 collective-permute-start.29
  82.6 3.9 %collective-permute-start.31 = (f32[12,16,128]{2,1,0:T(8,128)S(1)}, f32[12,16,128]{2,1,0:T(8,128)S(1)}, u32[]{:S(2)}, u32[]{:S(2)}) collective-permute-start(f32[12,16,128]{2,1,0:T(8,128)S(1)} %get-tuple-element.134), channel_id=1, source_target_pairs={{0,13},{1,4},{2,15},{3,6},{4,1},{5,8},{6,3},{7,10},{8,5},{9,12},{1... | collective-permute-start | bytes 294920 | tf_op jit(solution)/shard_map/ppermute | solution.py:349
  86.6 1.2 collective-permute-done.25
  87.8 0.6 collective-permute-start.26
  88.4 3.4 %collective-permute-done.26 = f32[5,16,128]{2,1,0:T(8,128)S(1)} collective-permute-done((f32[5,16,128]{2,1,0:T(8,128)S(1)}, f32[5,16,128]{2,1,0:T(8,128)S(1)}, u32[]{:S(2)}, u32[]{:S(2)}) %collective-permute-start.26) | collective-permute-done | bytes 40992 | tf_op jit(solution)/shard_map/ppermute | solution.py:382
  91.8 1.2 collective-permute-done.31.rest_4_
  93.0 2.0 %cg_step.3 = (f32[32,16,128]{2,1,0:T(8,128)S(1)}, f32[32,16,128]{2,1,0:T(8,128)S(1)}, f32[32,16,128]{2,1,0:T(8,128)S(1)}, f32[32,16,128]{2,1,0:T(8,128)S(1)}, f3...) custom-call(s32[136]{0:T(256)S(1)} %pad_add_fusion.tab, ...), custom_call_target="tpu_custom_call" | custom-call | tf_op jit(solution)/shard_map/cg_step/pallas_call | solution.py:90
  95.2 2.0 %collective-permute-start.35 = (f32[12,16,128]{2,1,0:T(8,128)S(1)}, f32[12,16,128]{2,1,0:T(8,128)S(1)}, u32[]{:S(2)}, u32[]{:S(2)}) collective-permute-start(f32[12,16,128]{2,1,0:T(8,128)S(1)} %get-tuple-element.141), channel_id=1, source_target_pairs={{0,1},{1,0},{2,4},{3,5},{4,2},{5,3},{6,8},{7,9},{8,6},{9,7},{10,12... | collective-permute-start | bytes 294920 | tf_op jit(solution)/shard_map/ppermute | solution.py:340
  97.2 2.8 %collective-permute-start.37 = (f32[12,16,128]{2,1,0:T(8,128)S(1)}, f32[12,16,128]{2,1,0:T(8,128)S(1)}, u32[]{:S(2)}, u32[]{:S(2)}) collective-permute-start(f32[12,16,128]{2,1,0:T(8,128)S(1)} %get-tuple-element.143), channel_id=1, source_target_pairs={{0,13},{1,4},{2,15},{3,6},{4,1},{5,8},{6,3},{7,10},{8,5},{9,12},{1... | collective-permute-start | bytes 294920 | tf_op jit(solution)/shard_map/ppermute | solution.py:340
  100.2 2.7 %collective-permute-done.34.rest_1_ = f32[12,16,128]{2,1,0:T(8,128)S(1)} collective-permute-done((f32[12,16,128]{2,1,0:T(8,128)S(1)}, f32[12,16,128]{2,1,0:T(8,128)S(1)}, u32[]{:S(2)}, u32[]{:S(2)}) %collective-permute-start.34) | collective-permute-done | bytes 98336 | tf_op jit(solution)/shard_map/ppermute | solution.py:340
  102.9 3.4 %collective-permute-done.37.rest_4_ = f32[12,16,128]{2,1,0:T(8,128)S(1)} collective-permute-done((f32[12,16,128]{2,1,0:T(8,128)S(1)}, f32[12,16,128]{2,1,0:T(8,128)S(1)}, u32[]{:S(2)}, u32[]{:S(2)}) %collective-permute-start.37) | collective-permute-done | bytes 98336 | tf_op jit(solution)/shard_map/ppermute | solution.py:340
  106.3 3.7 %precond_apply.4 = (f32[32,16,128]{2,1,0:T(8,128)S(1)}, f32[32,16,128]{2,1,0:T(8,128)S(1)}, f32[5,16,128]{2,1,0:T(8,128)S(1)}, f32[12,16,128]{2,1,0:T(8,128)S(1)...) custom-call(s32[136]{0:T(256)S(1)} %pad_add_fusion.tab, ...), custom_call_target="tpu_custom_call" | custom-call | flops 268435456 | bytes 16777216 | tf_op jit(solution)/shard_map/precond_apply/pallas_call | solution.py:90
  110.3 0.6 collective-permute-start.39
  110.9 3.4 %collective-permute-done.39 = f32[5,16,128]{2,1,0:T(8,128)S(1)} collective-permute-done((f32[5,16,128]{2,1,0:T(8,128)S(1)}, f32[5,16,128]{2,1,0:T(8,128)S(1)}, u32[]{:S(2)}, u32[]{:S(2)}) %collective-permute-start.39) | collective-permute-done | bytes 40992 | tf_op jit(solution)/shard_map/ppermute | solution.py:382
  114.3 2.0 %collective-permute-start.40 = (f32[5,16,128]{2,1,0:T(8,128)S(1)}, f32[5,16,128]{2,1,0:T(8,128)S(1)}, u32[]{:S(2)}, u32[]{:S(2)}) collective-permute-start(f32[5,16,128]{2,1,0:T(8,128)S(1)} %add.193), channel_id=1, source_target_pairs={{0,8},{1,9},{2,10},{3,11},{4,12},{5,13},{6,14},{7,15},{8,0},{9,1},... | collective-permute-start | bytes 122888 | tf_op jit(solution)/shard_map/ppermute | solution.py:382
  116.3 0.5 collective-permute-start.45
  116.9 3.5 %collective-permute-start.47 = (f32[12,16,128]{2,1,0:T(8,128)S(1)}, f32[12,16,128]{2,1,0:T(8,128)S(1)}, u32[]{:S(2)}, u32[]{:S(2)}) collective-permute-start(f32[12,16,128]{2,1,0:T(8,128)S(1)} %get-tuple-element.160), channel_id=1, source_target_pairs={{0,13},{1,4},{2,15},{3,6},{4,1},{5,8},{6,3},{7,10},{8,5},{9,12},{1... | collective-permute-start | bytes 294920 | tf_op jit(solution)/shard_map/ppermute | solution.py:349
  120.5 1.2 collective-permute-done.41
  121.7 0.8 collective-permute-start.42
  122.5 3.2 %collective-permute-done.42 = f32[5,16,128]{2,1,0:T(8,128)S(1)} collective-permute-done((f32[5,16,128]{2,1,0:T(8,128)S(1)}, f32[5,16,128]{2,1,0:T(8,128)S(1)}, u32[]{:S(2)}, u32[]{:S(2)}) %collective-permute-start.42) | collective-permute-done | bytes 40992 | tf_op jit(solution)/shard_map/ppermute | solution.py:382
  125.7 1.1 collective-permute-done.47.rest_8_
  126.9 2.1 %cg_step.4 = (f32[32,16,128]{2,1,0:T(8,128)S(1)}, f32[32,16,128]{2,1,0:T(8,128)S(1)}, f32[32,16,128]{2,1,0:T(8,128)S(1)}, f32[32,16,128]{2,1,0:T(8,128)S(1)}, f3...) custom-call(s32[136]{0:T(256)S(1)} %pad_add_fusion.tab, ...), custom_call_target="tpu_custom_call" | custom-call | tf_op jit(solution)/shard_map/cg_step/pallas_call | solution.py:90
  129.0 0.5 collective-permute-start.50
  129.6 1.6 collective-permute-start.51
  131.2 2.7 %collective-permute-start.53 = (f32[12,16,128]{2,1,0:T(8,128)S(1)}, f32[12,16,128]{2,1,0:T(8,128)S(1)}, u32[]{:S(2)}, u32[]{:S(2)}) collective-permute-start(f32[12,16,128]{2,1,0:T(8,128)S(1)} %get-tuple-element.169), channel_id=1, source_target_pairs={{0,13},{1,4},{2,15},{3,6},{4,1},{5,8},{6,3},{7,10},{8,5},{9,12},{1... | collective-permute-start | bytes 294920 | tf_op jit(solution)/shard_map/ppermute | solution.py:340
  134.2 2.7 %collective-permute-done.50.rest_1_ = f32[12,16,128]{2,1,0:T(8,128)S(1)} collective-permute-done((f32[12,16,128]{2,1,0:T(8,128)S(1)}, f32[12,16,128]{2,1,0:T(8,128)S(1)}, u32[]{:S(2)}, u32[]{:S(2)}) %collective-permute-start.50) | collective-permute-done | bytes 98336 | tf_op jit(solution)/shard_map/ppermute | solution.py:340
  136.9 3.4 %collective-permute-done.53.rest_4_ = f32[12,16,128]{2,1,0:T(8,128)S(1)} collective-permute-done((f32[12,16,128]{2,1,0:T(8,128)S(1)}, f32[12,16,128]{2,1,0:T(8,128)S(1)}, u32[]{:S(2)}, u32[]{:S(2)}) %collective-permute-start.53) | collective-permute-done | bytes 98336 | tf_op jit(solution)/shard_map/ppermute | solution.py:340
  140.3 3.7 %precond_apply.5 = (f32[32,16,128]{2,1,0:T(8,128)S(1)}, f32[32,16,128]{2,1,0:T(8,128)S(1)}, f32[5,16,128]{2,1,0:T(8,128)S(1)}, f32[12,16,128]{2,1,0:T(8,128)S(1)...) custom-call(s32[136]{0:T(256)S(1)} %pad_add_fusion.tab, ...), custom_call_target="tpu_custom_call" | custom-call | flops 268435456 | bytes 16777216 | tf_op jit(solution)/shard_map/precond_apply/pallas_call | solution.py:90
  144.2 1.4 collective-permute-start.55
  145.6 2.7 %collective-permute-done.55 = f32[5,16,128]{2,1,0:T(8,128)S(1)} collective-permute-done((f32[5,16,128]{2,1,0:T(8,128)S(1)}, f32[5,16,128]{2,1,0:T(8,128)S(1)}, u32[]{:S(2)}, u32[]{:S(2)}) %collective-permute-start.55) | collective-permute-done | bytes 40992 | tf_op jit(solution)/shard_map/ppermute | solution.py:382
  148.2 2.0 %collective-permute-start.56 = (f32[5,16,128]{2,1,0:T(8,128)S(1)}, f32[5,16,128]{2,1,0:T(8,128)S(1)}, u32[]{:S(2)}, u32[]{:S(2)}) collective-permute-start(f32[5,16,128]{2,1,0:T(8,128)S(1)} %add.197), channel_id=1, source_target_pairs={{0,8},{1,9},{2,10},{3,11},{4,12},{5,13},{6,14},{7,15},{8,0},{9,1},... | collective-permute-start | bytes 122888 | tf_op jit(solution)/shard_map/ppermute | solution.py:382
  150.3 0.5 collective-permute-start.61
  150.9 4.2 %collective-permute-start.63 = (f32[12,16,128]{2,1,0:T(8,128)S(1)}, f32[12,16,128]{2,1,0:T(8,128)S(1)}, u32[]{:S(2)}, u32[]{:S(2)}) collective-permute-start(f32[12,16,128]{2,1,0:T(8,128)S(1)} %get-tuple-element.186), channel_id=1, source_target_pairs={{0,13},{1,4},{2,15},{3,6},{4,1},{5,8},{6,3},{7,10},{8,5},{9,12},{1... | collective-permute-start | bytes 294920 | tf_op jit(solution)/shard_map/ppermute | solution.py:349
  155.2 1.2 collective-permute-done.57
  156.5 3.9 %collective-permute-done.58 = f32[5,16,128]{2,1,0:T(8,128)S(1)} collective-permute-done((f32[5,16,128]{2,1,0:T(8,128)S(1)}, f32[5,16,128]{2,1,0:T(8,128)S(1)}, u32[]{:S(2)}, u32[]{:S(2)}) %collective-permute-start.58) | collective-permute-done | bytes 40992 | tf_op jit(solution)/shard_map/ppermute | solution.py:382
  160.9 2.3 %cg_step.5 = (f32[32,16,128]{2,1,0:T(8,128)}, f32[32,16,128]{2,1,0:T(8,128)}) custom-call(s32[136]{0:T(256)S(1)} %pad_add_fusion.tab, f32[32,16,128]{2,1,0:T(8,128)S(1)} %get-tuple-element.171.image, f32[5,16,128]{2,1,0:T(8,128)S(1)} %add.200.summed, bf16[512,512]{1,0:T(8,128)(2,1)S(1)} %get-tuple-element.105.upper, ...), custom_call_target="tpu_custom_call" | custom-call | tf_op jit(solution)/shard_map/cg_step/pallas_call | solution.py:90
  (116 shorter events, 4.9 us)
Async XLA Ops:
  12.5 9.9 %collective-permute-start = (f32[568,128]{1,0:T(8,128)S(1)}, f32[568,128]{1,0:T(8,128)S(1)}, u32[]{:S(2)}, u32[]{:S(2)}) collective-permute-start(f32[568,128]{1,0:T(8,128)S(1)} %get-tuple-element.98), channel_id=1, source_target_pairs={{0,1},{1,0},{2,3},{3,2},{4,5},{5,4},{6,7},{7,6},{8,9},{9,8},{10,11... | collective-permute-start | bytes 872456 | tf_op jit(solution)/shard_map/ppermute | solution.py:361
  13.0 5.3 %collective-permute-start.6 = (f32[32,512]{1,0:T(8,128)S(1)}, f32[32,512]{1,0:T(8,128)S(1)}, u32[]{:S(2)}, u32[]{:S(2)}) collective-permute-start(f32[32,512]{1,0:T(8,128)S(1)} %copy-done.3), channel_id=1, source_target_pairs={{0,2},{1,3},{2,0},{3,1},{4,6},{5,7},{6,4},{7,5},{8,10},{9,11},{10,... | collective-permute-start | bytes 196616 | tf_op jit(solution)/shard_map/ppermute | solution.py:354
  15.6 17.9 %collective-permute-start.1 = (f32[568,128]{1,0:T(8,128)S(1)}, f32[568,128]{1,0:T(8,128)S(1)}, u32[]{:S(2)}, u32[]{:S(2)}) collective-permute-start(f32[568,128]{1,0:T(8,128)S(1)} %get-tuple-element.99), channel_id=1, source_target_pairs={{0,2},{1,3},{2,0},{3,1},{4,6},{5,7},{6,4},{7,5},{8,10},{9,11},{10,... | collective-permute-start | bytes 872456 | tf_op jit(solution)/shard_map/ppermute | solution.py:361
  15.7 17.9 %collective-permute-start.2 = (f32[568,128]{1,0:T(8,128)S(1)}, f32[568,128]{1,0:T(8,128)S(1)}, u32[]{:S(2)}, u32[]{:S(2)}) collective-permute-start(f32[568,128]{1,0:T(8,128)S(1)} %get-tuple-element.100), channel_id=1, source_target_pairs={{0,3},{1,2},{2,1},{3,0},{4,7},{5,6},{6,5},{7,4},{8,11},{9,10},{10,... | collective-permute-start | bytes 872456 | tf_op jit(solution)/shard_map/ppermute | solution.py:361
  18.3 8.5 %collective-permute-start.9 = (f32[64,512]{1,0:T(8,128)S(1)}, f32[64,512]{1,0:T(8,128)S(1)}, u32[]{:S(2)}, u32[]{:S(2)}) collective-permute-start(f32[64,512]{1,0:T(8,128)S(1)} %constant_dynamic-update-slice_fusion.rest_0_), channel_id=1, source_target_pairs={{0,12},{1,13},{2,14},{3,15},{4,8},{5,9},{6,10},{7,11},{8,4},{9,5},... | collective-permute-start | bytes 393224 | tf_op jit(solution)/shard_map/ppermute | solution.py:355
  22.4 10.7 %collective-permute-start.8 = (f32[64,512]{1,0:T(8,128)S(1)}, f32[64,512]{1,0:T(8,128)S(1)}, u32[]{:S(2)}, u32[]{:S(2)}) collective-permute-start(f32[64,512]{1,0:T(8,128)S(1)} %constant_dynamic-update-slice_fusion.rest_0_), channel_id=1, source_target_pairs={{0,8},{1,9},{2,10},{3,11},{4,12},{5,13},{6,14},{7,15},{8,0},{9,1},... | collective-permute-start | bytes 393224 | tf_op jit(solution)/shard_map/ppermute | solution.py:355
  22.4 10.7 %collective-permute-start.7 = (f32[64,512]{1,0:T(8,128)S(1)}, f32[64,512]{1,0:T(8,128)S(1)}, u32[]{:S(2)}, u32[]{:S(2)}) collective-permute-start(f32[64,512]{1,0:T(8,128)S(1)} %constant_dynamic-update-slice_fusion.rest_0_), channel_id=1, source_target_pairs={{0,4},{1,5},{2,6},{3,7},{4,0},{5,1},{6,2},{7,3},{8,12},{9,13},{10,... | collective-permute-start | bytes 393224 | tf_op jit(solution)/shard_map/ppermute | solution.py:355
  26.8 9.4 %collective-permute-start.10 = (f32[64,512]{1,0:T(8,128)S(1)}, f32[64,512]{1,0:T(8,128)S(1)}, u32[]{:S(2)}, u32[]{:S(2)}) collective-permute-start(f32[64,512]{1,0:T(8,128)S(1)} %constant_dynamic-update-slice_fusion.rest_0_), channel_id=1, source_target_pairs={{0,1},{1,0},{2,3},{3,2},{4,5},{5,4},{6,7},{7,6},{8,9},{9,8},{10,11... | collective-permute-start | bytes 393224 | tf_op jit(solution)/shard_map/ppermute | solution.py:356
  33.0 3.2 %collective-permute-start.13 = (f32[64,512]{1,0:T(8,128)S(1)}, f32[64,512]{1,0:T(8,128)S(1)}, u32[]{:S(2)}, u32[]{:S(2)}) collective-permute-start(f32[64,512]{1,0:T(8,128)S(1)} %collective-permute-done.9.rest_3_), channel_id=1, source_target_pairs={{0,1},{1,0},{2,3},{3,2},{4,5},{5,4},{6,7},{7,6},{8,9},{9,8},{10,11... | collective-permute-start | bytes 393224 | tf_op jit(solution)/shard_map/ppermute | solution.py:356
  33.1 5.1 %collective-permute-start.12 = (f32[64,512]{1,0:T(8,128)S(1)}, f32[64,512]{1,0:T(8,128)S(1)}, u32[]{:S(2)}, u32[]{:S(2)}) collective-permute-start(f32[64,512]{1,0:T(8,128)S(1)} %collective-permute-done.8.rest_2_), channel_id=1, source_target_pairs={{0,1},{1,0},{2,3},{3,2},{4,5},{5,4},{6,7},{7,6},{8,9},{9,8},{10,11... | collective-permute-start | bytes 393224 | tf_op jit(solution)/shard_map/ppermute | solution.py:356
  33.6 4.6 %collective-permute-start.11 = (f32[64,512]{1,0:T(8,128)S(1)}, f32[64,512]{1,0:T(8,128)S(1)}, u32[]{:S(2)}, u32[]{:S(2)}) collective-permute-start(f32[64,512]{1,0:T(8,128)S(1)} %collective-permute-done.7.rest_1_), channel_id=1, source_target_pairs={{0,1},{1,0},{2,3},{3,2},{4,5},{5,4},{6,7},{7,6},{8,9},{9,8},{10,11... | collective-permute-start | bytes 393224 | tf_op jit(solution)/shard_map/ppermute | solution.py:356
  33.7 6.2 %collective-permute-start.5 = (f32[5,16,128]{2,1,0:T(8,128)S(1)}, f32[5,16,128]{2,1,0:T(8,128)S(1)}, u32[]{:S(2)}, u32[]{:S(2)}) collective-permute-start(f32[5,16,128]{2,1,0:T(8,128)S(1)} %add_add_fusion.1), channel_id=1, source_target_pairs={{0,12},{1,13},{2,14},{3,15},{4,8},{5,9},{6,10},{7,11},{8,4},{9,5},... | collective-permute-start | bytes 122888 | tf_op jit(solution)/shard_map/ppermute | solution.py:369
  36.2 7.2 %collective-permute-start.4 = (f32[5,16,128]{2,1,0:T(8,128)S(1)}, f32[5,16,128]{2,1,0:T(8,128)S(1)}, u32[]{:S(2)}, u32[]{:S(2)}) collective-permute-start(f32[5,16,128]{2,1,0:T(8,128)S(1)} %add_add_fusion.1), channel_id=1, source_target_pairs={{0,8},{1,9},{2,10},{3,11},{4,12},{5,13},{6,14},{7,15},{8,0},{9,1},... | collective-permute-start | bytes 122888 | tf_op jit(solution)/shard_map/ppermute | solution.py:369
  36.2 7.2 %collective-permute-start.3 = (f32[5,16,128]{2,1,0:T(8,128)S(1)}, f32[5,16,128]{2,1,0:T(8,128)S(1)}, u32[]{:S(2)}, u32[]{:S(2)}) collective-permute-start(f32[5,16,128]{2,1,0:T(8,128)S(1)} %add_add_fusion.1), channel_id=1, source_target_pairs={{0,4},{1,5},{2,6},{3,7},{4,0},{5,1},{6,2},{7,3},{8,12},{9,13},{10,... | collective-permute-start | bytes 122888 | tf_op jit(solution)/shard_map/ppermute | solution.py:369
  38.1 5.3 %collective-permute-start.14 = (f32[488,128]{1,0:T(8,128)S(1)}, f32[488,128]{1,0:T(8,128)S(1)}, u32[]{:S(2)}, u32[]{:S(2)}) collective-permute-start(f32[488,128]{1,0:T(8,128)S(1)} %get-tuple-element.107), channel_id=1, source_target_pairs={{0,1},{1,0},{2,4},{3,5},{4,2},{5,3},{6,8},{7,9},{8,6},{9,7},{10,12... | collective-permute-start | bytes 749576 | tf_op jit(solution)/shard_map/ppermute | solution.py:368
  38.1 5.3 %collective-permute-start.15 = (f32[488,128]{1,0:T(8,128)S(1)}, f32[488,128]{1,0:T(8,128)S(1)}, u32[]{:S(2)}, u32[]{:S(2)}) collective-permute-start(f32[488,128]{1,0:T(8,128)S(1)} %get-tuple-element.108), channel_id=1, source_target_pairs={{0,1},{1,0},{2,5},{3,4},{4,3},{5,2},{6,9},{7,8},{8,7},{9,6},{10,13... | collective-permute-start | bytes 749576 | tf_op jit(solution)/shard_map/ppermute | solution.py:368
  39.9 18.0 %collective-permute-start.16 = (f32[488,128]{1,0:T(8,128)S(1)}, f32[488,128]{1,0:T(8,128)S(1)}, u32[]{:S(2)}, u32[]{:S(2)}) collective-permute-start(f32[488,128]{1,0:T(8,128)S(1)} %get-tuple-element.109), channel_id=1, source_target_pairs={{0,13},{1,4},{2,15},{3,6},{4,1},{5,8},{6,3},{7,10},{8,5},{9,12},{1... | collective-permute-start | bytes 749576 | tf_op jit(solution)/shard_map/ppermute | solution.py:368
  60.8 5.6 %collective-permute-start.17 = (f32[12,16,128]{2,1,0:T(8,128)S(1)}, f32[12,16,128]{2,1,0:T(8,128)S(1)}, u32[]{:S(2)}, u32[]{:S(2)}) collective-permute-start(f32[12,16,128]{2,1,0:T(8,128)S(1)} %get-tuple-element.116), channel_id=1, source_target_pairs={{0,2},{1,3},{2,0},{3,1},{4,6},{5,7},{6,4},{7,5},{8,10},{9,11},{10,... | collective-permute-start | bytes 294920 | tf_op jit(solution)/shard_map/ppermute | solution.py:340
  60.9 7.8 %collective-permute-start.18 = (f32[12,16,128]{2,1,0:T(8,128)S(1)}, f32[12,16,128]{2,1,0:T(8,128)S(1)}, u32[]{:S(2)}, u32[]{:S(2)}) collective-permute-start(f32[12,16,128]{2,1,0:T(8,128)S(1)} %get-tuple-element.117), channel_id=1, source_target_pairs={{0,3},{1,2},{2,1},{3,0},{4,7},{5,6},{6,5},{7,4},{8,11},{9,10},{10,... | collective-permute-start | bytes 294920 | tf_op jit(solution)/shard_map/ppermute | solution.py:340
  61.2 7.5 %collective-permute-start.19 = (f32[12,16,128]{2,1,0:T(8,128)S(1)}, f32[12,16,128]{2,1,0:T(8,128)S(1)}, u32[]{:S(2)}, u32[]{:S(2)}) collective-permute-start(f32[12,16,128]{2,1,0:T(8,128)S(1)} %get-tuple-element.118), channel_id=1, source_target_pairs={{0,1},{1,0},{2,4},{3,5},{4,2},{5,3},{6,8},{7,9},{8,6},{9,7},{10,12... | collective-permute-start | bytes 294920 | tf_op jit(solution)/shard_map/ppermute | solution.py:340
  63.0 5.7 %collective-permute-start.20 = (f32[12,16,128]{2,1,0:T(8,128)S(1)}, f32[12,16,128]{2,1,0:T(8,128)S(1)}, u32[]{:S(2)}, u32[]{:S(2)}) collective-permute-start(f32[12,16,128]{2,1,0:T(8,128)S(1)} %get-tuple-element.119), channel_id=1, source_target_pairs={{0,1},{1,0},{2,5},{3,4},{4,3},{5,2},{6,9},{7,8},{8,7},{9,6},{10,13... | collective-permute-start | bytes 294920 | tf_op jit(solution)/shard_map/ppermute | solution.py:340
  63.1 9.4 %collective-permute-start.21 = (f32[12,16,128]{2,1,0:T(8,128)S(1)}, f32[12,16,128]{2,1,0:T(8,128)S(1)}, u32[]{:S(2)}, u32[]{:S(2)}) collective-permute-start(f32[12,16,128]{2,1,0:T(8,128)S(1)} %get-tuple-element.120), channel_id=1, source_target_pairs={{0,13},{1,4},{2,15},{3,6},{4,1},{5,8},{6,3},{7,10},{8,5},{9,12},{1... | collective-permute-start | bytes 294920 | tf_op jit(solution)/shard_map/ppermute | solution.py:340
  66.4 6.1 %collective-permute-start.22 = (f32[12,16,128]{2,1,0:T(8,128)S(1)}, f32[12,16,128]{2,1,0:T(8,128)S(1)}, u32[]{:S(2)}, u32[]{:S(2)}) collective-permute-start(f32[12,16,128]{2,1,0:T(8,128)S(1)} %get-tuple-element.121), channel_id=1, source_target_pairs={{0,1},{1,0},{2,3},{3,2},{4,5},{5,4},{6,7},{7,6},{8,9},{9,8},{10,11... | collective-permute-start | bytes 294920 | tf_op jit(solution)/shard_map/ppermute | solution.py:340
  76.2 5.8 %collective-permute-start.27 = (f32[12,16,128]{2,1,0:T(8,128)S(1)}, f32[12,16,128]{2,1,0:T(8,128)S(1)}, u32[]{:S(2)}, u32[]{:S(2)}) collective-permute-start(f32[12,16,128]{2,1,0:T(8,128)S(1)} %get-tuple-element.125), channel_id=1, source_target_pairs={{0,2},{1,3},{2,0},{3,1},{4,6},{5,7},{6,4},{7,5},{8,10},{9,11},{10,... | collective-permute-start | bytes 294920 | tf_op jit(solution)/shard_map/ppermute | solution.py:345
  76.2 5.8 %collective-permute-start.28 = (f32[12,16,128]{2,1,0:T(8,128)S(1)}, f32[12,16,128]{2,1,0:T(8,128)S(1)}, u32[]{:S(2)}, u32[]{:S(2)}) collective-permute-start(f32[12,16,128]{2,1,0:T(8,128)S(1)} %get-tuple-element.126), channel_id=1, source_target_pairs={{0,3},{1,2},{2,1},{3,0},{4,7},{5,6},{6,5},{7,4},{8,11},{9,10},{10,... | collective-permute-start | bytes 294920 | tf_op jit(solution)/shard_map/ppermute | solution.py:345
  76.3 4.1 %collective-permute-start.23 = (f32[5,16,128]{2,1,0:T(8,128)S(1)}, f32[5,16,128]{2,1,0:T(8,128)S(1)}, u32[]{:S(2)}, u32[]{:S(2)}) collective-permute-start(f32[5,16,128]{2,1,0:T(8,128)S(1)} %get-tuple-element.123), channel_id=1, source_target_pairs={{0,4},{1,5},{2,6},{3,7},{4,0},{5,1},{6,2},{7,3},{8,12},{9,13},{10,... | collective-permute-start | bytes 122888 | tf_op jit(solution)/shard_map/ppermute | solution.py:382
  80.4 6.1 %collective-permute-start.24 = (f32[5,16,128]{2,1,0:T(8,128)S(1)}, f32[5,16,128]{2,1,0:T(8,128)S(1)}, u32[]{:S(2)}, u32[]{:S(2)}) collective-permute-start(f32[5,16,128]{2,1,0:T(8,128)S(1)} %add.189), channel_id=1, source_target_pairs={{0,8},{1,9},{2,10},{3,11},{4,12},{5,13},{6,14},{7,15},{8,0},{9,1},... | collective-permute-start | bytes 122888 | tf_op jit(solution)/shard_map/ppermute | solution.py:382
  82.0 9.8 %collective-permute-start.32 = (f32[12,16,128]{2,1,0:T(8,128)S(1)}, f32[12,16,128]{2,1,0:T(8,128)S(1)}, u32[]{:S(2)}, u32[]{:S(2)}) collective-permute-start(f32[12,16,128]{2,1,0:T(8,128)S(1)} %get-tuple-element.135), channel_id=1, source_target_pairs={{0,1},{1,0},{2,3},{3,2},{4,5},{5,4},{6,7},{7,6},{8,9},{9,8},{10,11... | collective-permute-start | bytes 294920 | tf_op jit(solution)/shard_map/ppermute | solution.py:345
  82.0 9.8 %collective-permute-start.29 = (f32[12,16,128]{2,1,0:T(8,128)S(1)}, f32[12,16,128]{2,1,0:T(8,128)S(1)}, u32[]{:S(2)}, u32[]{:S(2)}) collective-permute-start(f32[12,16,128]{2,1,0:T(8,128)S(1)} %get-tuple-element.132), channel_id=1, source_target_pairs={{0,1},{1,0},{2,4},{3,5},{4,2},{5,3},{6,8},{7,9},{8,6},{9,7},{10,12... | collective-permute-start | bytes 294920 | tf_op jit(solution)/shard_map/ppermute | solution.py:349
  82.5 9.3 %collective-permute-start.30 = (f32[12,16,128]{2,1,0:T(8,128)S(1)}, f32[12,16,128]{2,1,0:T(8,128)S(1)}, u32[]{:S(2)}, u32[]{:S(2)}) collective-permute-start(f32[12,16,128]{2,1,0:T(8,128)S(1)} %get-tuple-element.133), channel_id=1, source_target_pairs={{0,1},{1,0},{2,5},{3,4},{4,3},{5,2},{6,9},{7,8},{8,7},{9,6},{10,13... | collective-permute-start | bytes 294920 | tf_op jit(solution)/shard_map/ppermute | solution.py:349
  82.6 10.4 %collective-permute-start.31 = (f32[12,16,128]{2,1,0:T(8,128)S(1)}, f32[12,16,128]{2,1,0:T(8,128)S(1)}, u32[]{:S(2)}, u32[]{:S(2)}) collective-permute-start(f32[12,16,128]{2,1,0:T(8,128)S(1)} %get-tuple-element.134), channel_id=1, source_target_pairs={{0,13},{1,4},{2,15},{3,6},{4,1},{5,8},{6,3},{7,10},{8,5},{9,12},{1... | collective-permute-start | bytes 294920 | tf_op jit(solution)/shard_map/ppermute | solution.py:349
  87.8 4.0 %collective-permute-start.26 = (f32[5,16,128]{2,1,0:T(8,128)S(1)}, f32[5,16,128]{2,1,0:T(8,128)S(1)}, u32[]{:S(2)}, u32[]{:S(2)}) collective-permute-start(f32[5,16,128]{2,1,0:T(8,128)S(1)} %add.191), channel_id=1, source_target_pairs={{0,2},{1,3},{2,0},{3,1},{4,6},{5,7},{6,4},{7,5},{8,10},{9,11},{10,... | collective-permute-start | bytes 122888 | tf_op jit(solution)/shard_map/ppermute | solution.py:382
  95.0 5.2 %collective-permute-start.33 = (f32[12,16,128]{2,1,0:T(8,128)S(1)}, f32[12,16,128]{2,1,0:T(8,128)S(1)}, u32[]{:S(2)}, u32[]{:S(2)}) collective-permute-start(f32[12,16,128]{2,1,0:T(8,128)S(1)} %get-tuple-element.139), channel_id=1, source_target_pairs={{0,2},{1,3},{2,0},{3,1},{4,6},{5,7},{6,4},{7,5},{8,10},{9,11},{10,... | collective-permute-start | bytes 294920 | tf_op jit(solution)/shard_map/ppermute | solution.py:340
  95.1 7.8 %collective-permute-start.34 = (f32[12,16,128]{2,1,0:T(8,128)S(1)}, f32[12,16,128]{2,1,0:T(8,128)S(1)}, u32[]{:S(2)}, u32[]{:S(2)}) collective-permute-start(f32[12,16,128]{2,1,0:T(8,128)S(1)} %get-tuple-element.140), channel_id=1, source_target_pairs={{0,3},{1,2},{2,1},{3,0},{4,7},{5,6},{6,5},{7,4},{8,11},{9,10},{10,... | collective-permute-start | bytes 294920 | tf_op jit(solution)/shard_map/ppermute | solution.py:340
  95.2 7.8 %collective-permute-start.35 = (f32[12,16,128]{2,1,0:T(8,128)S(1)}, f32[12,16,128]{2,1,0:T(8,128)S(1)}, u32[]{:S(2)}, u32[]{:S(2)}) collective-permute-start(f32[12,16,128]{2,1,0:T(8,128)S(1)} %get-tuple-element.141), channel_id=1, source_target_pairs={{0,1},{1,0},{2,4},{3,5},{4,2},{5,3},{6,8},{7,9},{8,6},{9,7},{10,12... | collective-permute-start | bytes 294920 | tf_op jit(solution)/shard_map/ppermute | solution.py:340
  97.2 5.7 %collective-permute-start.36 = (f32[12,16,128]{2,1,0:T(8,128)S(1)}, f32[12,16,128]{2,1,0:T(8,128)S(1)}, u32[]{:S(2)}, u32[]{:S(2)}) collective-permute-start(f32[12,16,128]{2,1,0:T(8,128)S(1)} %get-tuple-element.142), channel_id=1, source_target_pairs={{0,1},{1,0},{2,5},{3,4},{4,3},{5,2},{6,9},{7,8},{8,7},{9,6},{10,13... | collective-permute-start | bytes 294920 | tf_op jit(solution)/shard_map/ppermute | solution.py:340
  97.2 9.1 %collective-permute-start.37 = (f32[12,16,128]{2,1,0:T(8,128)S(1)}, f32[12,16,128]{2,1,0:T(8,128)S(1)}, u32[]{:S(2)}, u32[]{:S(2)}) collective-permute-start(f32[12,16,128]{2,1,0:T(8,128)S(1)} %get-tuple-element.143), channel_id=1, source_target_pairs={{0,13},{1,4},{2,15},{3,6},{4,1},{5,8},{6,3},{7,10},{8,5},{9,12},{1... | collective-permute-start | bytes 294920 | tf_op jit(solution)/shard_map/ppermute | solution.py:340
  100.2 6.1 %collective-permute-start.38 = (f32[12,16,128]{2,1,0:T(8,128)S(1)}, f32[12,16,128]{2,1,0:T(8,128)S(1)}, u32[]{:S(2)}, u32[]{:S(2)}) collective-permute-start(f32[12,16,128]{2,1,0:T(8,128)S(1)} %get-tuple-element.144), channel_id=1, source_target_pairs={{0,1},{1,0},{2,3},{3,2},{4,5},{5,4},{6,7},{7,6},{8,9},{9,8},{10,11... | collective-permute-start | bytes 294920 | tf_op jit(solution)/shard_map/ppermute | solution.py:340
  110.0 6.3 %collective-permute-start.43 = (f32[12,16,128]{2,1,0:T(8,128)S(1)}, f32[12,16,128]{2,1,0:T(8,128)S(1)}, u32[]{:S(2)}, u32[]{:S(2)}) collective-permute-start(f32[12,16,128]{2,1,0:T(8,128)S(1)} %get-tuple-element.151), channel_id=1, source_target_pairs={{0,2},{1,3},{2,0},{3,1},{4,6},{5,7},{6,4},{7,5},{8,10},{9,11},{10,... | collective-permute-start | bytes 294920 | tf_op jit(solution)/shard_map/ppermute | solution.py:345
  110.1 6.2 %collective-permute-start.44 = (f32[12,16,128]{2,1,0:T(8,128)S(1)}, f32[12,16,128]{2,1,0:T(8,128)S(1)}, u32[]{:S(2)}, u32[]{:S(2)}) collective-permute-start(f32[12,16,128]{2,1,0:T(8,128)S(1)} %get-tuple-element.152), channel_id=1, source_target_pairs={{0,3},{1,2},{2,1},{3,0},{4,7},{5,6},{6,5},{7,4},{8,11},{9,10},{10,... | collective-permute-start | bytes 294920 | tf_op jit(solution)/shard_map/ppermute | solution.py:345
  110.3 4.0 %collective-permute-start.39 = (f32[5,16,128]{2,1,0:T(8,128)S(1)}, f32[5,16,128]{2,1,0:T(8,128)S(1)}, u32[]{:S(2)}, u32[]{:S(2)}) collective-permute-start(f32[5,16,128]{2,1,0:T(8,128)S(1)} %get-tuple-element.146), channel_id=1, source_target_pairs={{0,4},{1,5},{2,6},{3,7},{4,0},{5,1},{6,2},{7,3},{8,12},{9,13},{10,... | collective-permute-start | bytes 122888 | tf_op jit(solution)/shard_map/ppermute | solution.py:382
  114.3 6.1 %collective-permute-start.40 = (f32[5,16,128]{2,1,0:T(8,128)S(1)}, f32[5,16,128]{2,1,0:T(8,128)S(1)}, u32[]{:S(2)}, u32[]{:S(2)}) collective-permute-start(f32[5,16,128]{2,1,0:T(8,128)S(1)} %add.193), channel_id=1, source_target_pairs={{0,8},{1,9},{2,10},{3,11},{4,12},{5,13},{6,14},{7,15},{8,0},{9,1},... | collective-permute-start | bytes 122888 | tf_op jit(solution)/shard_map/ppermute | solution.py:382
  116.3 9.4 %collective-permute-start.48 = (f32[12,16,128]{2,1,0:T(8,128)S(1)}, f32[12,16,128]{2,1,0:T(8,128)S(1)}, u32[]{:S(2)}, u32[]{:S(2)}) collective-permute-start(f32[12,16,128]{2,1,0:T(8,128)S(1)} %get-tuple-element.161), channel_id=1, source_target_pairs={{0,1},{1,0},{2,3},{3,2},{4,5},{5,4},{6,7},{7,6},{8,9},{9,8},{10,11... | collective-permute-start | bytes 294920 | tf_op jit(solution)/shard_map/ppermute | solution.py:345
  116.3 9.4 %collective-permute-start.45 = (f32[12,16,128]{2,1,0:T(8,128)S(1)}, f32[12,16,128]{2,1,0:T(8,128)S(1)}, u32[]{:S(2)}, u32[]{:S(2)}) collective-permute-start(f32[12,16,128]{2,1,0:T(8,128)S(1)} %get-tuple-element.158), channel_id=1, source_target_pairs={{0,1},{1,0},{2,4},{3,5},{4,2},{5,3},{6,8},{7,9},{8,6},{9,7},{10,12... | collective-permute-start | bytes 294920 | tf_op jit(solution)/shard_map/ppermute | solution.py:349
  116.8 8.9 %collective-permute-start.46 = (f32[12,16,128]{2,1,0:T(8,128)S(1)}, f32[12,16,128]{2,1,0:T(8,128)S(1)}, u32[]{:S(2)}, u32[]{:S(2)}) collective-permute-start(f32[12,16,128]{2,1,0:T(8,128)S(1)} %get-tuple-element.159), channel_id=1, source_target_pairs={{0,1},{1,0},{2,5},{3,4},{4,3},{5,2},{6,9},{7,8},{8,7},{9,6},{10,13... | collective-permute-start | bytes 294920 | tf_op jit(solution)/shard_map/ppermute | solution.py:349
  116.9 10.0 %collective-permute-start.47 = (f32[12,16,128]{2,1,0:T(8,128)S(1)}, f32[12,16,128]{2,1,0:T(8,128)S(1)}, u32[]{:S(2)}, u32[]{:S(2)}) collective-permute-start(f32[12,16,128]{2,1,0:T(8,128)S(1)} %get-tuple-element.160), channel_id=1, source_target_pairs={{0,13},{1,4},{2,15},{3,6},{4,1},{5,8},{6,3},{7,10},{8,5},{9,12},{1... | collective-permute-start | bytes 294920 | tf_op jit(solution)/shard_map/ppermute | solution.py:349
  120.4 1.3 collective-permute-start.41
  121.7 4.0 %collective-permute-start.42 = (f32[5,16,128]{2,1,0:T(8,128)S(1)}, f32[5,16,128]{2,1,0:T(8,128)S(1)}, u32[]{:S(2)}, u32[]{:S(2)}) collective-permute-start(f32[5,16,128]{2,1,0:T(8,128)S(1)} %add.195), channel_id=1, source_target_pairs={{0,2},{1,3},{2,0},{3,1},{4,6},{5,7},{6,4},{7,5},{8,10},{9,11},{10,... | collective-permute-start | bytes 122888 | tf_op jit(solution)/shard_map/ppermute | solution.py:382
  129.0 5.2 %collective-permute-start.49 = (f32[12,16,128]{2,1,0:T(8,128)S(1)}, f32[12,16,128]{2,1,0:T(8,128)S(1)}, u32[]{:S(2)}, u32[]{:S(2)}) collective-permute-start(f32[12,16,128]{2,1,0:T(8,128)S(1)} %get-tuple-element.165), channel_id=1, source_target_pairs={{0,2},{1,3},{2,0},{3,1},{4,6},{5,7},{6,4},{7,5},{8,10},{9,11},{10,... | collective-permute-start | bytes 294920 | tf_op jit(solution)/shard_map/ppermute | solution.py:340
  129.0 7.8 %collective-permute-start.50 = (f32[12,16,128]{2,1,0:T(8,128)S(1)}, f32[12,16,128]{2,1,0:T(8,128)S(1)}, u32[]{:S(2)}, u32[]{:S(2)}) collective-permute-start(f32[12,16,128]{2,1,0:T(8,128)S(1)} %get-tuple-element.166), channel_id=1, source_target_pairs={{0,3},{1,2},{2,1},{3,0},{4,7},{5,6},{6,5},{7,4},{8,11},{9,10},{10,... | collective-permute-start | bytes 294920 | tf_op jit(solution)/shard_map/ppermute | solution.py:340
  129.6 7.3 %collective-permute-start.51 = (f32[12,16,128]{2,1,0:T(8,128)S(1)}, f32[12,16,128]{2,1,0:T(8,128)S(1)}, u32[]{:S(2)}, u32[]{:S(2)}) collective-permute-start(f32[12,16,128]{2,1,0:T(8,128)S(1)} %get-tuple-element.167), channel_id=1, source_target_pairs={{0,1},{1,0},{2,4},{3,5},{4,2},{5,3},{6,8},{7,9},{8,6},{9,7},{10,12... | collective-permute-start | bytes 294920 | tf_op jit(solution)/shard_map/ppermute | solution.py:340
  131.2 5.7 %collective-permute-start.52 = (f32[12,16,128]{2,1,0:T(8,128)S(1)}, f32[12,16,128]{2,1,0:T(8,128)S(1)}, u32[]{:S(2)}, u32[]{:S(2)}) collective-permute-start(f32[12,16,128]{2,1,0:T(8,128)S(1)} %get-tuple-element.168), channel_id=1, source_target_pairs={{0,1},{1,0},{2,5},{3,4},{4,3},{5,2},{6,9},{7,8},{8,7},{9,6},{10,13... | collective-permute-start | bytes 294920 | tf_op jit(solution)/shard_map/ppermute | solution.py:340
  131.2 9.2 %collective-permute-start.53 = (f32[12,16,128]{2,1,0:T(8,128)S(1)}, f32[12,16,128]{2,1,0:T(8,128)S(1)}, u32[]{:S(2)}, u32[]{:S(2)}) collective-permute-start(f32[12,16,128]{2,1,0:T(8,128)S(1)} %get-tuple-element.169), channel_id=1, source_target_pairs={{0,13},{1,4},{2,15},{3,6},{4,1},{5,8},{6,3},{7,10},{8,5},{9,12},{1... | collective-permute-start | bytes 294920 | tf_op jit(solution)/shard_map/ppermute | solution.py:340
  134.2 6.1 %collective-permute-start.54 = (f32[12,16,128]{2,1,0:T(8,128)S(1)}, f32[12,16,128]{2,1,0:T(8,128)S(1)}, u32[]{:S(2)}, u32[]{:S(2)}) collective-permute-start(f32[12,16,128]{2,1,0:T(8,128)S(1)} %get-tuple-element.170), channel_id=1, source_target_pairs={{0,1},{1,0},{2,3},{3,2},{4,5},{5,4},{6,7},{7,6},{8,9},{9,8},{10,11... | collective-permute-start | bytes 294920 | tf_op jit(solution)/shard_map/ppermute | solution.py:340
  144.0 6.3 %collective-permute-start.59 = (f32[12,16,128]{2,1,0:T(8,128)S(1)}, f32[12,16,128]{2,1,0:T(8,128)S(1)}, u32[]{:S(2)}, u32[]{:S(2)}) collective-permute-start(f32[12,16,128]{2,1,0:T(8,128)S(1)} %get-tuple-element.177), channel_id=1, source_target_pairs={{0,2},{1,3},{2,0},{3,1},{4,6},{5,7},{6,4},{7,5},{8,10},{9,11},{10,... | collective-permute-start | bytes 294920 | tf_op jit(solution)/shard_map/ppermute | solution.py:345
  144.1 6.2 %collective-permute-start.60 = (f32[12,16,128]{2,1,0:T(8,128)S(1)}, f32[12,16,128]{2,1,0:T(8,128)S(1)}, u32[]{:S(2)}, u32[]{:S(2)}) collective-permute-start(f32[12,16,128]{2,1,0:T(8,128)S(1)} %get-tuple-element.178), channel_id=1, source_target_pairs={{0,3},{1,2},{2,1},{3,0},{4,7},{5,6},{6,5},{7,4},{8,11},{9,10},{10,... | collective-permute-start | bytes 294920 | tf_op jit(solution)/shard_map/ppermute | solution.py:345
  144.2 4.1 %collective-permute-start.55 = (f32[5,16,128]{2,1,0:T(8,128)S(1)}, f32[5,16,128]{2,1,0:T(8,128)S(1)}, u32[]{:S(2)}, u32[]{:S(2)}) collective-permute-start(f32[5,16,128]{2,1,0:T(8,128)S(1)} %get-tuple-element.172), channel_id=1, source_target_pairs={{0,4},{1,5},{2,6},{3,7},{4,0},{5,1},{6,2},{7,3},{8,12},{9,13},{10,... | collective-permute-start | bytes 122888 | tf_op jit(solution)/shard_map/ppermute | solution.py:382
  148.2 6.8 %collective-permute-start.56 = (f32[5,16,128]{2,1,0:T(8,128)S(1)}, f32[5,16,128]{2,1,0:T(8,128)S(1)}, u32[]{:S(2)}, u32[]{:S(2)}) collective-permute-start(f32[5,16,128]{2,1,0:T(8,128)S(1)} %add.197), channel_id=1, source_target_pairs={{0,8},{1,9},{2,10},{3,11},{4,12},{5,13},{6,14},{7,15},{8,0},{9,1},... | collective-permute-start | bytes 122888 | tf_op jit(solution)/shard_map/ppermute | solution.py:382
  150.3 10.1 %collective-permute-start.64 = (f32[12,16,128]{2,1,0:T(8,128)S(1)}, f32[12,16,128]{2,1,0:T(8,128)S(1)}, u32[]{:S(2)}, u32[]{:S(2)}) collective-permute-start(f32[12,16,128]{2,1,0:T(8,128)S(1)} %get-tuple-element.187), channel_id=1, source_target_pairs={{0,1},{1,0},{2,3},{3,2},{4,5},{5,4},{6,7},{7,6},{8,9},{9,8},{10,11... | collective-permute-start | bytes 294920 | tf_op jit(solution)/shard_map/ppermute | solution.py:345
  150.3 10.1 %collective-permute-start.61 = (f32[12,16,128]{2,1,0:T(8,128)S(1)}, f32[12,16,128]{2,1,0:T(8,128)S(1)}, u32[]{:S(2)}, u32[]{:S(2)}) collective-permute-start(f32[12,16,128]{2,1,0:T(8,128)S(1)} %get-tuple-element.184), channel_id=1, source_target_pairs={{0,1},{1,0},{2,4},{3,5},{4,2},{5,3},{6,8},{7,9},{8,6},{9,7},{10,12... | collective-permute-start | bytes 294920 | tf_op jit(solution)/shard_map/ppermute | solution.py:349
  150.8 9.6 %collective-permute-start.62 = (f32[12,16,128]{2,1,0:T(8,128)S(1)}, f32[12,16,128]{2,1,0:T(8,128)S(1)}, u32[]{:S(2)}, u32[]{:S(2)}) collective-permute-start(f32[12,16,128]{2,1,0:T(8,128)S(1)} %get-tuple-element.185), channel_id=1, source_target_pairs={{0,1},{1,0},{2,5},{3,4},{4,3},{5,2},{6,9},{7,8},{8,7},{9,6},{10,13... | collective-permute-start | bytes 294920 | tf_op jit(solution)/shard_map/ppermute | solution.py:349
  150.9 10.0 %collective-permute-start.63 = (f32[12,16,128]{2,1,0:T(8,128)S(1)}, f32[12,16,128]{2,1,0:T(8,128)S(1)}, u32[]{:S(2)}, u32[]{:S(2)}) collective-permute-start(f32[12,16,128]{2,1,0:T(8,128)S(1)} %get-tuple-element.186), channel_id=1, source_target_pairs={{0,13},{1,4},{2,15},{3,6},{4,1},{5,8},{6,3},{7,10},{8,5},{9,12},{1... | collective-permute-start | bytes 294920 | tf_op jit(solution)/shard_map/ppermute | solution.py:349
  155.1 1.3 collective-permute-start.57
  156.4 4.0 %collective-permute-start.58 = (f32[5,16,128]{2,1,0:T(8,128)S(1)}, f32[5,16,128]{2,1,0:T(8,128)S(1)}, u32[]{:S(2)}, u32[]{:S(2)}) collective-permute-start(f32[5,16,128]{2,1,0:T(8,128)S(1)} %add.199), channel_id=1, source_target_pairs={{0,2},{1,3},{2,0},{3,1},{4,6},{5,7},{6,4},{7,5},{8,10},{9,11},{10,... | collective-permute-start | bytes 122888 | tf_op jit(solution)/shard_map/ppermute | solution.py:382
  (5 other events, 69.7 us)

commit v4 on v3

--- a/solution.py
+++ b/solution.py
@@ -18,6 +18,7 @@
 HBM = pl.BlockSpec(memory_space=pltpu.HBM)
 PARTS = 8
 FIRST_LIMIT = 31
+FIRST_FLOPS = 2 * 10**10
 NT = (((1,), (1,)), ((), ()))
 
 
@@ -352,24 +353,21 @@
 
 def gathered(rows, devices):
     pair = jnp.concatenate([rows, lax.ppermute(rows, "sub", flipped(2, devices))])
-    stacks = [(0, pair)] + [(mask, lax.ppermute(pair, "sub", flipped(mask, devices))) for mask in range(4, devices, 4)]
-    return stacks + [(mask ^ 1, lax.ppermute(stack, "sub", flipped(1, devices))) for mask, stack in stacks]
-
-
-def first_exchange(lanes, small, devices):
-    pairs = lane_pairs(devices)
-    arrived = {lane: lax.ppermute(lanes[lane], "sub", pairs[lane]) for lane in EARLY}
+    return [(0, pair)] + [(mask, lax.ppermute(pair, "sub", flipped(mask, devices))) for mask in range(4, devices, 4)]
+
+
+def first_exchange(lanes, small, stacks, devices):
+    arrived = exchange(lanes, devices)
     across, crossed, beside = [
         lax.optimization_barrier(arrived[lane])[-small.size // WIDE:].reshape(small.shape) for lane in EARLY
     ]
     plane = (small + beside) + (across + crossed)
-    late = [lane for lane in range(LANES) if lane not in EARLY]
-    plane, waiting = lax.optimization_barrier((plane, [lanes[lane] for lane in late]))
-    arrived.update({lane: lax.ppermute(value, "sub", pairs[lane]) for lane, value in zip(late, waiting)})
+    plane, stacks = lax.optimization_barrier((plane, stacks))
+    stacks = stacks + [lax.ppermute(stack, "sub", flipped(1, devices)) for stack in stacks]
     parts = [plane] + [lax.ppermute(plane, "sub", flipped(mask, devices)) for mask in range(4, devices, 4)]
     while len(parts) > 1:
         parts = [first + second for first, second in zip(parts[0::2], parts[1::2])]
-    return [arrived[lane] for lane in range(LANES)], parts[0]
+    return arrived, parts[0], stacks
 
 
 def over_devices(value, devices):
@@ -388,7 +386,9 @@
     z = Sizes(load, coupling, coarse_inv, devices)
     stacks = gathered(coarse_inv, devices)
     masks = tuple(mask for mask, _ in stacks)
+    masks = masks + tuple(mask ^ 1 for mask in masks)
     stacks = [stack for _, stack in stacks]
+    coupling, stacks[0] = lax.optimization_barrier((coupling, stacks[0]))
     tab = routing(partner, z.slots_per_lane)
 
     numbers = jnp.pad(corners.astype(F32), ((0, 0), (0, PAD - z.primal)), constant_values=-1.0)
@@ -412,10 +412,11 @@
         + [shape(z.carry_rows + (z.groups + 1) * z.loads * (lane in EARLY), z.dof) for lane in range(LANES)]
         + [shape(z.subs, z.unknowns, z.unknowns, dtype=BF), shape(z.subs, 4 * PAD, z.unknowns, dtype=BF)],
         (tab, load_faces, coupling, corner_row, spot, stiff_inv), [SMEM] + [VMEM] * 4 + [HBM],
-        apply_scratch + [pltpu.SemaphoreType.DMA((z.subs * PARTS,))], FIRST_LIMIT, "apply_load", **apply_cost,
+        apply_scratch + [pltpu.SemaphoreType.DMA((z.subs * PARTS,))], FIRST_LIMIT, "apply_load", flops=FIRST_FLOPS, moved=stiff_inv.size * 2,
     )
     near, weights = lanes[LANES:]
-    arrived, summed = first_exchange(lanes[:LANES], small, devices)
+    lanes, stacks = lax.optimization_barrier((lanes[:LANES], stacks))
+    arrived, summed, stacks = first_exchange(lanes, small, stacks, devices)
     spread, pick = call(
         unpack_kernel, z,
         [shape(z.total, 8 * PAD, z.dof, dtype=BF), shape(z.coarse, z.pick_width, dtype=BF)],

time: 163 us -> 161 us (0.988)
  starting transfers between devices: 57.4 us -> 52.8 us
    ppermute x18 -> x24, waiting for transfers between devices: 18.8 us -> 41.1 us  [exchange(): lax.ppermute(lane, 'sub', pairs)]
    ppermute x10 -> x4, waiting for transfers between devices: 14.5 us -> 1.3 us  [first_exchange(): lax.ppermute(stack, 'sub', flipped(1, devices))]
    ppermute x3, waiting for transfers between devices: 10 us -> 0.34 us  [gathered(): lax.ppermute(pair, 'sub', flipped(mask, devices))]
    ppermute x10 -> x4, starting transfers between devices: 6.49 us -> 0.82 us  [first_exchange(): lax.ppermute(stack, 'sub', flipped(1, devices))]
    ppermute x3, waiting for transfers between devices: 1.24 us -> 3.6 us  [first_exchange(): lax.ppermute(plane, 'sub', flipped(mask, devices))]
    ppermute x18 -> x24, starting transfers between devices: 15.5 us -> 17.3 us  [exchange(): lax.ppermute(lane, 'sub', pairs)]
  transfers between devices with their start and end apart: 65 -> 65, of which waited for: 25 -> 26; matrix products, arithmetic and copies ran while one was open for 0% -> 2% of each run, Pallas kernels for 0% -> 5%
where the time goes in v4:
time: 161 us
  waiting for transfers between devices  73.9 us (46%)
  starting transfers between devices  52.8 us (33%)
  Pallas kernels  28.2 us (18%)
  local copies, waits for them, and re-layouts  3.75 us (2%)
    ppermute x24, waiting for transfers between devices, exchange(): lax.ppermute(lane, 'sub', pairs)  41.1 us
    pallas_call x10, Pallas kernels, call(): pl.pallas_call(functools.partial(kernel, sizes), out_shape=outs, in_specs...  28.2 us
    ppermute x12, waiting for transfers between devices, over_devices(): value = value + lax.ppermute(value, 'sub', flipped(mask, devices))  24.2 us
    ppermute x24, starting transfers between devices, exchange(): lax.ppermute(lane, 'sub', pairs)  17.3 us
    ppermute x9, starting transfers between devices, exchange_in_turn(): lax.ppermute(value, 'sub', pairs[lane])  12.7 us
    ppermute x12, starting transfers between devices, over_devices(): value = value + lax.ppermute(value, 'sub', flipped(mask, devices))  9.47 us
    ppermute x3, starting transfers between devices, first_exchange(): lax.ppermute(plane, 'sub', flipped(mask, devices))  4.45 us
    ppermute x3, starting transfers between devices, gathered(): lax.ppermute(pair, 'sub', flipped(mask, devices))  4.45 us
  transfers between devices with their start and end apart: 65, of which 26 were waited for; matrix products, arithmetic and copies ran while one was open for 2% of the time, Pallas kernels for 5%

profile of v4, /device:TPU:0, one launch (start us, length us, event | category | flops | bytes accessed | tf_op | source)
XLA Modules:
  0.0 160.9 jit_solution(8776315560759823963)
XLA Ops:
  0.6 3.0 %collective-permute-start = (f32[32,512]{1,0:T(8,128)}, f32[32,512]{1,0:T(8,128)S(1)}, u32[]{:S(2)}, u32[]{:S(2)}) collective-permute-start(f32[32,512]{1,0:T(8,128)} %param.11), channel_id=1, source_target_pairs={{0,2},{1,3},{2,0},{3,1},{4,6},{5,7},{6,4},{7,5},{8,10},{9,11},{10,... | collective-permute-start | bytes 196616 | tf_op jit(solution)/shard_map/ppermute | solution.py:355
  3.7 0.7 convert_element_type.14
  4.4 0.8 constant_dynamic-update-slice_fusion.1
  5.3 0.8 reshape.197
  6.6 3.7 %collective-permute-start.3 = (f32[64,512]{1,0:T(8,128)S(1)}, f32[64,512]{1,0:T(8,128)S(1)}, u32[]{:S(2)}, u32[]{:S(2)}) collective-permute-start(f32[64,512]{1,0:T(8,128)S(1)} %constant_dynamic-update-slice_fusion.rest_0_), channel_id=1, source_target_pairs={{0,12},{1,13},{2,14},{3,15},{4,8},{5,9},{6,10},{7,11},{8,4},{9,5},... | collective-permute-start | bytes 393224 | tf_op jit(solution)/shard_map/ppermute | solution.py:356
  10.3 0.8 collective-permute-start.1
  11.1 1.0 copy-done.1
  12.1 0.9 copy-done.2
  13.1 7.7 %apply_load.1 = (f32[32,16,128]{2,1,0:T(8,128)S(1)}, f32[5,16,128]{2,1,0:T(8,128)S(1)}, f32[568,128]{1,0:T(8,128)S(1)}, f32[568,128]{1,0:T(8,128)S(1)}, f32[488,...) custom-call(s32[136]{0:T(256)S(1)} %pad_add_fusion.tab, ...), custom_call_target="tpu_custom_call" | custom-call | flops 20000000000 | bytes 16777216 | tf_op jit(solution)/shard_map/apply_load/pallas_call | solution.py:91
  21.1 1.2 collective-permute-start.5
  22.3 1.0 collective-permute-start.4
  23.8 16.6 %collective-permute-done.5.rest_0_ = f32[568,128]{1,0:T(8,128)S(1)} collective-permute-done((f32[568,128]{1,0:T(8,128)S(1)}, f32[568,128]{1,0:T(8,128)S(1)}, u32[]{:S(2)}, u32[]{:S(2)}) %collective-permute-start.5) | collective-permute-done | bytes 290848 | tf_op jit(solution)/shard_map/ppermute | solution.py:341
  40.4 3.7 %collective-permute-done.6.rest_1_ = f32[568,128]{1,0:T(8,128)S(1)} collective-permute-done((f32[568,128]{1,0:T(8,128)S(1)}, f32[568,128]{1,0:T(8,128)S(1)}, u32[]{:S(2)}, u32[]{:S(2)}) %collective-permute-start.6) | collective-permute-done | bytes 290848 | tf_op jit(solution)/shard_map/ppermute | solution.py:341
  44.1 2.6 %collective-permute-start.9 = (f32[5,16,128]{2,1,0:T(8,128)S(1)}, f32[5,16,128]{2,1,0:T(8,128)S(1)}, u32[]{:S(2)}, u32[]{:S(2)}) collective-permute-start(f32[5,16,128]{2,1,0:T(8,128)S(1)} %add_add_fusion.1), channel_id=1, source_target_pairs={{0,12},{1,13},{2,14},{3,15},{4,8},{5,9},{6,10},{7,11},{8,4},{9,5},... | collective-permute-start | bytes 122888 | tf_op jit(solution)/shard_map/ppermute | solution.py:367
  46.7 1.8 %collective-permute-start.7 = (f32[5,16,128]{2,1,0:T(8,128)S(1)}, f32[5,16,128]{2,1,0:T(8,128)S(1)}, u32[]{:S(2)}, u32[]{:S(2)}) collective-permute-start(f32[5,16,128]{2,1,0:T(8,128)S(1)} %add_add_fusion.1), channel_id=1, source_target_pairs={{0,4},{1,5},{2,6},{3,7},{4,0},{5,1},{6,2},{7,3},{8,12},{9,13},{10,... | collective-permute-start | bytes 122888 | tf_op jit(solution)/shard_map/ppermute | solution.py:367
  48.6 0.7 collective-permute-start.10
  49.4 1.0 unpack_coupling.1
  50.4 1.3 collective-permute-done.9
  51.7 2.3 %collective-permute-done.8 = f32[5,16,128]{2,1,0:T(8,128)S(1)} collective-permute-done((f32[5,16,128]{2,1,0:T(8,128)S(1)}, f32[5,16,128]{2,1,0:T(8,128)S(1)}, u32[]{:S(2)}, u32[]{:S(2)}) %collective-permute-start.8) | collective-permute-done | bytes 40992 | tf_op jit(solution)/shard_map/ppermute | solution.py:367
  54.0 1.3 collective-permute-done.13.rest_7_
  55.5 1.9 %first_residual.1 = (f32[32,16,128]{2,1,0:T(8,128)S(1)}, f32[32,16,128]{2,1,0:T(8,128)S(1)}, f32[12,16,128]{2,1,0:T(8,128)S(1)}, f32[12,16,128]{2,1,0:T(8,128)S(...) custom-call(s32[136]{0:T(256)S(1)} %pad_add_fusion.tab, ...), custom_call_target="tpu_custom_call" | custom-call | tf_op jit(solution)/shard_map/first_residual/pallas_call | solution.py:91
  57.4 1.5 collective-permute-start.17
  59.0 0.6 collective-permute-start.19
  59.6 3.2 %collective-permute-start.21 = (f32[12,16,128]{2,1,0:T(8,128)S(1)}, f32[12,16,128]{2,1,0:T(8,128)S(1)}, u32[]{:S(2)}, u32[]{:S(2)}) collective-permute-start(f32[12,16,128]{2,1,0:T(8,128)S(1)} %get-tuple-element.146), channel_id=1, source_target_pairs={{0,13},{1,4},{2,15},{3,6},{4,1},{5,8},{6,3},{7,10},{8,5},{9,12},{1... | collective-permute-start | bytes 294920 | tf_op jit(solution)/shard_map/ppermute | solution.py:341
  62.8 4.8 %collective-permute-done.18.rest_1_ = f32[12,16,128]{2,1,0:T(8,128)S(1)} collective-permute-done((f32[12,16,128]{2,1,0:T(8,128)S(1)}, f32[12,16,128]{2,1,0:T(8,128)S(1)}, u32[]{:S(2)}, u32[]{:S(2)}) %collective-permute-start.18) | collective-permute-done | bytes 98336 | tf_op jit(solution)/shard_map/ppermute | solution.py:341
  67.6 2.4 %collective-permute-done.21.rest_4_ = f32[12,16,128]{2,1,0:T(8,128)S(1)} collective-permute-done((f32[12,16,128]{2,1,0:T(8,128)S(1)}, f32[12,16,128]{2,1,0:T(8,128)S(1)}, u32[]{:S(2)}, u32[]{:S(2)}) %collective-permute-start.21) | collective-permute-done | bytes 98336 | tf_op jit(solution)/shard_map/ppermute | solution.py:341
  70.0 3.7 %precond_apply.3 = (f32[32,16,128]{2,1,0:T(8,128)S(1)}, f32[32,16,128]{2,1,0:T(8,128)S(1)}, f32[5,16,128]{2,1,0:T(8,128)S(1)}, f32[12,16,128]{2,1,0:T(8,128)S(1)...) custom-call(s32[136]{0:T(256)S(1)} %pad_add_fusion.tab, ...), custom_call_target="tpu_custom_call" | custom-call | flops 268435456 | bytes 16777216 | tf_op jit(solution)/shard_map/precond_apply/pallas_call | solution.py:91
  74.3 3.8 %collective-permute-done.23 = f32[5,16,128]{2,1,0:T(8,128)S(1)} collective-permute-done((f32[5,16,128]{2,1,0:T(8,128)S(1)}, f32[5,16,128]{2,1,0:T(8,128)S(1)}, u32[]{:S(2)}, u32[]{:S(2)}) %collective-permute-start.23) | collective-permute-done | bytes 40992 | tf_op jit(solution)/shard_map/ppermute | solution.py:380
  78.1 1.8 %collective-permute-start.24 = (f32[5,16,128]{2,1,0:T(8,128)S(1)}, f32[5,16,128]{2,1,0:T(8,128)S(1)}, u32[]{:S(2)}, u32[]{:S(2)}) collective-permute-start(f32[5,16,128]{2,1,0:T(8,128)S(1)} %add.189), channel_id=1, source_target_pairs={{0,8},{1,9},{2,10},{3,11},{4,12},{5,13},{6,14},{7,15},{8,0},{9,1},... | collective-permute-start | bytes 122888 | tf_op jit(solution)/shard_map/ppermute | solution.py:380
  80.5 3.6 %collective-permute-start.31 = (f32[12,16,128]{2,1,0:T(8,128)S(1)}, f32[12,16,128]{2,1,0:T(8,128)S(1)}, u32[]{:S(2)}, u32[]{:S(2)}) collective-permute-start(f32[12,16,128]{2,1,0:T(8,128)S(1)} %get-tuple-element.160), channel_id=1, source_target_pairs={{0,13},{1,4},{2,15},{3,6},{4,1},{5,8},{6,3},{7,10},{8,5},{9,12},{1... | collective-permute-start | bytes 294920 | tf_op jit(solution)/shard_map/ppermute | solution.py:350
  84.2 1.2 collective-permute-done.25
  86.0 3.4 %collective-permute-done.26 = f32[5,16,128]{2,1,0:T(8,128)S(1)} collective-permute-done((f32[5,16,128]{2,1,0:T(8,128)S(1)}, f32[5,16,128]{2,1,0:T(8,128)S(1)}, u32[]{:S(2)}, u32[]{:S(2)}) %collective-permute-start.26) | collective-permute-done | bytes 40992 | tf_op jit(solution)/shard_map/ppermute | solution.py:380
  89.4 1.1 collective-permute-done.31.rest_4_
  90.6 2.0 %cg_step.3 = (f32[32,16,128]{2,1,0:T(8,128)S(1)}, f32[32,16,128]{2,1,0:T(8,128)S(1)}, f32[32,16,128]{2,1,0:T(8,128)S(1)}, f32[32,16,128]{2,1,0:T(8,128)S(1)}, f3...) custom-call(s32[136]{0:T(256)S(1)} %pad_add_fusion.tab, ...), custom_call_target="tpu_custom_call" | custom-call | tf_op jit(solution)/shard_map/cg_step/pallas_call | solution.py:91
  92.6 0.8 collective-permute-start.34
  93.4 1.4 collective-permute-start.35
  94.8 2.4 %collective-permute-start.37 = (f32[12,16,128]{2,1,0:T(8,128)S(1)}, f32[12,16,128]{2,1,0:T(8,128)S(1)}, u32[]{:S(2)}, u32[]{:S(2)}) collective-permute-start(f32[12,16,128]{2,1,0:T(8,128)S(1)} %get-tuple-element.169), channel_id=1, source_target_pairs={{0,13},{1,4},{2,15},{3,6},{4,1},{5,8},{6,3},{7,10},{8,5},{9,12},{1... | collective-permute-start | bytes 294920 | tf_op jit(solution)/shard_map/ppermute | solution.py:341
  97.1 0.7 collective-permute-done.33.rest_0_
  97.8 2.8 %collective-permute-done.34.rest_1_ = f32[12,16,128]{2,1,0:T(8,128)S(1)} collective-permute-done((f32[12,16,128]{2,1,0:T(8,128)S(1)}, f32[12,16,128]{2,1,0:T(8,128)S(1)}, u32[]{:S(2)}, u32[]{:S(2)}) %collective-permute-start.34) | collective-permute-done | bytes 98336 | tf_op jit(solution)/shard_map/ppermute | solution.py:341
  100.6 3.4 %collective-permute-done.37.rest_4_ = f32[12,16,128]{2,1,0:T(8,128)S(1)} collective-permute-done((f32[12,16,128]{2,1,0:T(8,128)S(1)}, f32[12,16,128]{2,1,0:T(8,128)S(1)}, u32[]{:S(2)}, u32[]{:S(2)}) %collective-permute-start.37) | collective-permute-done | bytes 98336 | tf_op jit(solution)/shard_map/ppermute | solution.py:341
  104.0 3.7 %precond_apply.4 = (f32[32,16,128]{2,1,0:T(8,128)S(1)}, f32[32,16,128]{2,1,0:T(8,128)S(1)}, f32[5,16,128]{2,1,0:T(8,128)S(1)}, f32[12,16,128]{2,1,0:T(8,128)S(1)...) custom-call(s32[136]{0:T(256)S(1)} %pad_add_fusion.tab, ...), custom_call_target="tpu_custom_call" | custom-call | flops 268435456 | bytes 16777216 | tf_op jit(solution)/shard_map/precond_apply/pallas_call | solution.py:91
  107.9 0.6 collective-permute-start.39
  108.4 3.5 %collective-permute-done.39 = f32[5,16,128]{2,1,0:T(8,128)S(1)} collective-permute-done((f32[5,16,128]{2,1,0:T(8,128)S(1)}, f32[5,16,128]{2,1,0:T(8,128)S(1)}, u32[]{:S(2)}, u32[]{:S(2)}) %collective-permute-start.39) | collective-permute-done | bytes 40992 | tf_op jit(solution)/shard_map/ppermute | solution.py:380
  111.9 1.8 %collective-permute-start.40 = (f32[5,16,128]{2,1,0:T(8,128)S(1)}, f32[5,16,128]{2,1,0:T(8,128)S(1)}, u32[]{:S(2)}, u32[]{:S(2)}) collective-permute-start(f32[5,16,128]{2,1,0:T(8,128)S(1)} %add.193), channel_id=1, source_target_pairs={{0,8},{1,9},{2,10},{3,11},{4,12},{5,13},{6,14},{7,15},{8,0},{9,1},... | collective-permute-start | bytes 122888 | tf_op jit(solution)/shard_map/ppermute | solution.py:380
  114.3 3.8 %collective-permute-start.47 = (f32[12,16,128]{2,1,0:T(8,128)S(1)}, f32[12,16,128]{2,1,0:T(8,128)S(1)}, u32[]{:S(2)}, u32[]{:S(2)}) collective-permute-start(f32[12,16,128]{2,1,0:T(8,128)S(1)} %get-tuple-element.186), channel_id=1, source_target_pairs={{0,13},{1,4},{2,15},{3,6},{4,1},{5,8},{6,3},{7,10},{8,5},{9,12},{1... | collective-permute-start | bytes 294920 | tf_op jit(solution)/shard_map/ppermute | solution.py:350
  118.2 1.2 collective-permute-done.41
  119.4 0.7 collective-permute-start.42
  120.1 3.3 %collective-permute-done.42 = f32[5,16,128]{2,1,0:T(8,128)S(1)} collective-permute-done((f32[5,16,128]{2,1,0:T(8,128)S(1)}, f32[5,16,128]{2,1,0:T(8,128)S(1)}, u32[]{:S(2)}, u32[]{:S(2)}) %collective-permute-start.42) | collective-permute-done | bytes 40992 | tf_op jit(solution)/shard_map/ppermute | solution.py:380
  123.5 1.1 collective-permute-done.47.rest_8_
  124.6 2.1 %cg_step.4 = (f32[32,16,128]{2,1,0:T(8,128)S(1)}, f32[32,16,128]{2,1,0:T(8,128)S(1)}, f32[32,16,128]{2,1,0:T(8,128)S(1)}, f32[32,16,128]{2,1,0:T(8,128)S(1)}, f3...) custom-call(s32[136]{0:T(256)S(1)} %pad_add_fusion.tab, ...), custom_call_target="tpu_custom_call" | custom-call | tf_op jit(solution)/shard_map/cg_step/pallas_call | solution.py:91
  126.8 2.0 %collective-permute-start.51 = (f32[12,16,128]{2,1,0:T(8,128)S(1)}, f32[12,16,128]{2,1,0:T(8,128)S(1)}, u32[]{:S(2)}, u32[]{:S(2)}) collective-permute-start(f32[12,16,128]{2,1,0:T(8,128)S(1)} %get-tuple-element.193), channel_id=1, source_target_pairs={{0,1},{1,0},{2,4},{3,5},{4,2},{5,3},{6,8},{7,9},{8,6},{9,7},{10,12... | collective-permute-start | bytes 294920 | tf_op jit(solution)/shard_map/ppermute | solution.py:341
  128.9 2.5 %collective-permute-start.53 = (f32[12,16,128]{2,1,0:T(8,128)S(1)}, f32[12,16,128]{2,1,0:T(8,128)S(1)}, u32[]{:S(2)}, u32[]{:S(2)}) collective-permute-start(f32[12,16,128]{2,1,0:T(8,128)S(1)} %get-tuple-element.195), channel_id=1, source_target_pairs={{0,13},{1,4},{2,15},{3,6},{4,1},{5,8},{6,3},{7,10},{8,5},{9,12},{1... | collective-permute-start | bytes 294920 | tf_op jit(solution)/shard_map/ppermute | solution.py:341
  131.9 2.7 %collective-permute-done.50.rest_1_ = f32[12,16,128]{2,1,0:T(8,128)S(1)} collective-permute-done((f32[12,16,128]{2,1,0:T(8,128)S(1)}, f32[12,16,128]{2,1,0:T(8,128)S(1)}, u32[]{:S(2)}, u32[]{:S(2)}) %collective-permute-start.50) | collective-permute-done | bytes 98336 | tf_op jit(solution)/shard_map/ppermute | solution.py:341
  134.6 3.4 %collective-permute-done.53.rest_4_ = f32[12,16,128]{2,1,0:T(8,128)S(1)} collective-permute-done((f32[12,16,128]{2,1,0:T(8,128)S(1)}, f32[12,16,128]{2,1,0:T(8,128)S(1)}, u32[]{:S(2)}, u32[]{:S(2)}) %collective-permute-start.53) | collective-permute-done | bytes 98336 | tf_op jit(solution)/shard_map/ppermute | solution.py:341
  138.0 3.7 %precond_apply.5 = (f32[32,16,128]{2,1,0:T(8,128)S(1)}, f32[32,16,128]{2,1,0:T(8,128)S(1)}, f32[5,16,128]{2,1,0:T(8,128)S(1)}, f32[12,16,128]{2,1,0:T(8,128)S(1)...) custom-call(s32[136]{0:T(256)S(1)} %pad_add_fusion.tab, ...), custom_call_target="tpu_custom_call" | custom-call | flops 268435456 | bytes 16777216 | tf_op jit(solution)/shard_map/precond_apply/pallas_call | solution.py:91
  141.9 0.9 collective-permute-start.55
  142.7 3.2 %collective-permute-done.55 = f32[5,16,128]{2,1,0:T(8,128)S(1)} collective-permute-done((f32[5,16,128]{2,1,0:T(8,128)S(1)}, f32[5,16,128]{2,1,0:T(8,128)S(1)}, u32[]{:S(2)}, u32[]{:S(2)}) %collective-permute-start.55) | collective-permute-done | bytes 40992 | tf_op jit(solution)/shard_map/ppermute | solution.py:380
  145.9 2.0 %collective-permute-start.56 = (f32[5,16,128]{2,1,0:T(8,128)S(1)}, f32[5,16,128]{2,1,0:T(8,128)S(1)}, u32[]{:S(2)}, u32[]{:S(2)}) collective-permute-start(f32[5,16,128]{2,1,0:T(8,128)S(1)} %add.197), channel_id=1, source_target_pairs={{0,8},{1,9},{2,10},{3,11},{4,12},{5,13},{6,14},{7,15},{8,0},{9,1},... | collective-permute-start | bytes 122888 | tf_op jit(solution)/shard_map/ppermute | solution.py:380
  148.6 3.5 %collective-permute-start.63 = (f32[12,16,128]{2,1,0:T(8,128)S(1)}, f32[12,16,128]{2,1,0:T(8,128)S(1)}, u32[]{:S(2)}, u32[]{:S(2)}) collective-permute-start(f32[12,16,128]{2,1,0:T(8,128)S(1)} %get-tuple-element.212), channel_id=1, source_target_pairs={{0,13},{1,4},{2,15},{3,6},{4,1},{5,8},{6,3},{7,10},{8,5},{9,12},{1... | collective-permute-start | bytes 294920 | tf_op jit(solution)/shard_map/ppermute | solution.py:350
  152.2 1.2 collective-permute-done.57
  153.4 0.8 collective-permute-start.58
  154.2 3.2 %collective-permute-done.58 = f32[5,16,128]{2,1,0:T(8,128)S(1)} collective-permute-done((f32[5,16,128]{2,1,0:T(8,128)S(1)}, f32[5,16,128]{2,1,0:T(8,128)S(1)}, u32[]{:S(2)}, u32[]{:S(2)}) %collective-permute-start.58) | collective-permute-done | bytes 40992 | tf_op jit(solution)/shard_map/ppermute | solution.py:380
  157.5 1.1 collective-permute-done.63.rest_8_
  158.6 2.3 %cg_step.5 = (f32[32,16,128]{2,1,0:T(8,128)}, f32[32,16,128]{2,1,0:T(8,128)}) custom-call(s32[136]{0:T(256)S(1)} %pad_add_fusion.tab, f32[32,16,128]{2,1,0:T(8,128)S(1)} %get-tuple-element.197.image, f32[5,16,128]{2,1,0:T(8,128)S(1)} %add.200.summed, bf16[512,512]{1,0:T(8,128)(2,1)S(1)} %get-tuple-element.131.upper, ...), custom_call_target="tpu_custom_call" | custom-call | tf_op jit(solution)/shard_map/cg_step/pallas_call | solution.py:91
  (114 shorter events, 6.2 us)
Async XLA Ops:
  0.6 6.0 %collective-permute-start = (f32[32,512]{1,0:T(8,128)}, f32[32,512]{1,0:T(8,128)S(1)}, u32[]{:S(2)}, u32[]{:S(2)}) collective-permute-start(f32[32,512]{1,0:T(8,128)} %param.11), channel_id=1, source_target_pairs={{0,2},{1,3},{2,0},{3,1},{4,6},{5,7},{6,4},{7,5},{8,10},{9,11},{10,... | collective-permute-start | bytes 196616 | tf_op jit(solution)/shard_map/ppermute | solution.py:355
  6.6 14.1 %collective-permute-start.3 = (f32[64,512]{1,0:T(8,128)S(1)}, f32[64,512]{1,0:T(8,128)S(1)}, u32[]{:S(2)}, u32[]{:S(2)}) collective-permute-start(f32[64,512]{1,0:T(8,128)S(1)} %constant_dynamic-update-slice_fusion.rest_0_), channel_id=1, source_target_pairs={{0,12},{1,13},{2,14},{3,15},{4,8},{5,9},{6,10},{7,11},{8,4},{9,5},... | collective-permute-start | bytes 393224 | tf_op jit(solution)/shard_map/ppermute | solution.py:356
  10.3 10.8 %collective-permute-start.2 = (f32[64,512]{1,0:T(8,128)S(1)}, f32[64,512]{1,0:T(8,128)S(1)}, u32[]{:S(2)}, u32[]{:S(2)}) collective-permute-start(f32[64,512]{1,0:T(8,128)S(1)} %constant_dynamic-update-slice_fusion.rest_0_), channel_id=1, source_target_pairs={{0,8},{1,9},{2,10},{3,11},{4,12},{5,13},{6,14},{7,15},{8,0},{9,1},... | collective-permute-start | bytes 393224 | tf_op jit(solution)/shard_map/ppermute | solution.py:356
  10.3 10.8 %collective-permute-start.1 = (f32[64,512]{1,0:T(8,128)S(1)}, f32[64,512]{1,0:T(8,128)S(1)}, u32[]{:S(2)}, u32[]{:S(2)}) collective-permute-start(f32[64,512]{1,0:T(8,128)S(1)} %constant_dynamic-update-slice_fusion.rest_0_), channel_id=1, source_target_pairs={{0,4},{1,5},{2,6},{3,7},{4,0},{5,1},{6,2},{7,3},{8,12},{9,13},{10,... | collective-permute-start | bytes 393224 | tf_op jit(solution)/shard_map/ppermute | solution.py:356
  21.1 19.3 %collective-permute-start.5 = (f32[568,128]{1,0:T(8,128)S(1)}, f32[568,128]{1,0:T(8,128)S(1)}, u32[]{:S(2)}, u32[]{:S(2)}) collective-permute-start(f32[568,128]{1,0:T(8,128)S(1)} %get-tuple-element.120), channel_id=1, source_target_pairs={{0,2},{1,3},{2,0},{3,1},{4,6},{5,7},{6,4},{7,5},{8,10},{9,11},{10,... | collective-permute-start | bytes 872456 | tf_op jit(solution)/shard_map/ppermute | solution.py:341
  22.3 21.8 %collective-permute-start.6 = (f32[568,128]{1,0:T(8,128)S(1)}, f32[568,128]{1,0:T(8,128)S(1)}, u32[]{:S(2)}, u32[]{:S(2)}) collective-permute-start(f32[568,128]{1,0:T(8,128)S(1)} %get-tuple-element.121), channel_id=1, source_target_pairs={{0,3},{1,2},{2,1},{3,0},{4,7},{5,6},{6,5},{7,4},{8,11},{9,10},{10,... | collective-permute-start | bytes 872456 | tf_op jit(solution)/shard_map/ppermute | solution.py:341
  22.3 21.8 %collective-permute-start.4 = (f32[568,128]{1,0:T(8,128)S(1)}, f32[568,128]{1,0:T(8,128)S(1)}, u32[]{:S(2)}, u32[]{:S(2)}) collective-permute-start(f32[568,128]{1,0:T(8,128)S(1)} %get-tuple-element.119), channel_id=1, source_target_pairs={{0,1},{1,0},{2,3},{3,2},{4,5},{5,4},{6,7},{7,6},{8,9},{9,8},{10,11... | collective-permute-start | bytes 872456 | tf_op jit(solution)/shard_map/ppermute | solution.py:341
  23.3 23.5 %collective-permute-start.14 = (f32[488,128]{1,0:T(8,128)S(1)}, f32[488,128]{1,0:T(8,128)S(1)}, u32[]{:S(2)}, u32[]{:S(2)}) collective-permute-start(f32[488,128]{1,0:T(8,128)S(1)} %get-tuple-element.133), channel_id=1, source_target_pairs={{0,1},{1,0},{2,4},{3,5},{4,2},{5,3},{6,8},{7,9},{8,6},{9,7},{10,12... | collective-permute-start | bytes 749576 | tf_op jit(solution)/shard_map/ppermute | solution.py:341
  23.3 25.3 %collective-permute-start.15 = (f32[488,128]{1,0:T(8,128)S(1)}, f32[488,128]{1,0:T(8,128)S(1)}, u32[]{:S(2)}, u32[]{:S(2)}) collective-permute-start(f32[488,128]{1,0:T(8,128)S(1)} %get-tuple-element.134), channel_id=1, source_target_pairs={{0,1},{1,0},{2,5},{3,4},{4,3},{5,2},{6,9},{7,8},{8,7},{9,6},{10,13... | collective-permute-start | bytes 749576 | tf_op jit(solution)/shard_map/ppermute | solution.py:341
  40.4 8.9 %collective-permute-start.16 = (f32[488,128]{1,0:T(8,128)S(1)}, f32[488,128]{1,0:T(8,128)S(1)}, u32[]{:S(2)}, u32[]{:S(2)}) collective-permute-start(f32[488,128]{1,0:T(8,128)S(1)} %get-tuple-element.135), channel_id=1, source_target_pairs={{0,13},{1,4},{2,15},{3,6},{4,1},{5,8},{6,3},{7,10},{8,5},{9,12},{1... | collective-permute-start | bytes 749576 | tf_op jit(solution)/shard_map/ppermute | solution.py:341
  44.1 7.6 %collective-permute-start.9 = (f32[5,16,128]{2,1,0:T(8,128)S(1)}, f32[5,16,128]{2,1,0:T(8,128)S(1)}, u32[]{:S(2)}, u32[]{:S(2)}) collective-permute-start(f32[5,16,128]{2,1,0:T(8,128)S(1)} %add_add_fusion.1), channel_id=1, source_target_pairs={{0,12},{1,13},{2,14},{3,15},{4,8},{5,9},{6,10},{7,11},{8,4},{9,5},... | collective-permute-start | bytes 122888 | tf_op jit(solution)/shard_map/ppermute | solution.py:367
  46.7 7.3 %collective-permute-start.8 = (f32[5,16,128]{2,1,0:T(8,128)S(1)}, f32[5,16,128]{2,1,0:T(8,128)S(1)}, u32[]{:S(2)}, u32[]{:S(2)}) collective-permute-start(f32[5,16,128]{2,1,0:T(8,128)S(1)} %add_add_fusion.1), channel_id=1, source_target_pairs={{0,8},{1,9},{2,10},{3,11},{4,12},{5,13},{6,14},{7,15},{8,0},{9,1},... | collective-permute-start | bytes 122888 | tf_op jit(solution)/shard_map/ppermute | solution.py:367
  46.7 7.3 %collective-permute-start.7 = (f32[5,16,128]{2,1,0:T(8,128)S(1)}, f32[5,16,128]{2,1,0:T(8,128)S(1)}, u32[]{:S(2)}, u32[]{:S(2)}) collective-permute-start(f32[5,16,128]{2,1,0:T(8,128)S(1)} %add_add_fusion.1), channel_id=1, source_target_pairs={{0,4},{1,5},{2,6},{3,7},{4,0},{5,1},{6,2},{7,3},{8,12},{9,13},{10,... | collective-permute-start | bytes 122888 | tf_op jit(solution)/shard_map/ppermute | solution.py:367
  48.6 5.4 %collective-permute-start.10 = (f32[64,512]{1,0:T(8,128)S(1)}, f32[64,512]{1,0:T(8,128)S(1)}, u32[]{:S(2)}, u32[]{:S(2)}) collective-permute-start(f32[64,512]{1,0:T(8,128)S(1)} %constant_dynamic-update-slice_fusion.rest_0_), channel_id=1, source_target_pairs={{0,1},{1,0},{2,3},{3,2},{4,5},{5,4},{6,7},{7,6},{8,9},{9,8},{10,11... | collective-permute-start | bytes 393224 | tf_op jit(solution)/shard_map/ppermute | solution.py:366
  49.3 4.8 %collective-permute-start.11 = (f32[64,512]{1,0:T(8,128)S(1)}, f32[64,512]{1,0:T(8,128)S(1)}, u32[]{:S(2)}, u32[]{:S(2)}) collective-permute-start(f32[64,512]{1,0:T(8,128)S(1)} %collective-permute-done.1.rest_1_), channel_id=1, source_target_pairs={{0,1},{1,0},{2,3},{3,2},{4,5},{5,4},{6,7},{7,6},{8,9},{9,8},{10,11... | collective-permute-start | bytes 393224 | tf_op jit(solution)/shard_map/ppermute | solution.py:366
  51.7 2.3 %collective-permute-start.12 = (f32[64,512]{1,0:T(8,128)S(1)}, f32[64,512]{1,0:T(8,128)S(1)}, u32[]{:S(2)}, u32[]{:S(2)}) collective-permute-start(f32[64,512]{1,0:T(8,128)S(1)} %collective-permute-done.2.rest_2_), channel_id=1, source_target_pairs={{0,1},{1,0},{2,3},{3,2},{4,5},{5,4},{6,7},{7,6},{8,9},{9,8},{10,11... | collective-permute-start | bytes 393224 | tf_op jit(solution)/shard_map/ppermute | solution.py:366
  54.0 1.3 collective-permute-start.13
  57.4 5.4 %collective-permute-start.17 = (f32[12,16,128]{2,1,0:T(8,128)S(1)}, f32[12,16,128]{2,1,0:T(8,128)S(1)}, u32[]{:S(2)}, u32[]{:S(2)}) collective-permute-start(f32[12,16,128]{2,1,0:T(8,128)S(1)} %get-tuple-element.142), channel_id=1, source_target_pairs={{0,2},{1,3},{2,0},{3,1},{4,6},{5,7},{6,4},{7,5},{8,10},{9,11},{10,... | collective-permute-start | bytes 294920 | tf_op jit(solution)/shard_map/ppermute | solution.py:341
  58.9 8.7 %collective-permute-start.18 = (f32[12,16,128]{2,1,0:T(8,128)S(1)}, f32[12,16,128]{2,1,0:T(8,128)S(1)}, u32[]{:S(2)}, u32[]{:S(2)}) collective-permute-start(f32[12,16,128]{2,1,0:T(8,128)S(1)} %get-tuple-element.143), channel_id=1, source_target_pairs={{0,3},{1,2},{2,1},{3,0},{4,7},{5,6},{6,5},{7,4},{8,11},{9,10},{10,... | collective-permute-start | bytes 294920 | tf_op jit(solution)/shard_map/ppermute | solution.py:341
  59.0 8.6 %collective-permute-start.19 = (f32[12,16,128]{2,1,0:T(8,128)S(1)}, f32[12,16,128]{2,1,0:T(8,128)S(1)}, u32[]{:S(2)}, u32[]{:S(2)}) collective-permute-start(f32[12,16,128]{2,1,0:T(8,128)S(1)} %get-tuple-element.144), channel_id=1, source_target_pairs={{0,1},{1,0},{2,4},{3,5},{4,2},{5,3},{6,8},{7,9},{8,6},{9,7},{10,12... | collective-permute-start | bytes 294920 | tf_op jit(solution)/shard_map/ppermute | solution.py:341
  59.6 8.0 %collective-permute-start.20 = (f32[12,16,128]{2,1,0:T(8,128)S(1)}, f32[12,16,128]{2,1,0:T(8,128)S(1)}, u32[]{:S(2)}, u32[]{:S(2)}) collective-permute-start(f32[12,16,128]{2,1,0:T(8,128)S(1)} %get-tuple-element.145), channel_id=1, source_target_pairs={{0,1},{1,0},{2,5},{3,4},{4,3},{5,2},{6,9},{7,8},{8,7},{9,6},{10,13... | collective-permute-start | bytes 294920 | tf_op jit(solution)/shard_map/ppermute | solution.py:341
  59.6 10.4 %collective-permute-start.21 = (f32[12,16,128]{2,1,0:T(8,128)S(1)}, f32[12,16,128]{2,1,0:T(8,128)S(1)}, u32[]{:S(2)}, u32[]{:S(2)}) collective-permute-start(f32[12,16,128]{2,1,0:T(8,128)S(1)} %get-tuple-element.146), channel_id=1, source_target_pairs={{0,13},{1,4},{2,15},{3,6},{4,1},{5,8},{6,3},{7,10},{8,5},{9,12},{1... | collective-permute-start | bytes 294920 | tf_op jit(solution)/shard_map/ppermute | solution.py:341
  62.8 7.3 %collective-permute-start.22 = (f32[12,16,128]{2,1,0:T(8,128)S(1)}, f32[12,16,128]{2,1,0:T(8,128)S(1)}, u32[]{:S(2)}, u32[]{:S(2)}) collective-permute-start(f32[12,16,128]{2,1,0:T(8,128)S(1)} %get-tuple-element.147), channel_id=1, source_target_pairs={{0,1},{1,0},{2,3},{3,2},{4,5},{5,4},{6,7},{7,6},{8,9},{9,8},{10,11... | collective-permute-start | bytes 294920 | tf_op jit(solution)/shard_map/ppermute | solution.py:341
  73.7 6.1 %collective-permute-start.27 = (f32[12,16,128]{2,1,0:T(8,128)S(1)}, f32[12,16,128]{2,1,0:T(8,128)S(1)}, u32[]{:S(2)}, u32[]{:S(2)}) collective-permute-start(f32[12,16,128]{2,1,0:T(8,128)S(1)} %get-tuple-element.151), channel_id=1, source_target_pairs={{0,2},{1,3},{2,0},{3,1},{4,6},{5,7},{6,4},{7,5},{8,10},{9,11},{10,... | collective-permute-start | bytes 294920 | tf_op jit(solution)/shard_map/ppermute | solution.py:346
  73.8 6.1 %collective-permute-start.28 = (f32[12,16,128]{2,1,0:T(8,128)S(1)}, f32[12,16,128]{2,1,0:T(8,128)S(1)}, u32[]{:S(2)}, u32[]{:S(2)}) collective-permute-start(f32[12,16,128]{2,1,0:T(8,128)S(1)} %get-tuple-element.152), channel_id=1, source_target_pairs={{0,3},{1,2},{2,1},{3,0},{4,7},{5,6},{6,5},{7,4},{8,11},{9,10},{10,... | collective-permute-start | bytes 294920 | tf_op jit(solution)/shard_map/ppermute | solution.py:346
  74.0 4.0 %collective-permute-start.23 = (f32[5,16,128]{2,1,0:T(8,128)S(1)}, f32[5,16,128]{2,1,0:T(8,128)S(1)}, u32[]{:S(2)}, u32[]{:S(2)}) collective-permute-start(f32[5,16,128]{2,1,0:T(8,128)S(1)} %get-tuple-element.149), channel_id=1, source_target_pairs={{0,4},{1,5},{2,6},{3,7},{4,0},{5,1},{6,2},{7,3},{8,12},{9,13},{10,... | collective-permute-start | bytes 122888 | tf_op jit(solution)/shard_map/ppermute | solution.py:380
  78.1 6.0 %collective-permute-start.24 = (f32[5,16,128]{2,1,0:T(8,128)S(1)}, f32[5,16,128]{2,1,0:T(8,128)S(1)}, u32[]{:S(2)}, u32[]{:S(2)}) collective-permute-start(f32[5,16,128]{2,1,0:T(8,128)S(1)} %add.189), channel_id=1, source_target_pairs={{0,8},{1,9},{2,10},{3,11},{4,12},{5,13},{6,14},{7,15},{8,0},{9,1},... | collective-permute-start | bytes 122888 | tf_op jit(solution)/shard_map/ppermute | solution.py:380
  79.9 9.5 %collective-permute-start.32 = (f32[12,16,128]{2,1,0:T(8,128)S(1)}, f32[12,16,128]{2,1,0:T(8,128)S(1)}, u32[]{:S(2)}, u32[]{:S(2)}) collective-permute-start(f32[12,16,128]{2,1,0:T(8,128)S(1)} %get-tuple-element.161), channel_id=1, source_target_pairs={{0,1},{1,0},{2,3},{3,2},{4,5},{5,4},{6,7},{7,6},{8,9},{9,8},{10,11... | collective-permute-start | bytes 294920 | tf_op jit(solution)/shard_map/ppermute | solution.py:346
  79.9 9.5 %collective-permute-start.29 = (f32[12,16,128]{2,1,0:T(8,128)S(1)}, f32[12,16,128]{2,1,0:T(8,128)S(1)}, u32[]{:S(2)}, u32[]{:S(2)}) collective-permute-start(f32[12,16,128]{2,1,0:T(8,128)S(1)} %get-tuple-element.158), channel_id=1, source_target_pairs={{0,1},{1,0},{2,4},{3,5},{4,2},{5,3},{6,8},{7,9},{8,6},{9,7},{10,12... | collective-permute-start | bytes 294920 | tf_op jit(solution)/shard_map/ppermute | solution.py:350
  80.4 9.0 %collective-permute-start.30 = (f32[12,16,128]{2,1,0:T(8,128)S(1)}, f32[12,16,128]{2,1,0:T(8,128)S(1)}, u32[]{:S(2)}, u32[]{:S(2)}) collective-permute-start(f32[12,16,128]{2,1,0:T(8,128)S(1)} %get-tuple-element.159), channel_id=1, source_target_pairs={{0,1},{1,0},{2,5},{3,4},{4,3},{5,2},{6,9},{7,8},{8,7},{9,6},{10,13... | collective-permute-start | bytes 294920 | tf_op jit(solution)/shard_map/ppermute | solution.py:350
  80.5 10.1 %collective-permute-start.31 = (f32[12,16,128]{2,1,0:T(8,128)S(1)}, f32[12,16,128]{2,1,0:T(8,128)S(1)}, u32[]{:S(2)}, u32[]{:S(2)}) collective-permute-start(f32[12,16,128]{2,1,0:T(8,128)S(1)} %get-tuple-element.160), channel_id=1, source_target_pairs={{0,13},{1,4},{2,15},{3,6},{4,1},{5,8},{6,3},{7,10},{8,5},{9,12},{1... | collective-permute-start | bytes 294920 | tf_op jit(solution)/shard_map/ppermute | solution.py:350
  84.1 1.3 collective-permute-start.25
  85.4 4.0 %collective-permute-start.26 = (f32[5,16,128]{2,1,0:T(8,128)S(1)}, f32[5,16,128]{2,1,0:T(8,128)S(1)}, u32[]{:S(2)}, u32[]{:S(2)}) collective-permute-start(f32[5,16,128]{2,1,0:T(8,128)S(1)} %add.191), channel_id=1, source_target_pairs={{0,2},{1,3},{2,0},{3,1},{4,6},{5,7},{6,4},{7,5},{8,10},{9,11},{10,... | collective-permute-start | bytes 122888 | tf_op jit(solution)/shard_map/ppermute | solution.py:380
  92.6 5.2 %collective-permute-start.33 = (f32[12,16,128]{2,1,0:T(8,128)S(1)}, f32[12,16,128]{2,1,0:T(8,128)S(1)}, u32[]{:S(2)}, u32[]{:S(2)}) collective-permute-start(f32[12,16,128]{2,1,0:T(8,128)S(1)} %get-tuple-element.165), channel_id=1, source_target_pairs={{0,2},{1,3},{2,0},{3,1},{4,6},{5,7},{6,4},{7,5},{8,10},{9,11},{10,... | collective-permute-start | bytes 294920 | tf_op jit(solution)/shard_map/ppermute | solution.py:341
  92.6 8.0 %collective-permute-start.34 = (f32[12,16,128]{2,1,0:T(8,128)S(1)}, f32[12,16,128]{2,1,0:T(8,128)S(1)}, u32[]{:S(2)}, u32[]{:S(2)}) collective-permute-start(f32[12,16,128]{2,1,0:T(8,128)S(1)} %get-tuple-element.166), channel_id=1, source_target_pairs={{0,3},{1,2},{2,1},{3,0},{4,7},{5,6},{6,5},{7,4},{8,11},{9,10},{10,... | collective-permute-start | bytes 294920 | tf_op jit(solution)/shard_map/ppermute | solution.py:341
  93.4 7.2 %collective-permute-start.35 = (f32[12,16,128]{2,1,0:T(8,128)S(1)}, f32[12,16,128]{2,1,0:T(8,128)S(1)}, u32[]{:S(2)}, u32[]{:S(2)}) collective-permute-start(f32[12,16,128]{2,1,0:T(8,128)S(1)} %get-tuple-element.167), channel_id=1, source_target_pairs={{0,1},{1,0},{2,4},{3,5},{4,2},{5,3},{6,8},{7,9},{8,6},{9,7},{10,12... | collective-permute-start | bytes 294920 | tf_op jit(solution)/shard_map/ppermute | solution.py:341
  94.8 5.9 %collective-permute-start.36 = (f32[12,16,128]{2,1,0:T(8,128)S(1)}, f32[12,16,128]{2,1,0:T(8,128)S(1)}, u32[]{:S(2)}, u32[]{:S(2)}) collective-permute-start(f32[12,16,128]{2,1,0:T(8,128)S(1)} %get-tuple-element.168), channel_id=1, source_target_pairs={{0,1},{1,0},{2,5},{3,4},{4,3},{5,2},{6,9},{7,8},{8,7},{9,6},{10,13... | collective-permute-start | bytes 294920 | tf_op jit(solution)/shard_map/ppermute | solution.py:341
  94.8 9.3 %collective-permute-start.37 = (f32[12,16,128]{2,1,0:T(8,128)S(1)}, f32[12,16,128]{2,1,0:T(8,128)S(1)}, u32[]{:S(2)}, u32[]{:S(2)}) collective-permute-start(f32[12,16,128]{2,1,0:T(8,128)S(1)} %get-tuple-element.169), channel_id=1, source_target_pairs={{0,13},{1,4},{2,15},{3,6},{4,1},{5,8},{6,3},{7,10},{8,5},{9,12},{1... | collective-permute-start | bytes 294920 | tf_op jit(solution)/shard_map/ppermute | solution.py:341
  97.8 6.2 %collective-permute-start.38 = (f32[12,16,128]{2,1,0:T(8,128)S(1)}, f32[12,16,128]{2,1,0:T(8,128)S(1)}, u32[]{:S(2)}, u32[]{:S(2)}) collective-permute-start(f32[12,16,128]{2,1,0:T(8,128)S(1)} %get-tuple-element.170), channel_id=1, source_target_pairs={{0,1},{1,0},{2,3},{3,2},{4,5},{5,4},{6,7},{7,6},{8,9},{9,8},{10,11... | collective-permute-start | bytes 294920 | tf_op jit(solution)/shard_map/ppermute | solution.py:341
  107.7 6.0 %collective-permute-start.43 = (f32[12,16,128]{2,1,0:T(8,128)S(1)}, f32[12,16,128]{2,1,0:T(8,128)S(1)}, u32[]{:S(2)}, u32[]{:S(2)}) collective-permute-start(f32[12,16,128]{2,1,0:T(8,128)S(1)} %get-tuple-element.177), channel_id=1, source_target_pairs={{0,2},{1,3},{2,0},{3,1},{4,6},{5,7},{6,4},{7,5},{8,10},{9,11},{10,... | collective-permute-start | bytes 294920 | tf_op jit(solution)/shard_map/ppermute | solution.py:346
  107.8 5.9 %collective-permute-start.44 = (f32[12,16,128]{2,1,0:T(8,128)S(1)}, f32[12,16,128]{2,1,0:T(8,128)S(1)}, u32[]{:S(2)}, u32[]{:S(2)}) collective-permute-start(f32[12,16,128]{2,1,0:T(8,128)S(1)} %get-tuple-element.178), channel_id=1, source_target_pairs={{0,3},{1,2},{2,1},{3,0},{4,7},{5,6},{6,5},{7,4},{8,11},{9,10},{10,... | collective-permute-start | bytes 294920 | tf_op jit(solution)/shard_map/ppermute | solution.py:346
  107.9 4.1 %collective-permute-start.39 = (f32[5,16,128]{2,1,0:T(8,128)S(1)}, f32[5,16,128]{2,1,0:T(8,128)S(1)}, u32[]{:S(2)}, u32[]{:S(2)}) collective-permute-start(f32[5,16,128]{2,1,0:T(8,128)S(1)} %get-tuple-element.172), channel_id=1, source_target_pairs={{0,4},{1,5},{2,6},{3,7},{4,0},{5,1},{6,2},{7,3},{8,12},{9,13},{10,... | collective-permute-start | bytes 122888 | tf_op jit(solution)/shard_map/ppermute | solution.py:380
  111.9 6.2 %collective-permute-start.40 = (f32[5,16,128]{2,1,0:T(8,128)S(1)}, f32[5,16,128]{2,1,0:T(8,128)S(1)}, u32[]{:S(2)}, u32[]{:S(2)}) collective-permute-start(f32[5,16,128]{2,1,0:T(8,128)S(1)} %add.193), channel_id=1, source_target_pairs={{0,8},{1,9},{2,10},{3,11},{4,12},{5,13},{6,14},{7,15},{8,0},{9,1},... | collective-permute-start | bytes 122888 | tf_op jit(solution)/shard_map/ppermute | solution.py:380
  113.7 9.7 %collective-permute-start.48 = (f32[12,16,128]{2,1,0:T(8,128)S(1)}, f32[12,16,128]{2,1,0:T(8,128)S(1)}, u32[]{:S(2)}, u32[]{:S(2)}) collective-permute-start(f32[12,16,128]{2,1,0:T(8,128)S(1)} %get-tuple-element.187), channel_id=1, source_target_pairs={{0,1},{1,0},{2,3},{3,2},{4,5},{5,4},{6,7},{7,6},{8,9},{9,8},{10,11... | collective-permute-start | bytes 294920 | tf_op jit(solution)/shard_map/ppermute | solution.py:346
  113.7 9.7 %collective-permute-start.45 = (f32[12,16,128]{2,1,0:T(8,128)S(1)}, f32[12,16,128]{2,1,0:T(8,128)S(1)}, u32[]{:S(2)}, u32[]{:S(2)}) collective-permute-start(f32[12,16,128]{2,1,0:T(8,128)S(1)} %get-tuple-element.184), channel_id=1, source_target_pairs={{0,1},{1,0},{2,4},{3,5},{4,2},{5,3},{6,8},{7,9},{8,6},{9,7},{10,12... | collective-permute-start | bytes 294920 | tf_op jit(solution)/shard_map/ppermute | solution.py:350
  114.2 9.2 %collective-permute-start.46 = (f32[12,16,128]{2,1,0:T(8,128)S(1)}, f32[12,16,128]{2,1,0:T(8,128)S(1)}, u32[]{:S(2)}, u32[]{:S(2)}) collective-permute-start(f32[12,16,128]{2,1,0:T(8,128)S(1)} %get-tuple-element.185), channel_id=1, source_target_pairs={{0,1},{1,0},{2,5},{3,4},{4,3},{5,2},{6,9},{7,8},{8,7},{9,6},{10,13... | collective-permute-start | bytes 294920 | tf_op jit(solution)/shard_map/ppermute | solution.py:350
  114.3 10.3 %collective-permute-start.47 = (f32[12,16,128]{2,1,0:T(8,128)S(1)}, f32[12,16,128]{2,1,0:T(8,128)S(1)}, u32[]{:S(2)}, u32[]{:S(2)}) collective-permute-start(f32[12,16,128]{2,1,0:T(8,128)S(1)} %get-tuple-element.186), channel_id=1, source_target_pairs={{0,13},{1,4},{2,15},{3,6},{4,1},{5,8},{6,3},{7,10},{8,5},{9,12},{1... | collective-permute-start | bytes 294920 | tf_op jit(solution)/shard_map/ppermute | solution.py:350
  118.1 1.3 collective-permute-start.41
  119.4 4.0 %collective-permute-start.42 = (f32[5,16,128]{2,1,0:T(8,128)S(1)}, f32[5,16,128]{2,1,0:T(8,128)S(1)}, u32[]{:S(2)}, u32[]{:S(2)}) collective-permute-start(f32[5,16,128]{2,1,0:T(8,128)S(1)} %add.195), channel_id=1, source_target_pairs={{0,2},{1,3},{2,0},{3,1},{4,6},{5,7},{6,4},{7,5},{8,10},{9,11},{10,... | collective-permute-start | bytes 122888 | tf_op jit(solution)/shard_map/ppermute | solution.py:380
  126.7 5.2 %collective-permute-start.49 = (f32[12,16,128]{2,1,0:T(8,128)S(1)}, f32[12,16,128]{2,1,0:T(8,128)S(1)}, u32[]{:S(2)}, u32[]{:S(2)}) collective-permute-start(f32[12,16,128]{2,1,0:T(8,128)S(1)} %get-tuple-element.191), channel_id=1, source_target_pairs={{0,2},{1,3},{2,0},{3,1},{4,6},{5,7},{6,4},{7,5},{8,10},{9,11},{10,... | collective-permute-start | bytes 294920 | tf_op jit(solution)/shard_map/ppermute | solution.py:341
  126.7 7.8 %collective-permute-start.50 = (f32[12,16,128]{2,1,0:T(8,128)S(1)}, f32[12,16,128]{2,1,0:T(8,128)S(1)}, u32[]{:S(2)}, u32[]{:S(2)}) collective-permute-start(f32[12,16,128]{2,1,0:T(8,128)S(1)} %get-tuple-element.192), channel_id=1, source_target_pairs={{0,3},{1,2},{2,1},{3,0},{4,7},{5,6},{6,5},{7,4},{8,11},{9,10},{10,... | collective-permute-start | bytes 294920 | tf_op jit(solution)/shard_map/ppermute | solution.py:341
  126.8 7.8 %collective-permute-start.51 = (f32[12,16,128]{2,1,0:T(8,128)S(1)}, f32[12,16,128]{2,1,0:T(8,128)S(1)}, u32[]{:S(2)}, u32[]{:S(2)}) collective-permute-start(f32[12,16,128]{2,1,0:T(8,128)S(1)} %get-tuple-element.193), channel_id=1, source_target_pairs={{0,1},{1,0},{2,4},{3,5},{4,2},{5,3},{6,8},{7,9},{8,6},{9,7},{10,12... | collective-permute-start | bytes 294920 | tf_op jit(solution)/shard_map/ppermute | solution.py:341
  128.9 5.7 %collective-permute-start.52 = (f32[12,16,128]{2,1,0:T(8,128)S(1)}, f32[12,16,128]{2,1,0:T(8,128)S(1)}, u32[]{:S(2)}, u32[]{:S(2)}) collective-permute-start(f32[12,16,128]{2,1,0:T(8,128)S(1)} %get-tuple-element.194), channel_id=1, source_target_pairs={{0,1},{1,0},{2,5},{3,4},{4,3},{5,2},{6,9},{7,8},{8,7},{9,6},{10,13... | collective-permute-start | bytes 294920 | tf_op jit(solution)/shard_map/ppermute | solution.py:341
  128.9 9.2 %collective-permute-start.53 = (f32[12,16,128]{2,1,0:T(8,128)S(1)}, f32[12,16,128]{2,1,0:T(8,128)S(1)}, u32[]{:S(2)}, u32[]{:S(2)}) collective-permute-start(f32[12,16,128]{2,1,0:T(8,128)S(1)} %get-tuple-element.195), channel_id=1, source_target_pairs={{0,13},{1,4},{2,15},{3,6},{4,1},{5,8},{6,3},{7,10},{8,5},{9,12},{1... | collective-permute-start | bytes 294920 | tf_op jit(solution)/shard_map/ppermute | solution.py:341
  131.9 6.1 %collective-permute-start.54 = (f32[12,16,128]{2,1,0:T(8,128)S(1)}, f32[12,16,128]{2,1,0:T(8,128)S(1)}, u32[]{:S(2)}, u32[]{:S(2)}) collective-permute-start(f32[12,16,128]{2,1,0:T(8,128)S(1)} %get-tuple-element.196), channel_id=1, source_target_pairs={{0,1},{1,0},{2,3},{3,2},{4,5},{5,4},{6,7},{7,6},{8,9},{9,8},{10,11... | collective-permute-start | bytes 294920 | tf_op jit(solution)/shard_map/ppermute | solution.py:341
  141.7 6.3 %collective-permute-start.59 = (f32[12,16,128]{2,1,0:T(8,128)S(1)}, f32[12,16,128]{2,1,0:T(8,128)S(1)}, u32[]{:S(2)}, u32[]{:S(2)}) collective-permute-start(f32[12,16,128]{2,1,0:T(8,128)S(1)} %get-tuple-element.203), channel_id=1, source_target_pairs={{0,2},{1,3},{2,0},{3,1},{4,6},{5,7},{6,4},{7,5},{8,10},{9,11},{10,... | collective-permute-start | bytes 294920 | tf_op jit(solution)/shard_map/ppermute | solution.py:346
  141.8 6.2 %collective-permute-start.60 = (f32[12,16,128]{2,1,0:T(8,128)S(1)}, f32[12,16,128]{2,1,0:T(8,128)S(1)}, u32[]{:S(2)}, u32[]{:S(2)}) collective-permute-start(f32[12,16,128]{2,1,0:T(8,128)S(1)} %get-tuple-element.204), channel_id=1, source_target_pairs={{0,3},{1,2},{2,1},{3,0},{4,7},{5,6},{6,5},{7,4},{8,11},{9,10},{10,... | collective-permute-start | bytes 294920 | tf_op jit(solution)/shard_map/ppermute | solution.py:346
  141.9 4.1 %collective-permute-start.55 = (f32[5,16,128]{2,1,0:T(8,128)S(1)}, f32[5,16,128]{2,1,0:T(8,128)S(1)}, u32[]{:S(2)}, u32[]{:S(2)}) collective-permute-start(f32[5,16,128]{2,1,0:T(8,128)S(1)} %get-tuple-element.198), channel_id=1, source_target_pairs={{0,4},{1,5},{2,6},{3,7},{4,0},{5,1},{6,2},{7,3},{8,12},{9,13},{10,... | collective-permute-start | bytes 122888 | tf_op jit(solution)/shard_map/ppermute | solution.py:380
  145.9 6.2 %collective-permute-start.56 = (f32[5,16,128]{2,1,0:T(8,128)S(1)}, f32[5,16,128]{2,1,0:T(8,128)S(1)}, u32[]{:S(2)}, u32[]{:S(2)}) collective-permute-start(f32[5,16,128]{2,1,0:T(8,128)S(1)} %add.197), channel_id=1, source_target_pairs={{0,8},{1,9},{2,10},{3,11},{4,12},{5,13},{6,14},{7,15},{8,0},{9,1},... | collective-permute-start | bytes 122888 | tf_op jit(solution)/shard_map/ppermute | solution.py:380
  148.0 9.4 %collective-permute-start.64 = (f32[12,16,128]{2,1,0:T(8,128)S(1)}, f32[12,16,128]{2,1,0:T(8,128)S(1)}, u32[]{:S(2)}, u32[]{:S(2)}) collective-permute-start(f32[12,16,128]{2,1,0:T(8,128)S(1)} %get-tuple-element.213), channel_id=1, source_target_pairs={{0,1},{1,0},{2,3},{3,2},{4,5},{5,4},{6,7},{7,6},{8,9},{9,8},{10,11... | collective-permute-start | bytes 294920 | tf_op jit(solution)/shard_map/ppermute | solution.py:346
  148.0 9.4 %collective-permute-start.61 = (f32[12,16,128]{2,1,0:T(8,128)S(1)}, f32[12,16,128]{2,1,0:T(8,128)S(1)}, u32[]{:S(2)}, u32[]{:S(2)}) collective-permute-start(f32[12,16,128]{2,1,0:T(8,128)S(1)} %get-tuple-element.210), channel_id=1, source_target_pairs={{0,1},{1,0},{2,4},{3,5},{4,2},{5,3},{6,8},{7,9},{8,6},{9,7},{10,12... | collective-permute-start | bytes 294920 | tf_op jit(solution)/shard_map/ppermute | solution.py:350
  148.5 8.9 %collective-permute-start.62 = (f32[12,16,128]{2,1,0:T(8,128)S(1)}, f32[12,16,128]{2,1,0:T(8,128)S(1)}, u32[]{:S(2)}, u32[]{:S(2)}) collective-permute-start(f32[12,16,128]{2,1,0:T(8,128)S(1)} %get-tuple-element.211), channel_id=1, source_target_pairs={{0,1},{1,0},{2,5},{3,4},{4,3},{5,2},{6,9},{7,8},{8,7},{9,6},{10,13... | collective-permute-start | bytes 294920 | tf_op jit(solution)/shard_map/ppermute | solution.py:350
  148.6 10.0 %collective-permute-start.63 = (f32[12,16,128]{2,1,0:T(8,128)S(1)}, f32[12,16,128]{2,1,0:T(8,128)S(1)}, u32[]{:S(2)}, u32[]{:S(2)}) collective-permute-start(f32[12,16,128]{2,1,0:T(8,128)S(1)} %get-tuple-element.212), channel_id=1, source_target_pairs={{0,13},{1,4},{2,15},{3,6},{4,1},{5,8},{6,3},{7,10},{8,5},{9,12},{1... | collective-permute-start | bytes 294920 | tf_op jit(solution)/shard_map/ppermute | solution.py:350
  153.4 4.0 %collective-permute-start.58 = (f32[5,16,128]{2,1,0:T(8,128)S(1)}, f32[5,16,128]{2,1,0:T(8,128)S(1)}, u32[]{:S(2)}, u32[]{:S(2)}) collective-permute-start(f32[5,16,128]{2,1,0:T(8,128)S(1)} %add.199), channel_id=1, source_target_pairs={{0,2},{1,3},{2,0},{3,1},{4,6},{5,7},{6,4},{7,5},{8,10},{9,11},{10,... | collective-permute-start | bytes 122888 | tf_op jit(solution)/shard_map/ppermute | solution.py:380
  (4 other events, 45.6 us)
